TPU v7x, 32 devices: a whole 2x2x4 slice. The times are simulated.
32 devices in a mesh: dp: 16 (over z, y, x), stream: 2 (over core).
Axes of the slice: x: 2, y: 2, z: 4, core: 2. Of those that a mesh axis runs over, the one named last changes fastest.
Arguments:
- tokens: bfloat16 [32768, 1024], P('dp'), may hold values from -6 to 6
- norm_gain: float32 [1024], replicated, may hold values from 0.1 to 1.9
- w_qkv: bfloat16 [1024, 3072], replicated, may hold values from -0.1875 to 0.1875
- w_proj: bfloat16 [1024, 1024], replicated, may hold values from -4 to 4
- w_in: bfloat16 [1024, 4096], replicated, may hold values from -0.1875 to 0.1875
- w_out: bfloat16 [4096, 1024], replicated, may hold values from -0.09375 to 0.09375
- feature_weight: float32 [1024], replicated, may hold values from 0.25 to 4
- lengths: int32 [16], P('dp'), may hold values from 128 to 2048, as said below
- cotangent: bfloat16 [32768, 1024], P('dp'), may hold values from -6 to 6
Outputs:
- output: bfloat16 [32768, 1024], P('dp')
- input_grad: bfloat16 [32768, 1024], P('dp')
- gain_grad: float32 [1024], P(('dp', 'stream'))
- qkv_grad: float32 [1024, 3072], P(('dp', 'stream'))
- proj_grad: float32 [1024, 1024], P(('dp', 'stream'))
- in_grad: float32 [1024, 4096], P(('dp', 'stream'))
- out_grad: float32 [4096, 1024], P(('dp', 'stream'))
- feature_grad: float32 [1024], P(('dp', 'stream'))
Inputs may be any that keep to these rules, and one draw needn't show every extreme that they name: `lengths`: lengths have many short values; some slot holds 2048 and some holds 128.
All inputs are finite; a program needn't handle non-finite values.
Results may differ from a plain program's by a relative error of at most 0.015.
Values sent between devices are 32-bit elements; how exact they have to be, the bound alone decides.
A program may use at most 320 MiB of HBM per device.

v0:
```python
from functools import partial

import jax
import jax.numpy as jnp
from jax import lax
from jax.sharding import PartitionSpec as P

D = 1024
HEADS = 16
HEAD = 64
FF = 4096
ROT = 16
SPAN = 64
SLOT = 2048


EPSILON = 1e-05
HIGHEST = lax.Precision.HIGHEST


def feature_table():
    indices = jnp.arange(HEAD).astype(jnp.float32)
    cos_table = jnp.cos(jnp.pi * (2.0 * indices[:, None] + 1.0) * indices[None, :] / (2.0 * HEAD))
    weights = jnp.where(indices == 0, jnp.sqrt(1.0 / HEAD), jnp.sqrt(2.0 / HEAD))
    quantiles = jnp.sqrt(2.0) * lax.erf_inv(2.0 * (indices + 0.5) / HEAD - 1.0)
    return cos_table * (weights * 0.5 * quantiles)[None, :]


def rotary_tables():
    half_rot = ROT // 2
    positions = jnp.arange(SLOT).astype(jnp.float32)
    inverse = 10000.0 ** (-2.0 * jnp.arange(half_rot).astype(jnp.float32) / ROT)
    angles = positions[:, None] * inverse[None, :]
    return (jnp.cos(angles)[None, :, None, :], jnp.sin(angles)[None, :, None, :])


def rotate(heads_in, cosine, sine_table):
    half_rot = ROT // 2
    upper_half = heads_in[..., :half_rot]
    lower_half = heads_in[..., half_rot:ROT]
    return jnp.concatenate(
        [
            upper_half * cosine - lower_half * sine_table,
            lower_half * cosine + upper_half * sine_table,
            heads_in[..., ROT:],
        ],
        axis=-1,
    )


def unrotate(grad_rot, cosine, sine_table):
    half_rot = ROT // 2
    upper_half = grad_rot[..., :half_rot]
    lower_half = grad_rot[..., half_rot:ROT]
    return jnp.concatenate(
        [
            upper_half * cosine + lower_half * sine_table,
            lower_half * cosine - upper_half * sine_table,
            grad_rot[..., ROT:],
        ],
        axis=-1,
    )


def exclusive(blocks_in):
    running = jnp.cumsum(blocks_in, axis=2)
    return jnp.concatenate([jnp.zeros_like(running[:, :, :1]), running[:, :, :-1]], axis=2)


def exclusive_later(blocks_in):
    running = jnp.flip(jnp.cumsum(jnp.flip(blocks_in, 2), axis=2), 2)
    return jnp.concatenate([running[:, :, 1:], jnp.zeros_like(running[:, :, :1])], axis=2)


def to_blocks(blocks_in):
    slot_count = blocks_in.shape[0]
    return blocks_in.reshape(slot_count, SLOT // SPAN, SPAN, HEADS, HEAD).transpose(0, 3, 1, 2, 4)


def from_blocks(blocks_in):
    slot_count = blocks_in.shape[0]
    return blocks_in.transpose(0, 2, 3, 1, 4).reshape(slot_count, SLOT, HEADS, HEAD)


def body(tokens, norm_gain, w_qkv, w_proj, w_in, w_out, feature_weight, lengths, cotangent):
    f32 = jnp.float32
    bf16 = jnp.bfloat16
    row_count = tokens.shape[0]
    slot_count = row_count // SLOT
    inputs = tokens.astype(f32)
    positions = jnp.arange(SLOT)
    valid_slots = (positions[None, :] < lengths[:, None]).astype(f32)
    valid_rows = valid_slots.reshape(row_count, 1)
    valid_heads = valid_slots[:, :, None, None]
    average = jnp.mean(inputs, axis=-1, keepdims=True)
    centered = inputs - average
    variance = jnp.mean(centered * centered, axis=-1, keepdims=True)
    inv_std = lax.rsqrt(variance + EPSILON)
    unit_rows = centered * inv_std
    normed = (unit_rows * norm_gain).astype(bf16)
    cot_rows = cotangent.astype(f32)
    kept_grad = (cot_rows * valid_rows).astype(bf16)

    def attention_half():
        projected = jnp.dot(normed, w_qkv, preferred_element_type=f32)
        heads_view = projected.reshape(slot_count, SLOT, 3, HEADS, HEAD)
        cosine, sine_table = rotary_tables()
        feature_map = feature_table()
        scales = feature_weight.reshape(HEADS, HEAD)
        queries = rotate(heads_view[:, :, 0], cosine, sine_table)
        keys_rot = rotate(heads_view[:, :, 1], cosine, sine_table)
        q_expo = jnp.exp(jnp.einsum("bshi,im->bshm", queries, feature_map, precision=HIGHEST))
        k_expo = jnp.exp(jnp.einsum("bshi,im->bshm", keys_rot, feature_map, precision=HIGHEST))
        q_phi = scales * q_expo
        k_phi = scales * k_expo * valid_heads
        q_low = to_blocks(q_phi.astype(bf16))
        k_low = to_blocks(k_phi.astype(bf16))
        v_low = to_blocks(heads_view[:, :, 2].astype(bf16))
        causal = (jnp.arange(SPAN)[:, None] >= jnp.arange(SPAN)[None, :]).astype(f32)
        score_low = (
            jnp.einsum("bhnqm,bhnkm->bhnqk", q_low, k_low, preferred_element_type=f32) * causal
        ).astype(bf16)
        kv_block = jnp.einsum("bhnkm,bhnkd->bhnmd", k_low, v_low, preferred_element_type=f32)
        state_low = exclusive(kv_block).astype(bf16)
        key_low = exclusive(jnp.sum(k_low, axis=3, dtype=f32)).astype(bf16)
        numerator = jnp.einsum(
            "bhnqk,bhnkd->bhnqd", score_low, v_low, preferred_element_type=f32
        ) + jnp.einsum("bhnqm,bhnmd->bhnqd", q_low, state_low, preferred_element_type=f32)
        denominator = jnp.sum(score_low, axis=-1, dtype=f32) + jnp.einsum(
            "bhnqm,bhnm->bhnq", q_low, key_low, preferred_element_type=f32
        )
        attended = numerator / denominator[..., None]
        mixed_heads = from_blocks(attended.astype(bf16)).reshape(row_count, D)
        branch = jnp.dot(mixed_heads, w_proj, preferred_element_type=f32)
        g_proj = jnp.dot(mixed_heads.T, kept_grad, preferred_element_type=f32)
        d_mixed = jnp.dot(kept_grad, w_proj.T, preferred_element_type=f32)
        d_attended = to_blocks(d_mixed.reshape(slot_count, SLOT, HEADS, HEAD))
        d_numer = (d_attended / denominator[..., None]).astype(bf16)
        d_denom = (-jnp.sum(d_attended * attended, axis=-1) / denominator).astype(bf16)
        d_score = jnp.einsum(
            "bhnqd,bhnkd->bhnqk", d_numer, v_low, preferred_element_type=f32
        ) + d_denom[..., None].astype(f32)
        d_score_low = (d_score * causal).astype(bf16)
        d_state = jnp.einsum(
            "bhnqm,bhnqd->bhnmd", q_low, d_numer, preferred_element_type=f32
        ).astype(bf16)
        d_key_state = jnp.einsum(
            "bhnq,bhnqm->bhnm", d_denom, q_low, preferred_element_type=f32
        ).astype(bf16)
        d_kv = exclusive_later(d_state.astype(f32)).astype(bf16)
        d_key_sum = exclusive_later(d_key_state.astype(f32))
        d_query = (
            jnp.einsum("bhnqd,bhnmd->bhnqm", d_numer, state_low, preferred_element_type=f32)
            + d_denom[..., None].astype(f32) * key_low[:, :, :, None, :].astype(f32)
            + jnp.einsum("bhnqk,bhnkm->bhnqm", d_score_low, k_low, preferred_element_type=f32)
        )
        d_key = (
            jnp.einsum("bhnqk,bhnqm->bhnkm", d_score_low, q_low, preferred_element_type=f32)
            + jnp.einsum("bhnkd,bhnmd->bhnkm", v_low, d_kv, preferred_element_type=f32)
            + d_key_sum[:, :, :, None, :]
        )
        d_values = jnp.einsum(
            "bhnqk,bhnqd->bhnkd", score_low, d_numer, preferred_element_type=f32
        ) + jnp.einsum("bhnkm,bhnmd->bhnkd", k_low, d_kv, preferred_element_type=f32)
        d_q_phi = from_blocks(d_query)
        d_k_phi = from_blocks(d_key) * valid_heads
        g_feature = jnp.sum(d_q_phi * q_expo + d_k_phi * k_expo, axis=(0, 1)).reshape(D)
        d_q_rot = jnp.einsum("bshm,im->bshi", d_q_phi * q_phi, feature_map, precision=HIGHEST)
        d_k_rot = jnp.einsum(
            "bshm,im->bshi", d_k_phi * scales * k_expo, feature_map, precision=HIGHEST
        )
        d_queries = unrotate(d_q_rot, cosine, sine_table)
        d_keys = unrotate(d_k_rot, cosine, sine_table)
        d_projected = (
            jnp.stack([d_queries, d_keys, from_blocks(d_values)], axis=2)
            .reshape(row_count, 3 * D)
            .astype(bf16)
        )
        g_qkv = jnp.dot(normed.T, d_projected, preferred_element_type=f32)
        d_normed = jnp.dot(d_projected, w_qkv.T, preferred_element_type=f32)
        return (
            branch,
            d_normed,
            g_qkv,
            g_proj,
            jnp.zeros((D, FF), f32),
            jnp.zeros((FF, D), f32),
            g_feature,
        )

    def feed_half():
        hidden = jnp.dot(normed, w_in, preferred_element_type=f32)
        gelu_value, gelu_back = jax.vjp(partial(jax.nn.gelu, approximate=False), hidden)
        active = gelu_value.astype(bf16)
        branch = jnp.dot(active, w_out, preferred_element_type=f32)
        g_out = jnp.dot(active.T, kept_grad, preferred_element_type=f32)
        d_active = jnp.dot(kept_grad, w_out.T, preferred_element_type=f32)
        d_hidden = gelu_back(d_active)[0].astype(bf16)
        g_in = jnp.dot(normed.T, d_hidden, preferred_element_type=f32)
        d_normed = jnp.dot(d_hidden, w_in.T, preferred_element_type=f32)
        return (
            branch,
            d_normed,
            jnp.zeros((D, 3 * D), f32),
            jnp.zeros((D, D), f32),
            g_in,
            g_out,
            jnp.zeros((D,), f32),
        )

    stream_index = lax.axis_index("stream")
    branch, d_normed, g_qkv, g_proj, g_in, g_out, g_feature = lax.cond(
        stream_index == 0, attention_half, feed_half
    )
    branch_sum, normed_grad = lax.psum((branch * valid_rows, d_normed), "stream")
    output = (inputs + branch_sum).astype(bf16)
    scaled = normed_grad * norm_gain
    g_gain = jnp.where(stream_index == 0, jnp.sum(normed_grad * unit_rows, axis=0), 0.0)
    correction = (
        scaled
        - jnp.mean(scaled, axis=-1, keepdims=True)
        - unit_rows * jnp.mean(scaled * unit_rows, axis=-1, keepdims=True)
    )
    input_grad = (cot_rows + inv_std * correction).astype(bf16)
    final = (
        lax.psum_scatter(g_gain, ("dp", "stream"), scatter_dimension=0, tiled=True),
        lax.psum_scatter(g_qkv, ("dp", "stream"), scatter_dimension=0, tiled=True),
        lax.psum_scatter(g_proj, ("dp", "stream"), scatter_dimension=0, tiled=True),
        lax.psum_scatter(g_in, ("dp", "stream"), scatter_dimension=0, tiled=True),
        lax.psum_scatter(g_out, ("dp", "stream"), scatter_dimension=0, tiled=True),
        lax.psum_scatter(g_feature, ("dp", "stream"), scatter_dimension=0, tiled=True),
    )
    return (output, input_grad, final[0], final[1], final[2], final[3], final[4], final[5])


def solution(mesh):
    return jax.shard_map(
        body,
        mesh=mesh,
        in_specs=(P("dp", None), P(), P(), P(), P(), P(), P(), P("dp"), P("dp", None)),
        out_specs=(
            P("dp", None),
            P("dp", None),
            P(("dp", "stream")),
            P(("dp", "stream"), None),
            P(("dp", "stream"), None),
            P(("dp", "stream"), None),
            P(("dp", "stream"), None),
            P(("dp", "stream")),
        ),
        check_vma=False,
    )
```

profile of v0, /device:TPU:0, one launch (start us, length us, event | category | flops | bytes accessed | tf_op | source)
XLA Modules:
  0.0 1356.0 jit_solution(14423479329913647824)
XLA Ops:
  21.9 639.1 %conditional.1 = (f32[2048,1024]{1,0:T(8,128)}, f32[2048,1024]{1,0:T(8,128)S(1)}, f32[1024,3072]{0,1:T(8,128)}, f32[1024,1024]{1,0:T(8,128)}, f32[1024,4096]{1,0...) conditional(s32[]{:T(128)} %convert_element_type.236, (bf16[2048,1024]{1,0:T(8,128)(2,1)}, ...), branch_computations={%region_2.0_spmd, %region_3.12_spmd} | conditional | flops 103741915136 | bytes 1070276608 | solution.py:212
  30.0 19.8 %fusion.151 = f32[2048,3072]{0,1:T(8,128)} fusion(bf16[2048,1024]{1,0:T(8,128)(2,1)} %get-tuple-element.25, bf16[1024,3072]{1,0:T(8,128)(2,1)} %get-tuple-element.60), kind=kOutput, calls=%fused_computation.216 | convolution fusion | flops 12884901888 | bytes 35651584 | tf_op jit(solution)/shard_map/cond/branch_1_fun/dot_general | solution.py:105
  57.8 13.7 %fusion.12 = f32[2048,16,64]{0,2,1:T(8,128)} fusion(f32[1,2048,16,48]{1,3,2,0:T(8,128)S(1)} %slice.72, f32[1,2048,16,8]{1,3,2,0:T(8,128)S(1)} %get-tuple-element.109, f32[1,2048,16,8]{1,3,2,0:T(8,128)S(1)} %get-tuple-element.110, f32[64]{0:T(128)S(1)} %get-tuple-element.121, f32[64]{0:T(128)S(1)} %iota_convert_fusion.1, f32[64]{0:T(128)S(1)} %get-tuple-element.122), kind=kOutput, calls=%fused_computation.40 | convolution fusion | flops 1614819328 | bytes 16777984 | tf_op jit(solution)/shard_map/cond/branch_1_fun/bshi,im->bshm/dot_general | solution.py:113
  74.7 30.7 %multiply_convert_fusion.4 = (bf16[2048,16,64]{0,2,1:T(8,128)(2,1)}, bf16[2048,16,64]{0,2,1:T(8,128)(2,1)}, f32[2048,16,64]{0,2,1:T(8,128)}) fusion(f32[16,64]{1,0:T(8,128)S(1)} %mul.384, f32[2048]{0:T(1024)S(1)} %bitcast.219, f32[2048,16,64]{0,2,1:T(8,128)} %fusion.12, f32[64]{0:T(128)S(1)} %get-tuple-element.121, f32[64]{0:T(128)S(1)} %iota_convert_fusion.1, ...), kind=kOutput, calls=%fused_computation.85 | convolution fusion | flops 1625305088 | bytes 33567488 | tf_op jit(solution)/shard_map/cond/branch_1_fun/bshi,im->bshm/dot_general | solution.py:112
  119.9 12.9 convert_element_type.192
  144.3 12.6 fusion.10
  177.2 13.2 reshape.393
  190.4 15.1 %fusion.35 = f32[16,32,64,64]{2,3,1,0:T(8,128)} fusion(bf16[1,16,31,64,64]{3,4,2,1,0:T(8,128)(2,1)} %copy.161, bf16[16,32,64,64]{2,1,3,0:T(8,128)(2,1)} %bitcast.201), kind=kOutput, calls=%fused_computation.64 | convolution fusion | flops 268435456 | bytes 16646144 | tf_op jit(solution)/shard_map/cond/branch_1_fun/bhnqm,bhnmd->bhnqd/dot_general | solution.py:128
  219.0 12.8 convert_reduce_fusion.1
  240.3 13.4 reshape.402
  253.6 18.4 %copy.101 = f32[1,32,64,16,64]{2,4,1,3,0:T(8,128)} copy(f32[1,32,64,16,64]{4,3,2,1,0:T(8,128)} %reshape.402) | data formatting | bytes 16777216 | tf_op jit(solution)/shard_map/cond/branch_1_fun/reshape;cond/branch_1_fun/reshape | solution.py:77
  272.1 23.0 %fusion.8 = (f32[16,32,64]{2,1,0:T(8,128)S(1)}, bf16[1,16,32,64,64]{3,4,2,1,0:T(8,128)(2,1)}, bf16[16,32,64,64]{2,3,1,0:T(8,128)(2,1)}) fusion(f32[1,32,64,16,64]{2,4,1,3,0:T(8,128)} %copy.101, f32[16,32,64]{2,1,0:T(8,128)S(1)} %add.124, f32[16,32,64,64]{2,3,1,0:T(8,128)} %fusion.35, bf16[16,32,64,64]{2,3,1,0:T(8,128)(2,1)} %get-tuple-element.119, ...), kind=kOutput, calls=%fused_computation.21 | convolution fusion | flops 283082752 | bytes 33816576 | tf_op jit(solution)/shard_map/cond/branch_1_fun/bhnqk,bhnkd->bhnqd/dot_general | solution.py:126
  316.6 20.0 %add_bitcast_fusion = f32[1,32,64,16,64]{2,4,1,3,0:T(8,128)} fusion(f32[16,32,64,64]{2,3,1,0:T(8,128)} %fusion.32, f32[16,32,64]{2,1,0:T(8,128)S(1)} %copy.104, f32[16,32,64]{2,1,0:T(8,128)S(1)} %get-tuple-element.92, bf16[16,32,64,64]{2,3,1,0:T(8,128)(2,1)} %multiply_convert_fusion.1, bf16[16,32,64,64]{3,2,1,0:T(8,128)(2,1)} %bitcast.196), kind=kOutput, calls=%fused_computation.28 | convolution fusion | flops 274726912 | bytes 25427968 | tf_op jit(solution)/shard_map/cond/branch_1_fun/bhnqk,bhnkm->bhnqm/dot_general | solution.py:155
  336.6 17.7 %copy.111 = f32[1,32,64,16,64]{2,1,4,3,0:T(8,128)} copy(f32[1,32,64,16,64]{2,4,1,3,0:T(8,128)} %add_bitcast_fusion) | data formatting | bytes 16777216 | tf_op jit(solution)/shard_map/cond/branch_1_fun/transpose | solution.py:82
  354.3 15.2 %reshape.404 = f32[2048,16,64]{0,2,1:T(8,128)} reshape(f32[1,32,64,16,64]{2,1,4,3,0:T(8,128)} %copy.111) | data formatting | bytes 16777216 | tf_op jit(solution)/shard_map/cond/branch_1_fun/reshape | solution.py:82
  402.9 12.8 fusion.6
  444.6 16.8 %add_add_fusion = f32[16,32,64,64]{3,2,1,0:T(8,128)} fusion(f32[16,32,64,64]{3,2,1,0:T(8,128)} %fusion.24, f32[16,32,64]{2,1,0:T(8,128)S(1)} %copy.115, bf16[16,32,64,64]{2,3,1,0:T(8,128)(2,1)} %multiply_convert_fusion.1, bf16[16,32,64,64]{2,1,3,0:T(8,128)(2,1)} %bitcast.203), kind=kOutput, calls=%fused_computation.27 | convolution fusion | flops 272629760 | bytes 25296896 | tf_op jit(solution)/shard_map/cond/branch_1_fun/bhnqk,bhnqm->bhnkm/dot_general | solution.py:158
  461.4 12.8 copy.159
  486.9 17.0 %fusion.78 = f32[1,2048,16,64]{1,3,2,0:T(8,128)S(1)} fusion(f32[2048,16,64]{0,2,1:T(8,128)} %reshape.404, f32[2048,16,64]{0,2,1:T(8,128)} %get-tuple-element.117, f32[16,64]{1,0:T(8,128)S(1)} %copy-done.15, f32[64]{0:T(128)S(1)} %copy-done.26, f32[64]{0:T(128)S(1)} %copy-done.30, f32[64]{0:T(128)S(1)} %copy-done.28), kind=kOutput, calls=%fused_computation.105 | convolution fusion | flops 1614819328 | bytes 25170688 | tf_op jit(solution)/shard_map/cond/branch_1_fun/bshm,im->bshi/dot_general | solution.py:168
  506.1 15.5 %fusion.81 = f32[1,2048,16,64]{1,3,2,0:T(8,128)S(1)} fusion(f32[2048,16,64]{0,2,1:T(8,128)S(1)} %copy-done, f32[2048,16,64]{0,2,1:T(8,128)} %fusion.12, f32[2048]{0:T(1024)S(1)} %bitcast.221, f32[16,64]{1,0:T(8,128)S(1)} %copy-done.15, f32[64]{0:T(128)S(1)} %copy-done.26, f32[64]{0:T(128)S(1)} %copy-done.30, f32[64]{0:T(128)S(1)} %copy-done.28), kind=kOutput, calls=%fused_computation.106 | convolution fusion | flops 1616916480 | bytes 25178880 | tf_op jit(solution)/shard_map/cond/branch_1_fun/bshm,im->bshi/dot_general | solution.py:169
  528.7 13.7 %fusion.22 = f32[16,32,64,64]{3,2,1,0:T(8,128)} fusion(bf16[16,32,64,64]{3,2,1,0:T(8,128)(2,1)} %bitcast.197, bf16[1,16,31,64,64]{4,3,2,1,0:T(8,128)(2,1)} %slice.110), kind=kOutput, calls=%fused_computation.51 | convolution fusion | flops 268435456 | bytes 16646144 | tf_op jit(solution)/shard_map/cond/branch_1_fun/bhnkm,bhnmd->bhnkd/dot_general | solution.py:164
  542.5 15.6 %add_convert_fusion.1 = bf16[16,32,64,64]{3,2,1,0:T(8,128)(2,1)} fusion(f32[16,32,64,64]{3,2,1,0:T(8,128)} %fusion.22, bf16[16,32,64,64]{2,3,1,0:T(8,128)(2,1)} %get-tuple-element.119, bf16[1,16,32,64,64]{3,4,2,1,0:T(8,128)(2,1)} %get-tuple-element.98), kind=kOutput, calls=%fused_computation.26 | convolution fusion | flops 272629760 | bytes 20971520 | tf_op jit(solution)/shard_map/cond/branch_1_fun/bhnqk,bhnqd->bhnkd/dot_general | solution.py:162
  572.2 16.9 %convolution_bitcast_fusion.1 = f32[1024,3072]{0,1:T(8,128)} fusion(bf16[2048,3072]{0,1:T(8,128)(2,1)S(1)} %bitcast.211, bf16[2048,1024]{1,0:T(8,128)(2,1)} %get-tuple-element.25), kind=kOutput, calls=%fused_computation.92 | convolution fusion | flops 12884901888 | bytes 29360128 | tf_op jit(solution)/shard_map/cond/branch_1_fun/dot_general | solution.py:179
  589.2 15.8 %fusion.154 = f32[2048,1024]{1,0:T(8,128)} fusion(bf16[2048,3072]{0,1:T(8,128)(2,1)S(1)} %bitcast.212, bf16[1024,3072]{1,0:T(8,128)(2,1)S(1)} %bitcast.223), kind=kOutput, calls=%fused_computation.219 | convolution fusion | flops 12884901888 | bytes 27262976 | tf_op jit(solution)/shard_map/cond/branch_1_fun/dot_general | solution.py:180
  672.0 13.0 copy.119
  686.3 47.9 %all-reduce.10.cloned.1.call-done = (f32[2048,1024]{1,0:T(8,128)}, f32[2048,1024]{1,0:T(8,128)}) async-done(((f32[2048,1024]{1,0:T(8,128)}, f32[2048,1024]{1,0:T(8,128)}), (f32[2048,1024]{1,0:T(8,128)}, f32[2048,1024]{1,0:T(8,128)})) %all-reduce.10.cloned.1.call-update) | async-done | bytes 16777232 | tf_op jit(solution)/shard_map/psum | solution.py:215
  740.6 41.0 %all-reduce.6 = (f32[1024]{0:T(1024)S(1)}, f32[1024]{0:T(1024)S(1)}) all-reduce(f32[1024]{0:T(1024)S(1)} %broadcast_select_fusion, f32[1024]{0:T(1024)S(1)} %copy-done.24), channel_id=2, replica_groups=mesh['dp'=16,'stream'=2] {'dp','stream'}, use_global_device_ids=true, to_apply=%region_17.18.clone | all-reduce | flops 2048 | bytes 16384
  782.8 13.4 fusion.143
  796.1 22.4 %reduce-scatter.7.cloned.1.call-done = f32[32,1024]{1,0:T(8,128)} async-done(((f32[1024,1024]{1,0:T(8,128)}), f32[32,1024]{1,0:T(8,128)}) %reduce-scatter.7.cloned.1.call-update) | async-done | bytes 131088 | tf_op jit(solution)/shard_map/reduce_scatter | solution.py:228
  818.5 158.1 %reduce-scatter.5.cloned.1.call-done = f32[32,3072]{1,0:T(8,128)} async-done(((f32[1024,3072]{1,0:T(8,128)}), f32[32,3072]{1,0:T(8,128)}) %reduce-scatter.5.cloned.1.call-update) | async-done | bytes 393232 | tf_op jit(solution)/shard_map/reduce_scatter | solution.py:227
  976.6 184.2 %reduce-scatter.11.cloned.1.call-done = f32[128,1024]{1,0:T(8,128)} async-done(((f32[4096,1024]{1,0:T(8,128)}), f32[128,1024]{1,0:T(8,128)}) %reduce-scatter.11.cloned.1.call-update) | async-done | bytes 524304 | tf_op jit(solution)/shard_map/reduce_scatter | solution.py:230
  1160.8 187.3 %reduce-scatter.9.cloned.1.call-done = f32[32,4096]{1,0:T(8,128)} async-done(((f32[1024,4096]{1,0:T(8,128)}), f32[32,4096]{1,0:T(8,128)}) %reduce-scatter.9.cloned.1.call-update) | async-done | bytes 524304 | tf_op jit(solution)/shard_map/reduce_scatter | solution.py:229
  (158 shorter events, 287.6 us)
Async XLA Ops:
  8.0 726.2 %all-reduce.10.cloned.1.call-start = ((), (), s32[]{:S(2)}) async-start(), calls=%async_computation.8 | async-start | bytes 33554432 | tf_op jit(solution)/shard_map/psum | solution.py:215
  10.9 11.0 copy-start.12
  21.9 639.1 %copy-start.21 = (f32[2048]{0:T(1024)S(1)}, f32[2048]{0:T(1024)}, u32[]{:S(2)}) copy-start(f32[2048]{0:T(1024)} %copy-done.20) | copy-start | bytes 24580
  30.0 44.7 %copy-start.18 = (f32[1,2048,1,1]{1,3,2,0:T(1,128)}, f32[1,2048,1,1]{1,3,2,0:T(1,128)S(1)}, u32[]{:S(2)}) copy-start(f32[1,2048,1,1]{1,3,2,0:T(1,128)S(1)} %get-tuple-element.27) | copy-start | bytes 24580 | tf_op jit(solution)/shard_map/cond
  57.8 16.9 %copy-start.25 = (f32[64]{0:T(128)}, f32[64]{0:T(128)S(1)}, u32[]{:S(2)}) copy-start(f32[64]{0:T(128)S(1)} %get-tuple-element.121) | copy-start | bytes 772 | tf_op jit(solution)/shard_map/cond
  57.8 16.9 %copy-start.27 = (f32[64]{0:T(128)}, f32[64]{0:T(128)S(1)}, u32[]{:S(2)}) copy-start(f32[64]{0:T(128)S(1)} %get-tuple-element.122) | copy-start | bytes 772 | tf_op jit(solution)/shard_map/cond
  57.8 16.9 %copy-start.29 = (f32[64]{0:T(128)}, f32[64]{0:T(128)S(1)}, u32[]{:S(2)}) copy-start(f32[64]{0:T(128)S(1)} %iota_convert_fusion.1) | copy-start | bytes 772 | tf_op jit(solution)/shard_map/cond
  74.7 30.8 %copy-start.14 = (f32[16,64]{1,0:T(8,128)}, f32[16,64]{1,0:T(8,128)S(1)}, u32[]{:S(2)}) copy-start(f32[16,64]{1,0:T(8,128)S(1)} %mul.384) | copy-start | bytes 12292 | tf_op jit(solution)/shard_map/cond
  205.5 13.4 slice-start
  219.0 12.8 copy-start.6
  461.4 12.8 copy-start.19
  474.2 12.7 copy-start.15
  474.2 12.7 copy-start.26
  474.2 12.7 copy-start.28
  474.2 12.7 copy-start.30
  486.9 19.2 %copy-start = (f32[2048,16,64]{0,2,1:T(8,128)S(1)}, f32[2048,16,64]{0,2,1:T(8,128)}, u32[]{:S(2)}) copy-start(f32[2048,16,64]{0,2,1:T(8,128)} %copy.159) | copy-start | bytes 25165828 | tf_op jit(solution)/shard_map/cond
  506.1 15.5 %copy-start.9 = (f32[2048,8]{0,1:T(8,128)S(1)}, f32[2048,8]{0,1:T(8,128)}, u32[]{:S(2)}) copy-start(f32[2048,8]{0,1:T(8,128)} %copy-done.8) | copy-start | bytes 196612 | tf_op jit(solution)/shard_map/cond
  506.1 15.5 %copy-start.11 = (f32[2048,8]{0,1:T(8,128)S(1)}, f32[2048,8]{0,1:T(8,128)}, u32[]{:S(2)}) copy-start(f32[2048,8]{0,1:T(8,128)} %copy-done.10) | copy-start | bytes 196612 | tf_op jit(solution)/shard_map/cond
  566.6 22.6 %slice-start.4 = ((s8[6291456]{0:T(1024)(128)(4,1)}), s8[4194304]{0:T(1024)(128)(4,1)S(1)}, s32[]{:S(2)}) async-start(s8[6291456]{0:T(1024)(128)(4,1)} %bitcast.222), calls=%async_computation.13 | async-start | bytes 8388608 | tf_op jit(solution)/shard_map/cond
  572.2 17.0 %slice-start.5 = ((s8[6291456]{0:T(1024)(128)(4,1)}), s8[2097152]{0:T(1024)(128)(4,1)S(1)}, s32[]{:S(2)}) async-start(s8[6291456]{0:T(1024)(128)(4,1)} %bitcast.222), calls=%async_computation.14 | async-start | bytes 4194304 | tf_op jit(solution)/shard_map/cond
  617.5 12.0 copy-start.32
  629.6 9.1 copy-start.7
  645.0 15.7 %slice-start.2 = ((s8[8388608]{0:T(1024)(128)(4,1)}), s8[4194304]{0:T(1024)(128)(4,1)S(1)}, s32[]{:S(2)}) async-start(s8[8388608]{0:T(1024)(128)(4,1)} %bitcast.214), calls=%async_computation.11 | async-start | bytes 8388608 | tf_op jit(solution)/shard_map/cond
  661.0 10.3 copy-start.3
  671.3 147.2 %reduce-scatter.7.cloned.1.call-start = ((), (), s32[]{:S(2)}) async-start(), calls=%async_computation.5 | async-start | bytes 4325376 | tf_op jit(solution)/shard_map/reduce_scatter | solution.py:228
  671.9 304.7 %reduce-scatter.5.cloned.1.call-start = ((), (), s32[]{:S(2)}) async-start(), calls=%async_computation.4 | async-start | bytes 12976128 | tf_op jit(solution)/shard_map/reduce_scatter | solution.py:227
  685.0 475.8 %reduce-scatter.11.cloned.1.call-start = ((), (), s32[]{:S(2)}) async-start(), calls=%async_computation.7 | async-start | bytes 17301504 | tf_op jit(solution)/shard_map/reduce_scatter | solution.py:230
  685.6 662.5 %reduce-scatter.9.cloned.1.call-start = ((), (), s32[]{:S(2)}) async-start(), calls=%async_computation.6 | async-start | bytes 17301504 | tf_op jit(solution)/shard_map/reduce_scatter | solution.py:229
  685.6 48.6 %copy-start.13 = (f32[2048]{0:T(1024)S(1)}, f32[2048]{0:T(1024)}, u32[]{:S(2)}) copy-start(f32[2048]{0:T(1024)} %copy-done.12) | copy-start | bytes 24580
  685.6 48.6 %copy-start.17 = (f32[2048]{0:T(1024)S(1)}, f32[2048]{0:T(1024)}, u32[]{:S(2)}) copy-start(f32[2048]{0:T(1024)} %copy-done.16) | copy-start | bytes 24580
  685.6 48.5 %copy-start.23 = (f32[1024]{0:T(1024)S(1)}, f32[1024]{0:T(1024)}, u32[]{:S(2)}) copy-start(f32[1024]{0:T(1024)} %param.12) | copy-start | bytes 12292
  686.3 54.2 %copy-start.24 = (f32[1024]{0:T(1024)S(1)}, f32[1024]{0:T(1024)}, u32[]{:S(2)}) copy-start(f32[1024]{0:T(1024)} %get-tuple-element.51) | copy-start | bytes 12292
  (11 other events, 60.9 us)
Sparse Core Ops, SparseCore 0:
  671.5 62.6 all-reduce.9
Sparse Core Ops, SparseCore 1:
  674.7 143.7 reduce-scatter.6
  826.0 150.5 reduce-scatter.4
  979.4 181.4 reduce-scatter.10
  1163.7 184.4 reduce-scatter.8
where the time goes:
time: 1360 us
  waiting for transfers between devices  602 us (44%)
  matrix products  340 us (25%)
  local copies, waits for them, and re-layouts  245 us (18%)
  other arithmetic  102 us (8%)
  blocking collectives  41 us (3%)
  between operations  16.8 us (1%)
    reduce_scatter x1, waiting for transfers between devices, body(): lax.psum_scatter(g_in, ('dp', 'stream'), scatter_dimension=0, tiled=True)  187 us
    reduce_scatter x1, waiting for transfers between devices, body(): lax.psum_scatter(g_out, ('dp', 'stream'), scatter_dimension=0, tiled=True)  184 us
    reduce_scatter x1, waiting for transfers between devices, body(): lax.psum_scatter(g_qkv, ('dp', 'stream'), scatter_dimension=0, tiled=True)  158 us
    reshape x4, local copies, waits for them, and re-layouts, to_blocks(): blocks_in.reshape(slot_count, SLOT // SPAN, SPAN, HEADS, HEAD)  53.4 us
    psum x1, waiting for transfers between devices, body(): lax.psum((branch * valid_rows, d_normed), 'stream')  47.9 us
    unnamed x1, blocking collectives  41 us
    dot_general x1, matrix products, attention_half(): jnp.einsum('bshi,im->bshm', queries, feature_map, precision=HIGHEST)  30.7 us
    transpose x2, local copies, waits for them, and re-layouts, from_blocks(): blocks_in.transpose(0, 2, 3, 1, 4).reshape(slot_count, SLOT, HEADS, HEAD)  30.2 us
  transfers between devices with their start and end apart: 5, of which 5 were waited for; matrix products, arithmetic and copies ran while one was open for 3% of the time, Pallas kernels for 0%

commit v1 on v0

v1 whole, which is shorter than its diff:
```python
import math
from functools import partial

import jax
import jax.numpy as jnp
import numpy as np
from jax import lax
from jax.experimental import pallas as pl
from jax.experimental.pallas import tpu as pltpu
from jax.sharding import PartitionSpec as P

D = 1024
HEADS = 16
HEAD = 64
FF = 4096
ROT = 16
SLOT = 2048
EPSILON = 1e-05

f32 = jnp.float32
bf16 = jnp.bfloat16
VMEM_LIMIT = 56 * 1024 * 1024
BLK = 256
PAIR = 2 * HEAD


def dot(a, b):
    return lax.dot_general(a, b, (((1,), (0,)), ((), ())), preferred_element_type=f32)


def dot_nt(a, b):
    return lax.dot_general(a, b, (((1,), (1,)), ((), ())), preferred_element_type=f32)


def dot_tn(a, b):
    return lax.dot_general(a, b, (((0,), (0,)), ((), ())), preferred_element_type=f32)


def erf_inverse(y):
    x = 0.0
    for _ in range(200):
        step = (math.erf(x) - y) / (2.0 / math.sqrt(math.pi) * math.exp(-x * x))
        x -= max(-0.5, min(0.5, step))
    return x


def feature_table():
    i = np.arange(HEAD, dtype=np.float64)
    cos_table = np.cos(np.pi * (2.0 * i[:, None] + 1.0) * i[None, :] / (2.0 * HEAD))
    weights = np.where(i == 0, math.sqrt(1.0 / HEAD), math.sqrt(2.0 / HEAD))
    quantiles = math.sqrt(2.0) * np.array([erf_inverse(2.0 * (m + 0.5) / HEAD - 1.0) for m in range(HEAD)])
    return cos_table * (weights * 0.5 * quantiles)[None, :]


def split_table(table):
    high = table.astype(np.float32).astype(bf16)
    low = (table - high.astype(np.float64)).astype(np.float32).astype(bf16)
    return high, low


def attention_tables():
    half = ROT // 2
    pos = np.arange(SLOT, dtype=np.float32)
    inverse = (np.float32(10000.0) ** (-2.0 * np.arange(half, dtype=np.float32) / np.float32(ROT))).astype(np.float32)
    angles = (pos[:, None] * inverse[None, :]).astype(np.float32).astype(np.float64)
    cos_one = np.ones((SLOT, HEAD))
    sin_one = np.zeros((SLOT, HEAD))
    cos_one[:, :half] = np.cos(angles)
    cos_one[:, half:ROT] = np.cos(angles)
    sin_one[:, :half] = np.sin(angles)
    sin_one[:, half:ROT] = -np.sin(angles)
    cosine = np.concatenate([cos_one, cos_one], 1).astype(np.float32)
    sine = np.concatenate([sin_one, sin_one], 1).astype(np.float32)
    one = feature_table()
    pair = np.zeros((PAIR, PAIR))
    pair[:HEAD, :HEAD] = one
    pair[HEAD:, HEAD:] = one
    swapped = pair.copy()
    for base in (0, HEAD):
        swapped[base : base + half] = pair[base + half : base + ROT]
        swapped[base + half : base + ROT] = pair[base : base + half]
    both = np.concatenate([pair, swapped], 0)
    high, low = split_table(both)
    forward = np.concatenate([high, low], 1)
    back_high, back_low = split_table(np.concatenate([pair.T, swapped.T], 1))
    back_high2 = np.concatenate([back_high, back_high], 0)
    return cosine, sine, forward, back_high2, back_low


def params(**extra):
    return pltpu.CompilerParams(vmem_limit_bytes=VMEM_LIMIT, **extra)


def job_plan(job, steps):
    count, rows, _ = job[0][0].shape
    columns = sum(keep.shape[2] for keep, _ in job)
    half = max(count // 2, 1)
    blocks = math.gcd(half, steps) if steps < half else half
    return count, rows, columns, half, blocks


def with_jobs(kernel, scalars, steps, in_specs, out_specs, out_shape, jobs, **call):
    base_in, base_out = len(in_specs), len(out_specs)
    job_in, job_out, job_shape, arrays = [], [], [], []
    plans = [job_plan(job, steps) for job in jobs]
    for job, (count, rows, columns, half, blocks) in zip(jobs, plans):
        per = half // blocks
        for keep, recv in job:
            wide = keep.shape[2]
            low = pl.BlockSpec((per, rows, wide), lambda i, *_, b=blocks: (jnp.minimum(i, b - 1), 0, 0))
            high = pl.BlockSpec((per, rows, wide), lambda i, *_, b=blocks: (b + jnp.minimum(i, b - 1), 0, 0))
            if count == 1:
                job_in += [low, low]
                arrays += [keep, recv]
            else:
                job_in += [low, low, high, high]
                arrays += [keep, recv, keep, recv]
        spec = pl.BlockSpec((per, rows, columns), lambda i, *_, b=blocks: (jnp.minimum(i, b - 1), 0, 0))
        shape = jax.ShapeDtypeStruct((half, rows, columns), f32)
        outs = 1 if count == 1 else 2
        job_out += [spec] * outs
        job_shape += [shape] * outs

    def run(*refs):
        refs = list(refs)
        own = refs[: scalars + base_in]
        refs = refs[scalars + base_in :]
        ins, refs = refs[: len(job_in)], refs[len(job_in) :]
        own += refs[:base_out]
        refs = refs[base_out:]
        outs, rest = refs[: len(job_out)], refs[len(job_out) :]
        kernel(*own, *rest)
        step = pl.program_id(0)
        for job, (count, _, _, _, blocks) in zip(jobs, plans):
            parts_in = ins[: len(job) * (2 if count == 1 else 4)]
            ins = ins[len(parts_in) :]
            parts_out = outs[: 1 if count == 1 else 2]
            outs = outs[len(parts_out) :]

            @pl.when(step < blocks)
            def _(job=job, parts_in=parts_in, parts_out=parts_out):
                at = 0
                group = len(parts_in) // len(job)
                for n, (keep, _) in enumerate(job):
                    wide = keep.shape[2]
                    refs_in = parts_in[n * group : (n + 1) * group]
                    parts_out[0][:, :, at : at + wide] = refs_in[0][...] + refs_in[1][...]
                    if group == 4:
                        parts_out[1][:, :, at : at + wide] = refs_in[2][...] + refs_in[3][...]
                    at += wide

    grid_spec = pltpu.PrefetchScalarGridSpec(
        num_scalar_prefetch=scalars,
        grid=(steps,),
        in_specs=in_specs + job_in,
        out_specs=out_specs + job_out,
        scratch_shapes=call.pop("scratch_shapes", []),
    )
    operands = call.pop("operands")
    results = pl.pallas_call(
        run, grid_spec=grid_spec, out_shape=out_shape + job_shape, compiler_params=params(), **call
    )(*operands, *arrays)
    results = list(results)
    own, rest = results[:base_out], results[base_out:]
    sums = []
    for count, *_ in plans:
        outs = 1 if count == 1 else 2
        sums.append((None, rest[0]) if outs == 1 else (rest[1], rest[0]))
        rest = rest[outs:]
    return own, sums


def add_only(jobs, name):
    steps = max(1, max(job[0][0].shape[0] // 2 for job in jobs))
    return with_jobs(lambda *refs: None, 0, steps, [], [], [], jobs, operands=[], name=name)[1]


def prep_kernel(len_ref, tok_ref, cot_ref, gain_ref, normed_ref, g_ref):
    tile = tok_ref.shape[0]
    x = tok_ref[...].astype(f32)
    centered = x - jnp.mean(x, axis=-1, keepdims=True)
    var = jnp.mean(centered * centered, axis=-1, keepdims=True)
    normed_ref[...] = (centered * lax.rsqrt(var + EPSILON) * gain_ref[...]).astype(bf16)
    rows = pl.program_id(0) * tile + lax.broadcasted_iota(jnp.int32, (tile, 1), 0)
    valid = jnp.where(rows < len_ref[0], 1.0, 0.0)
    g_ref[...] = (cot_ref[...].astype(f32) * valid).astype(bf16)


def prep(lengths, tokens, cotangent, gain):
    rows = tokens.shape[0]
    tile = 256
    spec = pl.BlockSpec((tile, D), lambda i, n: (i, 0))
    shape = jax.ShapeDtypeStruct((rows, D), bf16)
    return pl.pallas_call(
        prep_kernel,
        grid_spec=pltpu.PrefetchScalarGridSpec(
            num_scalar_prefetch=1,
            grid=(rows // tile,),
            in_specs=[spec, spec, pl.BlockSpec((1, D), lambda i, n: (0, 0))],
            out_specs=[spec, spec],
        ),
        out_shape=[shape, shape],
        compiler_params=params(),
        name="prep",
    )(lengths, tokens, cotangent, gain)


ANY = pl.BlockSpec(memory_space=pl.ANY)


def copies(sources, targets, sems):
    return [pltpu.make_async_copy(a, b, sems.at[i]) for i, (a, b) in enumerate(zip(sources, targets))]


def piece_copy(table_ref, acc, share, rows, send_ref, keep_ref, sem, wait):
    half = keep_ref.shape[0]
    place = table_ref[share]
    source = acc.at[pl.ds(share * rows, rows), :]

    @pl.when(place >= half)
    def _():
        copy = pltpu.make_async_copy(source, send_ref.at[place - half], sem)
        copy.wait() if wait else copy.start()

    @pl.when(place < half)
    def _():
        copy = pltpu.make_async_copy(source, keep_ref.at[place], sem)
        copy.wait() if wait else copy.start()


def pieces_out(table_ref, acc, start, count, rows, send_ref, keep_ref, sems, wait=False):
    for share in range(start // rows, (start + count) // rows):
        piece_copy(table_ref, acc, share, rows, send_ref, keep_ref, sems.at[share], wait)


def piece_shapes(parts, rows, columns):
    shape = jax.ShapeDtypeStruct((parts // 2, rows, columns), f32)
    return [shape, shape]


def unit_sources(w_in_ref, w_out_ref, core, start, units, parts, streams, gathered):
    if gathered:
        return [(w_in_ref.at[:, pl.ds(start, units)], w_out_ref.at[pl.ds(start, units), :], 0, units)]
    unit = FF // (parts * streams)
    strips = []
    for at in range(start, start + units, unit):
        first = pl.multiple_of((at // unit * streams + core) * unit, unit)
        strips.append((w_in_ref.at[:, pl.ds(first, unit)], w_out_ref.at[pl.ds(first, unit), :], at - start, unit))
    return strips


def gather_units(core, w_in, w_out, parts, streams):
    unit = FF // (parts * streams)
    if unit % 128 == 0:
        return w_in, w_out, False
    a = lax.dynamic_index_in_dim(w_in.reshape(D, parts, streams, unit), core[0], 2, False)
    b = lax.dynamic_index_in_dim(w_out.reshape(parts, streams, unit, D), core[0], 1, False)
    return a.reshape(D, parts * unit), b.reshape(parts * unit, D), True


def gelu_parts(x):
    density = jnp.exp(x * x * -0.5)
    t = 1.0 / (1.0 + (0.3275911 / math.sqrt(2.0)) * jnp.abs(x))
    poly = 1.061405429 * t - 1.453152027
    poly = poly * t + 1.421413741
    poly = poly * t - 0.284496736
    poly = (poly * t + 0.254829592) * t
    tail = 0.5 * poly * density
    cdf = jnp.where(x >= 0, 1.0 - tail, tail)
    return x * cdf, cdf + x * density * (1.0 / math.sqrt(2.0 * math.pi))


TILE = 256


def ff_kernel(
    strips_of, start, steps, share_rows, core_ref, table_ref, normed_hbm, g_hbm, win_hbm, wout_hbm, *rest
):
    act_hbm, dh_hbm, send_hbm, keep_hbm = rest[-21:-17]
    normed, g, win, wout, h_a, h_b, d_a, d_b, act, d_hidden, acc = rest[-17:-6]
    row_sem, g_sem, in_sem, out_sem, piece_sem, store_sem = rest[-6:]
    step = pl.program_id(0)
    units = win.shape[1]
    rows = normed.shape[0]
    tile = 2 * TILE
    strips = strips_of(win_hbm, wout_hbm, core_ref[0])
    in_copies = copies([a for a, _, _, _ in strips], [win.at[:, pl.ds(at, n)] for _, _, at, n in strips], in_sem)
    out_copies = copies([b for _, b, _, _ in strips], [wout.at[pl.ds(at, n), :] for _, _, at, n in strips], out_sem)

    def row_copy(i, hbm, vmem, sem):
        here = pl.ds(pl.multiple_of(i * tile, tile), tile)
        return pltpu.make_async_copy(hbm.at[here, :], vmem.at[here, :], sem.at[i])

    @pl.when(step == 0)
    def _():
        row_copy(0, normed_hbm, normed, row_sem).start()
        for copy in in_copies:
            copy.start()
        row_copy(0, g_hbm, g, g_sem).start()
        for copy in out_copies:
            copy.start()
        for i in range(1, steps):
            row_copy(i, normed_hbm, normed, row_sem).start()
            row_copy(i, g_hbm, g, g_sem).start()
        for copy in in_copies + out_copies:
            copy.wait()

    def finish_tile(h, d, place):
        value, slope = gelu_parts(h[...])
        here = pl.ds(pl.multiple_of(place, TILE), TILE)
        act[here, :] = value.astype(bf16)
        d_hidden[here, :] = (d[...] * slope).astype(bf16)

    @pl.when(step < steps)
    def _():
        row_copy(step, normed_hbm, normed, row_sem).wait()
        row_copy(step, g_hbm, g, g_sem).wait()
        first = pl.multiple_of(step * tile, tile)
        here_a, here_b = pl.ds(first, TILE), pl.ds(first + TILE, TILE)
        finish_tile(h_b, d_b, step * tile)
        h_a[...] = dot(normed[here_a, :], win[...])
        d_a[...] = dot_nt(g[here_a, :], wout[...])
        finish_tile(h_a, d_a, step * tile + TILE)
        h_b[...] = dot(normed[here_b, :], win[...])
        d_b[...] = dot_nt(g[here_b, :], wout[...])

    columns = pl.ds(start, units)
    stores = [
        pltpu.make_async_copy(act.at[pl.ds(TILE, rows), :], act_hbm.at[:, columns], store_sem.at[0]),
        pltpu.make_async_copy(d_hidden.at[pl.ds(TILE, rows), :], dh_hbm.at[:, columns], store_sem.at[1]),
    ]

    @pl.when(step == steps)
    def _():
        finish_tile(h_b, d_b, step * tile)
        for copy in stores:
            copy.start()

    wide = 512
    for m in range(D // wide):

        @pl.when(step == steps + m)
        def _(m=m):
            acc[m * wide : (m + 1) * wide, :] = dot_tn(
                normed[:, m * wide : (m + 1) * wide], d_hidden[TILE : TILE + rows, :]
            )
            pieces_out(table_ref, acc, m * wide, wide, share_rows, send_hbm, keep_hbm, piece_sem)

    @pl.when(step == pl.num_programs(0) - 1)
    def _():
        pieces_out(table_ref, acc, 0, D, share_rows, send_hbm, keep_hbm, piece_sem, True)
        for copy in stores:
            copy.wait()


def ff_chunk(core, table, normed, g, weights, start, units, earlier, parts, streams, jobs=()):
    w_in, w_out, gathered = weights
    rows = normed.shape[0]
    total = FF // streams
    steps = rows // (2 * TILE)
    strips = 1 if gathered else units // (FF // (parts * streams))

    def strips_of(w_in_ref, w_out_ref, c):
        return unit_sources(w_in_ref, w_out_ref, c, start, units, parts, streams, gathered)

    low = jax.ShapeDtypeStruct((rows, total), bf16)
    return with_jobs(
        partial(ff_kernel, strips_of, start, steps, D // parts),
        2,
        steps + D // 512,
        [ANY] * (4 + len(earlier)),
        [ANY] * 4,
        [low, low] + piece_shapes(parts, D // parts, units),
        jobs,
        operands=[core, table, normed, g, w_in, w_out, *earlier],
        scratch_shapes=[
            pltpu.VMEM((rows, D), bf16),
            pltpu.VMEM((rows, D), bf16),
            pltpu.VMEM((D, units), bf16),
            pltpu.VMEM((units, D), bf16),
            pltpu.VMEM((TILE, units), f32),
            pltpu.VMEM((TILE, units), f32),
            pltpu.VMEM((TILE, units), f32),
            pltpu.VMEM((TILE, units), f32),
            pltpu.VMEM((rows + TILE, units), bf16),
            pltpu.VMEM((rows + TILE, units), bf16),
            pltpu.VMEM((D, units), f32),
            pltpu.SemaphoreType.DMA((steps,)),
            pltpu.SemaphoreType.DMA((steps,)),
            pltpu.SemaphoreType.DMA((strips,)),
            pltpu.SemaphoreType.DMA((strips,)),
            pltpu.SemaphoreType.DMA((parts,)),
            pltpu.SemaphoreType.DMA((2,)),
        ],
        input_output_aliases={6: 0, 7: 1} if earlier else {},
        cost_estimate=pl.CostEstimate(
            flops=6 * rows * D * units,
            bytes_accessed=2 * (2 * rows * D + 2 * units * D + 2 * rows * units) + 4 * D * units,
            transcendentals=rows * units,
        ),
        name=f"ff_chunk_{start}",
    )


def out_grad_kernel(share_rows, table_ref, left_ref, right_ref, after_ref, send_hbm, keep_hbm, acc, piece_sem):
    width = left_ref.shape[1]
    for m in range(acc.shape[0] // width):

        @pl.when(pl.program_id(0) == m)
        def _(m=m):
            acc[m * width : (m + 1) * width, :] = dot_tn(left_ref[...], right_ref[...])
            pieces_out(table_ref, acc, m * width, width, share_rows, send_hbm, keep_hbm, piece_sem)

    @pl.when(pl.program_id(0) == pl.num_programs(0) - 1)
    def _():
        pieces_out(table_ref, acc, 0, acc.shape[0], share_rows, send_hbm, keep_hbm, piece_sem, True)


def out_grad_pieces(table, left, right, block, columns, after, parts, jobs=()):
    rows, total = left.shape
    width = 512
    return with_jobs(
        partial(out_grad_kernel, total // parts),
        1,
        total // width,
        [
            pl.BlockSpec((rows, width), lambda i, t: (0, i)),
            pl.BlockSpec((rows, columns), lambda i, t: (0, block)),
            ANY,
        ],
        [ANY, ANY],
        piece_shapes(parts, total // parts, columns),
        jobs,
        operands=[table, left, right, after],
        scratch_shapes=[pltpu.VMEM((total, columns), f32), pltpu.SemaphoreType.DMA((parts,))],
        cost_estimate=pl.CostEstimate(
            flops=2 * rows * total * columns,
            bytes_accessed=2 * rows * (total + columns) + 4 * total * columns,
            transcendentals=0,
        ),
        name=f"out_grad_{block}",
    )


def proj_grad_kernel(
    share_rows, core_ref, table_ref, mine_ref, other_ref, right_ref, after_ref, send_hbm, keep_hbm, acc, piece_sem
):
    width = mine_ref.shape[1]
    core = core_ref[0]
    step = pl.program_id(0)

    @pl.when(step == 0)
    def _():
        acc[pl.ds(pl.multiple_of(core * width, width), width), :] = dot_tn(mine_ref[...], right_ref[...])

    @pl.when(step == 1)
    def _():
        acc[pl.ds(pl.multiple_of((1 - core) * width, width), width), :] = dot_tn(
            other_ref[...].astype(bf16), right_ref[...]
        )
        pieces_out(table_ref, acc, 0, acc.shape[0], share_rows, send_hbm, keep_hbm, piece_sem)
        pieces_out(table_ref, acc, 0, acc.shape[0], share_rows, send_hbm, keep_hbm, piece_sem, True)


def proj_grad_pieces(core, table, mine, other, right, after, parts, streams, jobs=()):
    rows, part = mine.shape
    columns = D // streams
    return with_jobs(
        partial(proj_grad_kernel, D // parts),
        2,
        2,
        [
            pl.BlockSpec((rows, part), lambda i, c, t: (0, 0)),
            pl.BlockSpec((rows, part), lambda i, c, t: (0, 0)),
            pl.BlockSpec((rows, columns), lambda i, c, t: (0, c[0])),
            ANY,
        ],
        [ANY, ANY],
        piece_shapes(parts, D // parts, columns),
        jobs,
        operands=[core, table, mine, other, right, after],
        scratch_shapes=[pltpu.VMEM((D, columns), f32), pltpu.SemaphoreType.DMA((parts,))],
        cost_estimate=pl.CostEstimate(
            flops=2 * rows * D * columns,
            bytes_accessed=rows * (6 * part + 2 * columns) + 4 * D * columns,
            transcendentals=0,
        ),
        name="proj_grad",
    )


def causal_mask(transposed):
    row = lax.broadcasted_iota(jnp.int32, (BLK, BLK), 0)
    col = lax.broadcasted_iota(jnp.int32, (BLK, BLK), 1)
    return col >= row if transposed else row >= col


def head_masks():
    lane = lax.broadcasted_iota(jnp.int32, (1, PAIR), 1)
    first = lane < HEAD
    m0 = jnp.where(first, 1.0, 0.0)
    return m0.astype(bf16), (1.0 - m0).astype(bf16)


def state_mask():
    row = lax.broadcasted_iota(jnp.int32, (PAIR, 2 * PAIR), 0)
    col = lax.broadcasted_iota(jnp.int32, (PAIR, 2 * PAIR), 1)
    return (row < HEAD) == (col < PAIR)


def attention_forward_kernel(
    groups, len_ref, core_ref, normed_ref, wq_ref, wk_ref, wv_ref, cos_ref, sin_ref, fw_ref, map_ref, after_ref,
    q_ref, k_ref, v_ref, mix_ref, den_ref, state_ref, send_ref, state,
):
    block = pl.program_id(0)

    @pl.when(block == 0)
    def _():
        state[...] = jnp.zeros_like(state)

    rows = normed_ref[...]
    queries_all, keys_all, values_all = dot(rows, wq_ref[...]), dot(rows, wk_ref[...]), dot(rows, wv_ref[...])
    cosine, sine = cos_ref[...], sin_ref[...]
    place = block * BLK + lax.broadcasted_iota(jnp.int32, (BLK, 1), 0)
    valid = jnp.where(place < len_ref[0], 1.0, 0.0)
    m0, m1 = head_masks()
    causal = causal_mask(False)
    keep_state = state_mask()
    first = lax.broadcasted_iota(jnp.int32, (BLK, PAIR), 1) < HEAD
    for group in range(groups):
        here = slice(group * PAIR, (group + 1) * PAIR)
        queries, keys = queries_all[:, here], keys_all[:, here]
        turned = jnp.concatenate(
            [
                jnp.concatenate([queries * cosine, queries * sine], 1),
                jnp.concatenate([keys * cosine, keys * sine], 1),
            ],
            0,
        )
        high = turned.astype(bf16)
        low = (turned - high.astype(f32)).astype(bf16)
        main = dot(high, map_ref[...])
        exponent = main[:, :PAIR] + main[:, PAIR:] + dot(low, map_ref[:, :PAIR])
        phi = jnp.exp(exponent) * fw_ref[:, here]
        q = phi[:BLK].astype(bf16)
        k = (phi[BLK:] * valid).astype(bf16)
        v = values_all[:, here].astype(bf16)
        q_ref[:, here] = q
        k_ref[:, here] = k
        v_ref[:, here] = v
        v0, v1 = v * m0 + m1, v * m1 + m0
        s0 = jnp.where(causal, dot_nt(q * m0, k), 0.0).astype(bf16)
        s1 = jnp.where(causal, dot_nt(q * m1, k), 0.0).astype(bf16)
        before = jnp.where(keep_state, state[group], 0.0).astype(bf16)
        state_ref[group, 0] = before
        far = dot(q, before)
        o0 = dot(s0, v0) + far[:, :PAIR]
        o1 = dot(s1, v1) + far[:, PAIR:]
        numerator = jnp.where(first, o0, o1)
        denominator = pltpu.roll(jnp.where(first, o1, o0), HEAD, 1)
        mixed = (numerator / denominator).astype(bf16)
        mix_ref[:, here] = mixed
        send_ref[:, here] = mixed.astype(f32)
        den_ref[:, here] = denominator
        state[group] += dot_tn(k, jnp.concatenate([v0, v1], 1))


def attention_forward(
    lengths, core, normed, w_qkv, cosine, sine, feature_weight, table, after, streams, jobs=()
):
    rows = normed.shape[0]
    groups = HEADS // streams // 2
    width = groups * PAIR
    blocks = rows // BLK
    row_spec = pl.BlockSpec((BLK, width), lambda b, n, c: (b, 0))
    table_spec = pl.BlockSpec((BLK, PAIR), lambda b, n, c: (b, 0))
    low_shape = jax.ShapeDtypeStruct((rows, width), bf16)
    wide_shape = jax.ShapeDtypeStruct((rows, width), f32)

    def weight_spec(which):
        return pl.BlockSpec((D, width), lambda b, n, c: (0, which * streams + c[0]))

    return with_jobs(
        partial(attention_forward_kernel, groups),
        2,
        blocks,
        [
            pl.BlockSpec((BLK, D), lambda b, n, c: (b, 0)),
            weight_spec(0),
            weight_spec(1),
            weight_spec(2),
            table_spec,
            table_spec,
            pl.BlockSpec((1, width), lambda b, n, c: (0, c[0])),
            pl.BlockSpec((2 * PAIR, 2 * PAIR), lambda b, n, c: (0, 0)),
            ANY,
        ],
        [
            row_spec,
            row_spec,
            row_spec,
            row_spec,
            row_spec,
            pl.BlockSpec((groups, 1, PAIR, 2 * PAIR), lambda b, n, c: (0, b, 0, 0)),
            row_spec,
        ],
        [
            low_shape,
            low_shape,
            low_shape,
            low_shape,
            wide_shape,
            jax.ShapeDtypeStruct((groups, blocks, PAIR, 2 * PAIR), bf16),
            wide_shape,
        ],
        jobs,
        operands=[lengths, core, normed, w_qkv, w_qkv, w_qkv, cosine, sine, feature_weight, table, after],
        scratch_shapes=[pltpu.VMEM((groups, PAIR, 2 * PAIR), f32)],
        cost_estimate=pl.CostEstimate(
            flops=groups * blocks * 2 * 65536 * 4600,
            bytes_accessed=rows * D * 2 + 3 * D * width * 2 + rows * width * 16,
            transcendentals=2 * rows * width,
        ),
        name="attention_forward",
    )


def attention_backward_kernel(
    blocks, groups, share_rows, core_ref, table_ref, g_ref, wp_ref, q_ref, k_ref, v_ref, mix_ref, den_ref, state_ref,
    cos_ref, sin_ref, back_ref, back_low_ref, sums_ref, normed_hbm, *rest,
):
    dq_ref, dk_ref, dv_ref, fg_ref, send_hbm, keep_hbm, later, d_all, acc, normed, load_sem, piece_sem = rest[-12:]
    step = pl.program_id(0)
    width = groups * PAIR
    load = pltpu.make_async_copy(normed_hbm, normed, load_sem)

    @pl.when(step == 0)
    def _():
        load.start()
        later[...] = jnp.zeros_like(later)
        fg_ref[...] = jnp.zeros_like(fg_ref)

    @pl.when(step < blocks)
    def _():
        m0, m1 = head_masks()
        first = lax.broadcasted_iota(jnp.int32, (BLK, PAIR), 1) < HEAD
        left = lax.broadcasted_iota(jnp.int32, (PAIR, PAIR), 1) < HEAD
        own = (lax.broadcasted_iota(jnp.int32, (PAIR, PAIR), 0) < HEAD) == left
        causal, flipped = causal_mask(False), causal_mask(True)
        keep_state = state_mask()
        cosine, sine = cos_ref[...], sin_ref[...]
        d_mixed_all = dot_nt(g_ref[...], wp_ref[...])
        place = pl.ds(pl.multiple_of((blocks - 1 - step) * BLK, BLK), BLK)
        for group in range(groups):
            here = slice(group * PAIR, (group + 1) * PAIR)
            numer = d_mixed_all[:, here] / den_ref[:, here]
            product = numer * mix_ref[:, here].astype(f32)
            p_high = product.astype(bf16)
            p_low = (product - p_high.astype(f32)).astype(bf16)
            sums = dot(jnp.concatenate([p_high, p_low], 1), sums_ref[...])
            d_o0 = jnp.where(first, numer, -sums).astype(bf16)
            d_o1 = jnp.where(first, -sums, numer).astype(bf16)
            low = numer.astype(bf16)
            dn0, dn1 = low * m0, low * m1
            q, k, v = q_ref[:, here], k_ref[:, here], v_ref[:, here]
            q0, q1 = q * m0, q * m1
            v0, v1 = v * m0 + m1, v * m1 + m0
            ds0 = jnp.where(causal, dot_nt(d_o0, v0), 0.0).astype(bf16)
            ds1 = jnp.where(causal, dot_nt(d_o1, v1), 0.0).astype(bf16)
            st0 = jnp.where(flipped, dot_nt(k, q0), 0.0).astype(bf16)
            st1 = jnp.where(flipped, dot_nt(k, q1), 0.0).astype(bf16)
            dst0 = jnp.where(flipped, dot_nt(v0, d_o0), 0.0).astype(bf16)
            dst1 = jnp.where(flipped, dot_nt(v1, d_o1), 0.0).astype(bf16)
            d_o = jnp.concatenate([d_o0, d_o1], 1)
            behind = later[group]
            after = jnp.where(keep_state, behind, 0.0).astype(bf16)
            after_v = jnp.where(own, jnp.where(left, behind[:, :PAIR], behind[:, PAIR:]), 0.0).astype(bf16)
            k0, k1 = k * m0, k * m1
            d_q = dot_nt(d_o, state_ref[group, 0]) + dot(ds0, k0) + dot(ds1, k1)
            d_k = dot_nt(jnp.concatenate([v0, v1], 1), after) + dot(dst0, q0) + dot(dst1, q1)
            d_v = dot(k, after_v) + dot(st0, dn0) + dot(st1, dn1)
            later[group] += dot_tn(q, d_o)
            e_q = d_q * q.astype(f32)
            e_k = d_k * k.astype(f32)
            both = jnp.concatenate([e_q, e_k], 0)
            fg_ref[:, here] += jnp.sum((e_q + e_k).reshape(BLK // 8, 8, PAIR), axis=0)
            high = both.astype(bf16)
            lower = (both - high.astype(f32)).astype(bf16)
            turned = dot(jnp.concatenate([high, lower], 1), back_ref[...]) + dot(high, back_low_ref[...])
            dq = (turned[:BLK, :PAIR] * cosine + turned[:BLK, PAIR:] * sine).astype(bf16)
            dk = (turned[BLK:, :PAIR] * cosine + turned[BLK:, PAIR:] * sine).astype(bf16)
            dv = d_v.astype(bf16)
            dq_ref[:, here] = dq
            dk_ref[:, here] = dk
            dv_ref[:, here] = dv
            d_all[place, group * PAIR : (group + 1) * PAIR] = dq
            d_all[place, width + group * PAIR : width + (group + 1) * PAIR] = dk
            d_all[place, 2 * width + group * PAIR : 2 * width + (group + 1) * PAIR] = dv

    @pl.when(step == blocks)
    def _():
        load.wait()

    wide = 512
    for m in range(D // wide):

        @pl.when(step == blocks + m)
        def _(m=m):
            acc[m * wide : (m + 1) * wide, :] = dot_tn(normed[:, m * wide : (m + 1) * wide], d_all[...])
            pieces_out(table_ref, acc, m * wide, wide, share_rows, send_hbm, keep_hbm, piece_sem)

    @pl.when(step == pl.num_programs(0) - 1)
    def _():
        pieces_out(table_ref, acc, 0, D, share_rows, send_hbm, keep_hbm, piece_sem, True)


def attention_backward(
    core, table, g, w_proj, kept, cosine, sine, backs, sums, normed, call, groups, earlier, after, parts, streams, jobs=()
):
    q, k, v, mixed, den, states = kept[:6]
    rows = g.shape[0]
    calls = HEADS // streams // 2 // groups
    blocks = rows // BLK
    width = groups * PAIR

    def at(i):
        return jnp.maximum(blocks - 1 - i, 0)

    row_spec = pl.BlockSpec((BLK, width), lambda i, c, t: (at(i), call))
    table_spec = pl.BlockSpec((BLK, PAIR), lambda i, c, t: (at(i), 0))
    low_shape = jax.ShapeDtypeStruct((rows, calls * width), bf16)
    return with_jobs(
        partial(attention_backward_kernel, blocks, groups, D // parts),
        2,
        blocks + D // 512,
        [
            pl.BlockSpec((BLK, D), lambda i, c, t: (at(i), 0)),
            pl.BlockSpec((width, D), lambda i, c, t: (c[0] * calls + call, 0)),
            row_spec,
            row_spec,
            row_spec,
            row_spec,
            row_spec,
            pl.BlockSpec((groups, 1, PAIR, 2 * PAIR), lambda i, c, t: (call, at(i), 0, 0)),
            table_spec,
            table_spec,
            pl.BlockSpec((2 * PAIR, 2 * PAIR), lambda i, c, t: (0, 0)),
            pl.BlockSpec((PAIR, 2 * PAIR), lambda i, c, t: (0, 0)),
            pl.BlockSpec((2 * PAIR, PAIR), lambda i, c, t: (0, 0)),
            ANY,
            ANY,
        ]
        + [ANY] * len(earlier),
        [row_spec, row_spec, row_spec, pl.BlockSpec((8, width), lambda i, c, t: (0, 0)), ANY, ANY],
        [low_shape, low_shape, low_shape, jax.ShapeDtypeStruct((8, width), f32)]
        + piece_shapes(parts, D // parts, 3 * width),
        jobs,
        operands=[
            core, table, g, w_proj, q, k, v, mixed, den, states, cosine, sine, *backs, sums, normed, after, *earlier
        ],
        scratch_shapes=[
            pltpu.VMEM((groups, PAIR, 2 * PAIR), f32),
            pltpu.VMEM((rows, 3 * width), bf16),
            pltpu.VMEM((D, 3 * width), f32),
            pltpu.VMEM((rows, D), bf16),
            pltpu.SemaphoreType.DMA,
            pltpu.SemaphoreType.DMA((parts,)),
        ],
        input_output_aliases={17: 0, 18: 1, 19: 2} if earlier else {},
        cost_estimate=pl.CostEstimate(
            flops=2 * 65536 * groups * (blocks * 6500 + 16384),
            bytes_accessed=2 * (2 * rows * D + width * D + rows * width * 12) + 4 * D * 3 * width,
            transcendentals=0,
        ),
        name=f"attention_backward_{call}",
    )


def tail_kernel(
    strips_of, tiles, act_ref, dh_ref, mix_ref, dq_ref, dk_ref, dv_ref, tok_ref, cot_ref, valid_ref, gain_ref,
    wproj_ref, wq_ref, wk_ref, wv_ref, win_hbm, wout_hbm, out_ref, grad_ref,
    win, wout, mine, arrived, in_sem, out_sem, send_sem, recv_sem,
):
    step = pl.program_id(0)
    chip, core = lax.axis_index("dp"), lax.axis_index("stream")
    partner = (chip, 1 - core)
    strips = strips_of(win_hbm, wout_hbm, core)
    loads = copies([a for a, _, _, _ in strips], [win.at[:, pl.ds(at, n)] for _, _, at, n in strips], in_sem)
    loads += copies([b for _, b, _, _ in strips], [wout.at[pl.ds(at, n), :] for _, _, at, n in strips], out_sem)

    def send(i):
        return pltpu.make_async_remote_copy(
            src_ref=mine.at[lax.rem(i, 2)],
            dst_ref=arrived.at[i],
            send_sem=send_sem.at[i],
            recv_sem=recv_sem.at[i],
            device_id=partner,
            device_id_type=pl.DeviceIdType.MESH,
        )

    @pl.when(step == 0)
    def _():
        for load in loads:
            load.start()
        barrier = pltpu.get_barrier_semaphore()
        pl.semaphore_signal(barrier, inc=1, device_id=partner, device_id_type=pl.DeviceIdType.MESH)
        pl.semaphore_wait(barrier, 1)
        for load in loads:
            load.wait()

    @pl.when((step >= 2) & (step < tiles))
    def _():
        send(step - 2).wait_send()

    @pl.when(step < tiles)
    def _():
        slot = lax.rem(step, 2)
        mine[slot, 0] = dot(act_ref[...], wout[...]) + dot(mix_ref[...], wproj_ref[...])
        d_normed = dot_nt(dh_ref[...], win[...]) + dot_nt(dq_ref[...], wq_ref[...])
        d_normed += dot_nt(dk_ref[...], wk_ref[...]) + dot_nt(dv_ref[...], wv_ref[...])
        mine[slot, 1] = d_normed
        send(step).start()

    @pl.when(step >= 1)
    def _():
        send(step - 1).wait_recv()
        slot = lax.rem(step + 1, 2)
        x = tok_ref[...].astype(f32)
        centered = x - jnp.mean(x, axis=-1, keepdims=True)
        var = jnp.mean(centered * centered, axis=-1, keepdims=True)
        inv_std = lax.rsqrt(var + EPSILON)
        unit = centered * inv_std
        out_ref[...] = (x + (mine[slot, 0] + arrived[step - 1, 0]) * valid_ref[...]).astype(bf16)
        scaled = (mine[slot, 1] + arrived[step - 1, 1]) * gain_ref[...]
        mean = jnp.mean(scaled, axis=-1, keepdims=True)
        cross = jnp.mean(scaled * unit, axis=-1, keepdims=True)
        grad_ref[...] = (cot_ref[...].astype(f32) + inv_std * (scaled - mean - unit * cross)).astype(bf16)

    @pl.when(step == tiles)
    def _():
        send(tiles - 2).wait_send()
        send(tiles - 1).wait_send()


def tail(active, d_hidden, mixed, d_qkv, tokens, cotangent, valid, gain, weights, w_proj, w_qkv, parts, streams):
    w_in, w_out, gathered = weights
    rows, units = active.shape
    width = mixed.shape[1]
    tiles = rows // TILE
    strips = 1 if gathered else parts

    def strips_of(w_in_ref, w_out_ref, core):
        return unit_sources(w_in_ref, w_out_ref, core, 0, units, parts, streams, gathered)

    def now(i):
        return (jnp.minimum(i, tiles - 1), 0)

    def before(i):
        return (jnp.maximum(i - 1, 0), 0)

    def weight(which):
        return pl.BlockSpec((D, width), lambda i: (0, which * streams + lax.axis_index("stream")))

    shape = jax.ShapeDtypeStruct((rows, D), bf16)
    return pl.pallas_call(
        partial(tail_kernel, strips_of, tiles),
        grid=(tiles + 1,),
        in_specs=[
            pl.BlockSpec((TILE, units), now),
            pl.BlockSpec((TILE, units), now),
            pl.BlockSpec((TILE, width), now),
            pl.BlockSpec((TILE, width), now),
            pl.BlockSpec((TILE, width), now),
            pl.BlockSpec((TILE, width), now),
            pl.BlockSpec((TILE, D), before),
            pl.BlockSpec((TILE, D), before),
            pl.BlockSpec((TILE, 1), before),
            pl.BlockSpec((1, D), lambda i: (0, 0)),
            pl.BlockSpec((width, D), lambda i: (lax.axis_index("stream"), 0)),
            weight(0),
            weight(1),
            weight(2),
            ANY,
            ANY,
        ],
        out_specs=[pl.BlockSpec((TILE, D), before), pl.BlockSpec((TILE, D), before)],
        out_shape=[shape, shape],
        scratch_shapes=[
            pltpu.VMEM((D, units), bf16),
            pltpu.VMEM((units, D), bf16),
            pltpu.VMEM((2, 2, TILE, D), f32),
            pltpu.VMEM((tiles, 2, TILE, D), f32),
            pltpu.SemaphoreType.DMA((strips,)),
            pltpu.SemaphoreType.DMA((strips,)),
            pltpu.SemaphoreType.DMA((tiles,)),
            pltpu.SemaphoreType.DMA((tiles,)),
        ],
        compiler_params=params(collective_id=0, has_side_effects=True),
        cost_estimate=pl.CostEstimate(
            flops=2 * rows * D * (2 * units + 4 * width),
            bytes_accessed=2 * (rows + D) * (2 * units + 4 * width) + 8 * rows * D,
            transcendentals=0,
        ),
        name="tail",
    )(
        active, d_hidden, mixed, *d_qkv, tokens, cotangent, valid, gain, w_proj, w_qkv, w_qkv, w_qkv, w_in, w_out
    )


def send_orders(parts, streams, kind):
    bits = [1 << b for b in range(parts.bit_length() - 1)]
    first = {"xy": ("xzy", "yzx"), "zz": ("zxy", "zyx"), "xx": ("xyz", "yxz")}[kind]
    orders = []
    for s in range(streams):
        order = list(bits)
        if len(bits) >= 3:
            order[:3] = [bits["xyz".index(axis)] for axis in first[s % 2]]
        orders.append(order)
    return orders


def relative_table(orders, parts):
    table = np.zeros((len(orders), parts), np.int32)
    for s, order in enumerate(orders):
        for p in range(parts):
            for b, mask in enumerate(order):
                if p >> (len(order) - 1 - b) & 1:
                    table[s, p] ^= mask
    return table


KINDS = ("xy", "zz", "xx")
FF_PLAN = ((512, "xy", ()), (512, "xy", ()), (1024, "xy", ("in0",)))
OUT_PLAN = (("xy", ("in1",)), ("xy", ("in0",)))
FORWARD_PLAN = ("in2", "in1")
PROJ_AT = 1
BACKWARD_PLAN = (("xy", ("out0",)), ("xy", ("out1",)))
PROJ_PLAN = ("xy", ("in2",))
AFTER_PLAN = ()


def solution(mesh):
    parts, streams = mesh.shape["dp"], mesh.shape["stream"]
    steps = parts.bit_length() - 1
    orders = {kind: send_orders(parts, streams, kind) for kind in KINDS}
    relative = {kind: relative_table(orders[kind], parts) for kind in KINDS}
    inverse = {kind: np.argsort(relative[kind], axis=1) for kind in KINDS}
    chips = np.arange(parts)
    place_np = np.stack([inverse[kind][:, chips[:, None] ^ chips[None, :]] for kind in KINDS]).astype(np.int32)
    cosine_np, sine_np, map_np, back_high_np, back_low_np = attention_tables()
    sums_np = np.zeros((2 * PAIR, PAIR), np.float32)
    for base in (0, PAIR):
        sums_np[base : base + HEAD, HEAD] = 1.0
        sums_np[base + HEAD : base + PAIR, 0] = 1.0

    def exchange(value, kind, step):
        pairs = []
        for d in range(parts):
            for s in range(streams):
                pairs.append((d * streams + s, (d ^ orders[kind][s][step]) * streams + s))
        return lax.ppermute(value, ("dp", "stream"), pairs)

    def partner(value):
        pairs = []
        for d in range(parts):
            for s in range(streams):
                pairs.append((d * streams + s, d * streams + (s ^ 1)))
        return lax.ppermute(value, ("dp", "stream"), pairs)

    def body(tokens, norm_gain, w_qkv, w_proj, w_in, w_out, feature_weight, lengths, cotangent):
        rows = tokens.shape[0]
        chip = lax.axis_index("dp")
        stream = lax.axis_index("stream")
        core = stream.astype(jnp.int32).reshape(1)
        places = lax.dynamic_slice(
            jnp.asarray(place_np), (0, stream, chip, 0), (len(KINDS), 1, 1, parts)
        ).reshape(len(KINDS), parts)
        places = {kind: places[n] for n, kind in enumerate(KINDS)}
        gain = norm_gain.reshape(1, D)
        fw = feature_weight.reshape(1, D)
        cosine, sine = jnp.asarray(cosine_np), jnp.asarray(sine_np)
        valid = (jnp.arange(rows) < lengths[0]).astype(f32).reshape(rows, 1)
        weights = gather_units(core, w_in, w_out, parts, streams)
        units = FF // streams

        flight, final = {}, {}

        widths = {}

        def launch(name, kind, send, keep, step=0):
            widths.setdefault(name, keep.shape[2])
            flight[name] = (kind, step, keep, exchange(send, kind, step))

        def jobs_of(names):
            groups = [name if isinstance(name, tuple) else (name,) for name in names]
            return [[flight[name][2:] for name in group] for group in groups], groups

        def landed(groups, sums):
            for group, (send, keep) in zip(groups, sums):
                kind, step = flight[group[0]][:2]
                for name in group:
                    del flight[name]
                name = group[0] if len(group) == 1 else "+".join(group)
                if step == steps - 1:
                    final[name] = keep[0]
                else:
                    launch(name, kind, send, keep, step + 1)

        def step_with(function, *args, names=(), **kwargs):
            jobs, groups = jobs_of(names)
            own, sums = function(*args, jobs=jobs, **kwargs)
            landed(groups, sums)
            return own

        normed, g = prep(lengths, tokens, cotangent, gain)

        earlier, start = [], 0
        for n, (size, kind, names) in enumerate(FF_PLAN):
            act, d_hidden, send, keep = step_with(
                ff_chunk, core, places[kind], normed, g, weights, start, size, earlier, parts, streams, names=names
            )
            earlier, start = [act, d_hidden], start + size
            launch(f"in{n}", kind, send, keep)
        width = D // len(OUT_PLAN)
        for n, (kind, names) in enumerate(OUT_PLAN):
            send, keep = step_with(
                out_grad_pieces, places[kind], act, g, n, width, keep, parts, names=names
            )
            launch(f"out{n}", kind, send, keep)

        kept = step_with(
            attention_forward, lengths, core, normed, w_qkv, cosine, sine, fw, jnp.asarray(map_np), keep, streams,
            names=FORWARD_PLAN,
        )
        mixed = kept[3]
        mixed_other = partner(kept[6])

        earlier, features = [], []
        after = mixed
        backs = (jnp.asarray(back_high_np), jnp.asarray(back_low_np))
        groups = 2
        for call, (kind, names) in enumerate(BACKWARD_PLAN):
            if call == PROJ_AT:
                send, keep = step_with(
                    proj_grad_pieces, core, places[PROJ_PLAN[0]], mixed, mixed_other, g, after, parts, streams,
                    names=PROJ_PLAN[1],
                )
                launch("proj", PROJ_PLAN[0], send, keep)
                after = keep
            dq, dk, dv, feature, send, keep = step_with(
                attention_backward, core, places[kind], g, w_proj, kept, cosine, sine, backs,
                jnp.asarray(sums_np, bf16), normed, call, groups, earlier, after, parts, streams, names=names,
            )
            earlier = [dq, dk, dv]
            after = keep
            features.append(jnp.sum(feature, axis=0))
            launch(f"qkv{call}", kind, send, keep)

        def feature_shares(feature_list):
            own = jnp.concatenate(feature_list) / lax.dynamic_slice_in_dim(
                feature_weight, stream * (D // streams), D // streams
            )
            spread = jnp.concatenate([jnp.where(stream == s, own, 0.0) for s in range(streams)])
            table = jnp.zeros((parts,), jnp.int32).at[places["xy"]].set(jnp.arange(parts, dtype=jnp.int32))
            shares = spread.reshape(parts, 1, D // parts)
            hot = (table[:, None] == jnp.arange(parts)[None, :]).astype(f32)
            shares = jnp.sum(hot[:, :, None, None] * shares[None], axis=1)
            return jnp.pad(shares, ((0, 0), (0, 7), (0, 128 - D // parts)))

        shares = feature_shares(features)
        launch("feature", "xy", shares[parts // 2 :], shares[: parts // 2])
        for n, names in enumerate(AFTER_PLAN):
            jobs, lists = jobs_of(names)
            landed(lists, add_only(jobs, f"sums_{n}"))
        output, input_grad = tail(
            act, d_hidden, mixed, earlier, tokens, cotangent, valid, gain, weights, w_proj, w_qkv, parts, streams
        )
        n = 0
        while flight:
            jobs, lists = jobs_of([(name,) for name in flight])
            landed(lists, add_only(jobs, f"rest_{n}"))
            n += 1

        value = final["feature"]
        value = value + partner(value)
        share = D // (parts * streams)
        feature_grad = lax.dynamic_slice(value, (0, stream * share), (1, share)).reshape(share)

        share_rows = D // parts
        half = share_rows // streams

        def keep_rows(piece):
            return lax.dynamic_slice_in_dim(piece, stream * half, half)

        def send_rows(piece):
            return lax.dynamic_slice_in_dim(piece, (1 - stream) * half, half)

        columns = {}
        for name, piece in final.items():
            at = 0
            for part in name.split("+"):
                columns[part] = piece[:, at : at + widths[part]]
                at += widths[part]
        pieces = [columns[f"in{n}"] for n in range(len(FF_PLAN))]
        pieces += [columns[f"qkv{n}"] for n in range(len(BACKWARD_PLAN))] + [columns["proj"]]
        mine = jnp.concatenate([keep_rows(p) for p in pieces], 1)
        other = partner(jnp.concatenate([send_rows(p) for p in pieces], 1))
        a = jnp.where(stream == 0, mine, other)
        b = jnp.where(stream == 0, other, mine)
        unit = units // parts
        in_grad = jnp.concatenate(
            [src[:, unit * i : unit * (i + 1)] for i in range(parts) for src in (a, b)], 1
        )
        qa, qb = a[:, units : units + 3 * D // streams], b[:, units : units + 3 * D // streams]
        wide = groups * PAIR
        calls = HEADS // streams // 2 // groups

        def third(src, which):
            return [src[:, (3 * n + which) * wide : (3 * n + which + 1) * wide] for n in range(calls)]

        qkv_grad = jnp.concatenate(sum([third(qa, w) + third(qb, w) for w in range(3)], []), 1)
        proj_grad = jnp.concatenate([a[:, units + 3 * D // streams :], b[:, units + 3 * D // streams :]], 1)
        out_grad = jnp.concatenate([columns[f"out{n}"] for n in range(len(OUT_PLAN))], 1)
        first_row = (chip * streams + stream) * half
        w_in_rows = lax.dynamic_slice_in_dim(w_in, first_row, half).astype(f32)
        w_qkv_rows = lax.dynamic_slice_in_dim(w_qkv, first_row, half).astype(f32)
        gain_rows = lax.dynamic_slice_in_dim(norm_gain, first_row, half)
        gain_grad = (jnp.sum(w_in_rows * in_grad, 1) + jnp.sum(w_qkv_rows * qkv_grad, 1)) / gain_rows
        return output, input_grad, gain_grad, qkv_grad, proj_grad, in_grad, out_grad, feature_grad

    both = P(("dp", "stream"), None)
    return jax.shard_map(
        body,
        mesh=mesh,
        in_specs=(P("dp", None), P(), P(), P(), P(), P(), P(), P("dp"), P("dp", None)),
        out_specs=(
            P("dp", None), P("dp", None), P(("dp", "stream")), both, both, both, both, P(("dp", "stream")),
        ),
        check_vma=False,
    )
```

time: 1360 us -> 527 us (0.39)
  waiting for transfers between devices: 602 us -> 188 us
  matrix products: 340 us -> 0 us
  Pallas kernels: 0 us -> 256 us
  local copies, waits for them, and re-layouts: 245 us -> 23.8 us
  other arithmetic: 102 us -> 8.5 us
  blocking collectives: 41 us -> 0 us
  starting transfers between devices: 0.21 us -> 39.5 us
  between operations: 16.8 us -> 2.72 us
    reduce_scatter x4 -> x0, waiting for transfers between devices: 552 us -> none  [the longest x1 187 us: body(): lax.psum_scatter(g_in, ('dp', 'stream'), scatter_dimension=0, tiled=True)]
    dot_general x24 -> x0, matrix products: 340 us -> none  [the longest x1 30.7 us: attention_half(): jnp.einsum('bshi,im->bshm', queries, feature_map, precision=HIGHEST)]
    pallas_call x0 -> x15, Pallas kernels: none -> 256 us  [the longest x13 198 us: with_jobs(): pl.pallas_call(run, grid_spec=grid_spec, out_shape=out_shape + job_shape,...]
    ppermute x0 -> x39, waiting for transfers between devices: none -> 188 us  [the longest x36 188 us: exchange(): return lax.ppermute(value, ('dp', 'stream'), pairs)]
    reshape x9 -> x1, local copies, waits for them, and re-layouts: 103 us -> 0.58 us  [body(): lax.dynamic_slice(value, (0, stream * share), (1, share)).reshape(share)]
    psum x1 -> x0, waiting for transfers between devices: 47.9 us -> none  [body(): lax.psum((branch * valid_rows, d_normed), 'stream')]
    unnamed x1 -> x0, blocking collectives: 41 us -> none
    ppermute x0 -> x39, starting transfers between devices: none -> 39.5 us  [the longest x36 38.8 us: exchange(): return lax.ppermute(value, ('dp', 'stream'), pairs)]
  transfers between devices with their start and end apart: 5 -> 39, of which waited for: 5 -> 13; matrix products, arithmetic and copies ran while one was open for 3% -> 1% of each run, Pallas kernels for 0% -> 29%
where the time goes in v1:
time: 527 us; the launch traced here: 519 us
  Pallas kernels  256 us (49%)
  waiting for transfers between devices  188 us (36%)
  starting transfers between devices  39.5 us (7%)
  local copies, waits for them, and re-layouts  23.8 us (5%)
  other arithmetic  8.5 us (2%)
    pallas_call x13, Pallas kernels, with_jobs(): pl.pallas_call(run, grid_spec=grid_spec, out_shape=out_shape + job_shape,...  198 us
    ppermute x36, waiting for transfers between devices, exchange(): return lax.ppermute(value, ('dp', 'stream'), pairs)  188 us
    pallas_call x1, Pallas kernels, tail(): pl.pallas_call(partial(tail_kernel, strips_of, tiles), grid=(tiles + 1,),...  48.2 us
    ppermute x36, starting transfers between devices, exchange(): return lax.ppermute(value, ('dp', 'stream'), pairs)  38.8 us
    unnamed x141, local copies, waits for them, and re-layouts  19.7 us
  transfers between devices with their start and end apart: 39, of which 13 were waited for; matrix products, arithmetic and copies ran while one was open for 1% of the time, Pallas kernels for 29%

profile of v1, /device:TPU:0, one launch (start us, length us, event | category | flops | bytes accessed | tf_op | source)
XLA Modules:
  0.0 519.1 jit_solution(14162959503693929808)
XLA Ops:
  2.5 9.8 %prep.1 = (bf16[2048,1024]{1,0:T(8,128)(2,1)}, bf16[2048,1024]{1,0:T(8,128)(2,1)}) custom-call(s32[1]{0:T(128)} %copy.93.len_ref.refs_0_, bf16[2048,1024]{1,0:T(8,128)(2,1)} %tok_ref.3, bf16[2048,1024]{1,0:T(8,128)(2,1)} %cot_ref.3, f32[1,1024]{1,0:T(1,128)} %bitcast.45), custom_call_target="tpu_custom_call" | custom-call | tf_op jit(solution)/shard_map/prep/pallas_call | solution.py:194
  12.3 15.6 %ff_chunk_0.1 = (bf16[2048,2048]{1,0:T(8,128)(2,1)}, bf16[2048,2048]{1,0:T(8,128)(2,1)}, f32[8,64,512]{2,1,0:T(8,128)}, f32[8,64,512]{2,1,0:T(8,128)}) custom-call(s32[1]{0:T(128)} %bitcast.refs_0_.refs_1_, s32[16]{0:T(128)} %fusion.6.refs_1_.refs_0_, bf16[2048,1024]{1,0:T(8,128)(2,1)} %get-tuple-element.112.refs_2_.refs_15_, ...), custom_call_target="tpu_custom_call" | custom-call | flops 6442450944 | bytes 16777216 | tf_op jit(solution)/shard_map/ff_chunk_0/pallas_call | solution.py:160
  28.0 3.0 collective-permute-start
  31.0 15.5 %ff_chunk_512.1 = (bf16[2048,2048]{1,0:T(8,128)(2,1)}, bf16[2048,2048]{1,0:T(8,128)(2,1)}, f32[8,64,512]{2,1,0:T(8,128)}, f32[8,64,512]{2,1,0:T(8,128)}) custom-call(s32[1]{0:T(128)} %bitcast.refs_0_.refs_1_, s32[16]{0:T(128)} %fusion.6.refs_1_.refs_0_, ...), custom_call_target="tpu_custom_call", output_to_operand_aliasing={{0}: (6, {}), {1}: (7, {})} | custom-call | flops 6442450944 | bytes 16777216 | tf_op jit(solution)/shard_map/ff_chunk_512/pallas_call | solution.py:160
  47.6 28.2 %ff_chunk_1024.1 = (bf16[2048,2048]{1,0:T(8,128)(2,1)}, bf16[2048,2048]{1,0:T(8,128)(2,1)}, f32[8,64,1024]{2,1,0:T(8,128)}, f32[8,64,1024]{2,1,0:T(8,128)}, f32[...) custom-call(s32[1]{0:T(128)} %bitcast.refs_0_.refs_1_, ...), custom_call_target="tpu_custom_call", output_to_operand_aliasing={{0}: (6, {}), {1}: (7, {})} | custom-call | flops 12884901888 | bytes 25165824 | tf_op jit(solution)/shard_map/ff_chunk_1024/pallas_call | solution.py:160
  79.4 33.9 %collective-permute-done.1.refs_5_.refs_7_ = f32[8,64,512]{2,1,0:T(8,128)S(1)} collective-permute-done((f32[8,64,512]{2,1,0:T(8,128)S(1)}, f32[8,64,512]{2,1,0:T(8,128)S(1)}, u32[]{:S(2)}, u32[]{:S(2)}) %collective-permute-start.1) | collective-permute-done | bytes 1048608 | tf_op jit(solution)/shard_map/ppermute | solution.py:961
  114.3 11.6 %out_grad_0.1 = (f32[8,128,512]{2,1,0:T(8,128)}, f32[8,128,512]{2,1,0:T(8,128)}, f32[4,64,512]{2,1,0:T(8,128)}, f32[4,64,512]{2,1,0:T(8,128)}) custom-call(s32[16]{0:T(128)} %fusion.6.refs_1_.refs_0_, bf16[2048,2048]{1,0:T(8,128)(2,1)} %get-tuple-element.120.refs_1_.act_ref, bf16[2048,1024]{1,0:T(8,128)(2,1)} %get-tuple-element.113.refs_3_.refs_2_.refs_4_, ...), custom_call_target="tpu_custom_call" | custom-call | flops 4294967296 | bytes 14680064 | tf_op jit(solution)/shard_map/out_grad_0/pallas_call | solution.py:160
  128.3 11.2 %out_grad_1.1 = (f32[8,128,512]{2,1,0:T(8,128)}, f32[8,128,512]{2,1,0:T(8,128)}, f32[2,64,512]{2,1,0:T(8,128)}, f32[2,64,512]{2,1,0:T(8,128)}) custom-call(s32[16]{0:T(128)} %fusion.6.refs_1_.refs_0_, bf16[2048,2048]{1,0:T(8,128)(2,1)} %get-tuple-element.120.refs_1_.act_ref, bf16[2048,1024]{1,0:T(8,128)(2,1)} %get-tuple-element.113.refs_3_.refs_2_.refs_4_, ...), custom_call_target="tpu_custom_call" | custom-call | flops 4294967296 | bytes 14680064 | tf_op jit(solution)/shard_map/out_grad_1/pallas_call | solution.py:160
  141.1 31.3 %attention_forward.1 = (bf16[2048,512]{1,0:T(8,128)(2,1)}, bf16[2048,512]{1,0:T(8,128)(2,1)}, bf16[2048,512]{1,0:T(8,128)(2,1)}, bf16[2048,512]{1,0:T(8,128)(2,1...) custom-call(s32[1]{0:T(128)} %copy.93.len_ref.refs_0_, ...), custom_call_target="tpu_custom_call" | custom-call | flops 19293798400 | bytes 24117248 | tf_op jit(solution)/shard_map/attention_forward/pallas_call | solution.py:160
  175.4 23.2 %collective-permute-done.6.refs_18_.refs_20_ = f32[8,128,512]{2,1,0:T(8,128)S(1)} collective-permute-done((f32[8,128,512]{2,1,0:T(8,128)S(1)}, f32[8,128,512]{2,1,0:T(8,128)S(1)}, u32[]{:S(2)}, u32[]{:S(2)}) %collective-permute-start.6) | collective-permute-done | bytes 2097184 | tf_op jit(solution)/shard_map/ppermute | solution.py:961
  199.9 28.1 %attention_backward_0.1 = (bf16[2048,512]{1,0:T(8,128)(2,1)}, bf16[2048,512]{1,0:T(8,128)(2,1)}, bf16[2048,512]{1,0:T(8,128)(2,1)}, f32[8,256]{1,0:T(8,128)}, f3...) custom-call(s32[1]{0:T(128)} %bitcast.refs_0_.refs_1_, ...), custom_call_target="tpu_custom_call" | custom-call | flops 17926455296 | bytes 24641536 | tf_op jit(solution)/shard_map/attention_backward_0/pallas_call | solution.py:160
  231.3 9.6 %proj_grad.1 = (f32[8,64,512]{2,1,0:T(8,128)}, f32[8,64,512]{2,1,0:T(8,128)}, f32[2,64,1024]{2,1,0:T(8,128)}, f32[2,64,1024]{2,1,0:T(8,128)}) custom-call(s32[1]{0:T(128)} %bitcast.refs_0_.refs_1_, s32[16]{0:T(128)} %fusion.6.refs_1_.refs_0_, bf16[2048,512]{1,0:T(8,128)(2,1)} %get-tuple-element.132.refs_7_.refs_16_.refs_2_.mix_ref, ...), custom_call_target="tpu_custom_call" | custom-call | flops 2147483648 | bytes 10485760 | tf_op jit(solution)/shard_map/proj_grad/pallas_call | solution.py:160
  241.0 28.3 %attention_backward_1.1 = (bf16[2048,512]{1,0:T(8,128)(2,1)}, bf16[2048,512]{1,0:T(8,128)(2,1)}, bf16[2048,512]{1,0:T(8,128)(2,1)}, f32[8,256]{1,0:T(8,128)}, f3...) custom-call(s32[1]{0:T(128)} %bitcast.refs_0_.refs_1_, ...), custom_call_target="tpu_custom_call", output_to_operand_aliasing={{0}: (17, {}), {1}: (18, {}), {2}: (19, {})} | custom-call | flops 17926455296 | bytes 24641536 | tf_op jit(solution)/shard_map/attention_backward_1/pallas_call | solution.py:160
  272.0 7.2 %collective-permute-done.9.refs_1_.refs_3_ = f32[2,64,512]{2,1,0:T(8,128)S(1)} collective-permute-done((f32[2,64,512]{2,1,0:T(8,128)S(1)}, f32[2,64,512]{2,1,0:T(8,128)S(1)}, u32[]{:S(2)}, u32[]{:S(2)}) %collective-permute-start.9) | collective-permute-done | bytes 262176 | tf_op jit(solution)/shard_map/ppermute | solution.py:961
  280.7 4.3 collective-permute-done.10.refs_5_.refs_7_
  291.3 19.6 %collective-permute-done.17.refs_33_.refs_35_ = f32[8,8,128]{2,1,0:T(8,128)S(1)} collective-permute-done((f32[8,8,128]{2,1,0:T(8,128)S(1)}, f32[8,8,128]{2,1,0:T(8,128)S(1)}, u32[]{:S(2)}, u32[]{:S(2)}) %collective-permute-start.17) | collective-permute-done | bytes 32800 | tf_op jit(solution)/shard_map/ppermute | solution.py:961
  312.1 8.8 %rest_0.1 = (f32[1,64,512]{2,1,0:T(8,128)}, f32[1,64,512]{2,1,0:T(8,128)}, f32[1,64,512]{2,1,0:T(8,128)}, f32[1,64,512]{2,1,0:T(8,128)}, f32[2,128,512]{2,1,0:T(...) custom-call(f32[2,64,512]{2,1,0:T(8,128)} %get-tuple-element.153.ref, ...), custom_call_target="tpu_custom_call" | custom-call | tf_op jit(solution)/shard_map/rest_0/pallas_call | solution.py:160
  320.9 2.7 collective-permute-start.22
  327.2 40.3 %collective-permute-done.26.refs_27_.refs_29_ = f32[4,8,128]{2,1,0:T(8,128)S(1)} collective-permute-done((f32[4,8,128]{2,1,0:T(8,128)}, f32[4,8,128]{2,1,0:T(8,128)S(1)}, u32[]{:S(2)}, u32[]{:S(2)}) %collective-permute-start.26) | collective-permute-done | bytes 16416 | tf_op jit(solution)/shard_map/ppermute | solution.py:961
  368.7 6.8 %collective-permute-done.19.refs_3_ = f32[1,64,512]{2,1,0:T(8,128)S(1)} collective-permute-done((f32[1,64,512]{2,1,0:T(8,128)}, f32[1,64,512]{2,1,0:T(8,128)S(1)}, u32[]{:S(2)}, u32[]{:S(2)}) %collective-permute-start.19) | collective-permute-done | bytes 131104 | tf_op jit(solution)/shard_map/ppermute | solution.py:961
  377.2 12.3 %collective-permute-done.23.refs_15_.refs_17_ = f32[4,64,512]{2,1,0:T(8,128)S(1)} collective-permute-done((f32[4,64,512]{2,1,0:T(8,128)}, f32[4,64,512]{2,1,0:T(8,128)S(1)}, u32[]{:S(2)}, u32[]{:S(2)}) %collective-permute-start.23) | collective-permute-done | bytes 524320 | tf_op jit(solution)/shard_map/ppermute | solution.py:961
  391.0 4.8 rest_1.1
  400.1 8.1 %collective-permute-done.32.refs_17_.refs_19_ = f32[2,8,128]{2,1,0:T(8,128)S(1)} collective-permute-done((f32[2,8,128]{2,1,0:T(8,128)}, f32[2,8,128]{2,1,0:T(8,128)S(1)}, u32[]{:S(2)}, u32[]{:S(2)}) %collective-permute-start.32) | collective-permute-done | bytes 8224 | tf_op jit(solution)/shard_map/ppermute | solution.py:961
  410.3 6.9 %collective-permute-done.27.refs_1_ = f32[1,128,512]{2,1,0:T(8,128)S(1)} collective-permute-done((f32[1,128,512]{2,1,0:T(8,128)}, f32[1,128,512]{2,1,0:T(8,128)S(1)}, u32[]{:S(2)}, u32[]{:S(2)}) %collective-permute-start.27) | collective-permute-done | bytes 262176 | tf_op jit(solution)/shard_map/ppermute | solution.py:961
  417.3 5.5 %collective-permute-done.30.refs_11_ = f32[1,128,512]{2,1,0:T(8,128)S(1)} collective-permute-done((f32[1,128,512]{2,1,0:T(8,128)}, f32[1,128,512]{2,1,0:T(8,128)S(1)}, u32[]{:S(2)}, u32[]{:S(2)}) %collective-permute-start.30) | collective-permute-done | bytes 262176 | tf_op jit(solution)/shard_map/ppermute | solution.py:961
  423.7 3.1 rest_2.1
  426.9 2.9 collective-permute-start.34
  429.9 2.9 collective-permute-start.36
  432.8 18.6 %collective-permute-done.36.refs_7_ = f32[1,8,128]{2,1,0:T(8,128)S(1)} collective-permute-done((f32[1,8,128]{2,1,0:T(8,128)}, f32[1,8,128]{2,1,0:T(8,128)S(1)}, u32[]{:S(2)}, u32[]{:S(2)}) %collective-permute-start.36) | collective-permute-done | bytes 4128 | tf_op jit(solution)/shard_map/ppermute | solution.py:961
  452.2 2.1 rest_3.1
  457.2 48.2 %tail.1 = (bf16[2048,1024]{1,0:T(8,128)(2,1)}, bf16[2048,1024]{1,0:T(8,128)(2,1)}) custom-call(bf16[2048,2048]{1,0:T(8,128)(2,1)} %get-tuple-element.120.refs_1_.act_ref, bf16[2048,2048]{1,0:T(8,128)(2,1)} %get-tuple-element.121.dh_ref, bf16[2048,512]{1,0:T(8,128)(2,1)} %get-tuple-element.132.refs_7_.refs_16_.refs_2_.mix_ref, ...), custom_call_target="tpu_custom_call" | custom-call | flops 25769803776 | bytes 54525952 | tf_op jit(solution)/shard_map/tail/pallas_call | solution.py:865
  512.9 2.1 copy.94
  (230 shorter events, 59.8 us)
Async XLA Ops:
  28.0 18.6 %collective-permute-start = (f32[8,64,512]{2,1,0:T(8,128)}, f32[8,64,512]{2,1,0:T(8,128)S(1)}, u32[]{:S(2)}, u32[]{:S(2)}) collective-permute-start(f32[8,64,512]{2,1,0:T(8,128)} %get-tuple-element.119), channel_id=1, source_target_pairs={{0,2},{1,5},{2,0},{3,7},{4,6},{5,1},{6,4},{7,3},{8,10},{9,13},{10,... | collective-permute-start | bytes 3145736 | tf_op jit(solution)/shard_map/ppermute | solution.py:961
  75.7 63.8 %collective-permute-start.3 = (f32[8,64,1024]{2,1,0:T(8,128)}, f32[8,64,1024]{2,1,0:T(8,128)S(1)}, u32[]{:S(2)}, u32[]{:S(2)}) collective-permute-start(f32[8,64,1024]{2,1,0:T(8,128)} %get-tuple-element.129), channel_id=1, source_target_pairs={{0,2},{1,5},{2,0},{3,7},{4,6},{5,1},{6,4},{7,3},{8,10},{9,13},{10,... | collective-permute-start | bytes 6291464 | tf_op jit(solution)/shard_map/ppermute | solution.py:961
  75.8 37.5 %collective-permute-start.1 = (f32[8,64,512]{2,1,0:T(8,128)S(1)}, f32[8,64,512]{2,1,0:T(8,128)S(1)}, u32[]{:S(2)}, u32[]{:S(2)}) collective-permute-start(f32[8,64,512]{2,1,0:T(8,128)S(1)} %copy-done.41), channel_id=1, source_target_pairs={{0,2},{1,5},{2,0},{3,7},{4,6},{5,1},{6,4},{7,3},{8,10},{9,13},{10,... | collective-permute-start | bytes 3145736 | tf_op jit(solution)/shard_map/ppermute | solution.py:961
  77.8 49.7 %collective-permute-start.2 = (f32[4,64,512]{2,1,0:T(8,128)}, f32[4,64,512]{2,1,0:T(8,128)S(1)}, u32[]{:S(2)}, u32[]{:S(2)}) collective-permute-start(f32[4,64,512]{2,1,0:T(8,128)} %get-tuple-element.127), channel_id=1, source_target_pairs={{0,8},{1,9},{2,10},{3,11},{4,12},{5,13},{6,14},{7,15},{8,0},{9,1},... | collective-permute-start | bytes 1572872 | tf_op jit(solution)/shard_map/ppermute | solution.py:961
  172.4 57.9 %collective-permute-start.5 = (f32[2048,512]{1,0:T(8,128)}, f32[2048,512]{1,0:T(8,128)}, u32[]{:S(2)}, u32[]{:S(2)}) collective-permute-start(f32[2048,512]{1,0:T(8,128)} %get-tuple-element.138), channel_id=1, source_target_pairs={{0,1},{1,0},{2,3},{3,2},{4,5},{5,4},{6,7},{7,6},{8,9},{9,8},{10,11... | collective-permute-start | bytes 12582920 | tf_op jit(solution)/shard_map/ppermute | solution.py:968
  172.5 26.1 %collective-permute-start.6 = (f32[8,128,512]{2,1,0:T(8,128)S(1)}, f32[8,128,512]{2,1,0:T(8,128)S(1)}, u32[]{:S(2)}, u32[]{:S(2)}) collective-permute-start(f32[8,128,512]{2,1,0:T(8,128)S(1)} %copy-done.38), channel_id=1, source_target_pairs={{0,2},{1,5},{2,0},{3,7},{4,6},{5,1},{6,4},{7,3},{8,10},{9,13},{10,... | collective-permute-start | bytes 6291464 | tf_op jit(solution)/shard_map/ppermute | solution.py:961
  173.1 67.8 %collective-permute-start.8 = (f32[8,128,512]{2,1,0:T(8,128)S(1)}, f32[8,128,512]{2,1,0:T(8,128)}, u32[]{:S(2)}, u32[]{:S(2)}) collective-permute-start(f32[8,128,512]{2,1,0:T(8,128)S(1)} %copy-done.37), channel_id=1, source_target_pairs={{0,2},{1,5},{2,0},{3,7},{4,6},{5,1},{6,4},{7,3},{8,10},{9,13},{10,... | collective-permute-start | bytes 6291464 | tf_op jit(solution)/shard_map/ppermute | solution.py:961
  174.6 55.7 %collective-permute-start.7 = (f32[4,64,1024]{2,1,0:T(8,128)}, f32[4,64,1024]{2,1,0:T(8,128)S(1)}, u32[]{:S(2)}, u32[]{:S(2)}) collective-permute-start(f32[4,64,1024]{2,1,0:T(8,128)} %get-tuple-element.142), channel_id=1, source_target_pairs={{0,8},{1,9},{2,10},{3,11},{4,12},{5,13},{6,14},{7,15},{8,0},{9,1},... | collective-permute-start | bytes 3145736 | tf_op jit(solution)/shard_map/ppermute | solution.py:961
  228.0 60.4 %collective-permute-start.11 = (f32[4,128,512]{2,1,0:T(8,128)}, f32[4,128,512]{2,1,0:T(8,128)}, u32[]{:S(2)}, u32[]{:S(2)}) collective-permute-start(f32[4,128,512]{2,1,0:T(8,128)} %get-tuple-element.158), channel_id=1, source_target_pairs={{0,8},{1,9},{2,10},{3,11},{4,12},{5,13},{6,14},{7,15},{8,0},{9,1},... | collective-permute-start | bytes 3145736 | tf_op jit(solution)/shard_map/ppermute | solution.py:961
  228.8 62.0 %collective-permute-start.12 = (f32[8,64,768]{2,1,0:T(8,128)}, f32[8,64,768]{2,1,0:T(8,128)S(1)}, u32[]{:S(2)}, u32[]{:S(2)}) collective-permute-start(f32[8,64,768]{2,1,0:T(8,128)} %get-tuple-element.159), channel_id=1, source_target_pairs={{0,2},{1,5},{2,0},{3,7},{4,6},{5,1},{6,4},{7,3},{8,10},{9,13},{10,... | collective-permute-start | bytes 4718600 | tf_op jit(solution)/shard_map/ppermute | solution.py:961
  269.3 41.7 %collective-permute-start.16 = (f32[8,64,768]{2,1,0:T(8,128)}, f32[8,64,768]{2,1,0:T(8,128)S(1)}, u32[]{:S(2)}, u32[]{:S(2)}) collective-permute-start(f32[8,64,768]{2,1,0:T(8,128)} %get-tuple-element.166), channel_id=1, source_target_pairs={{0,2},{1,5},{2,0},{3,7},{4,6},{5,1},{6,4},{7,3},{8,10},{9,13},{10,... | collective-permute-start | bytes 4718600 | tf_op jit(solution)/shard_map/ppermute | solution.py:961
  279.2 31.8 %collective-permute-start.14 = (f32[8,64,512]{2,1,0:T(8,128)}, f32[8,64,512]{2,1,0:T(8,128)}, u32[]{:S(2)}, u32[]{:S(2)}) collective-permute-start(f32[8,64,512]{2,1,0:T(8,128)} %get-tuple-element.162), channel_id=1, source_target_pairs={{0,2},{1,5},{2,0},{3,7},{4,6},{5,1},{6,4},{7,3},{8,10},{9,13},{10,... | collective-permute-start | bytes 3145736 | tf_op jit(solution)/shard_map/ppermute | solution.py:961
  284.9 26.1 %collective-permute-start.15 = (f32[4,128,512]{2,1,0:T(8,128)}, f32[4,128,512]{2,1,0:T(8,128)}, u32[]{:S(2)}, u32[]{:S(2)}) collective-permute-start(f32[4,128,512]{2,1,0:T(8,128)} %get-tuple-element.164), channel_id=1, source_target_pairs={{0,8},{1,9},{2,10},{3,11},{4,12},{5,13},{6,14},{7,15},{8,0},{9,1},... | collective-permute-start | bytes 3145736 | tf_op jit(solution)/shard_map/ppermute | solution.py:961
  288.4 22.6 %collective-permute-start.13 = (f32[2,64,1024]{2,1,0:T(8,128)}, f32[2,64,1024]{2,1,0:T(8,128)}, u32[]{:S(2)}, u32[]{:S(2)}) collective-permute-start(f32[2,64,1024]{2,1,0:T(8,128)} %get-tuple-element.161), channel_id=1, source_target_pairs={{0,4},{1,3},{2,6},{3,1},{4,0},{5,7},{6,2},{7,5},{8,12},{9,11},{10,... | collective-permute-start | bytes 1572872 | tf_op jit(solution)/shard_map/ppermute | solution.py:961
  290.8 20.1 %collective-permute-start.17 = (f32[8,8,128]{2,1,0:T(8,128)S(1)}, f32[8,8,128]{2,1,0:T(8,128)S(1)}, u32[]{:S(2)}, u32[]{:S(2)}) collective-permute-start(f32[8,8,128]{2,1,0:T(8,128)S(1)} %get-tuple-element.232), channel_id=1, source_target_pairs={{0,2},{1,5},{2,0},{3,7},{4,6},{5,1},{6,4},{7,3},{8,10},{9,13},{10,... | collective-permute-start | bytes 98312 | tf_op jit(solution)/shard_map/ppermute | solution.py:961
  320.9 54.6 %collective-permute-start.22 = (f32[1,64,1024]{2,1,0:T(8,128)}, f32[1,64,1024]{2,1,0:T(8,128)S(1)}, u32[]{:S(2)}, u32[]{:S(2)}) collective-permute-start(f32[1,64,1024]{2,1,0:T(8,128)} %get-tuple-element.178), channel_id=1, source_target_pairs={{0,16},{1,17},{2,18},{3,19},{4,20},{5,21},{6,22},{7,23},{8,24},{9,... | collective-permute-start | bytes 786440 | tf_op jit(solution)/shard_map/ppermute | solution.py:961
  323.7 65.9 %collective-permute-start.21 = (f32[4,64,768]{2,1,0:T(8,128)}, f32[4,64,768]{2,1,0:T(8,128)S(1)}, u32[]{:S(2)}, u32[]{:S(2)}) collective-permute-start(f32[4,64,768]{2,1,0:T(8,128)} %get-tuple-element.176), channel_id=1, source_target_pairs={{0,8},{1,9},{2,10},{3,11},{4,12},{5,13},{6,14},{7,15},{8,0},{9,1},... | collective-permute-start | bytes 2359304 | tf_op jit(solution)/shard_map/ppermute | solution.py:961
  324.8 64.7 %collective-permute-start.25 = (f32[4,64,768]{2,1,0:T(8,128)}, f32[4,64,768]{2,1,0:T(8,128)S(1)}, u32[]{:S(2)}, u32[]{:S(2)}) collective-permute-start(f32[4,64,768]{2,1,0:T(8,128)} %get-tuple-element.184), channel_id=1, source_target_pairs={{0,8},{1,9},{2,10},{3,11},{4,12},{5,13},{6,14},{7,15},{8,0},{9,1},... | collective-permute-start | bytes 2359304 | tf_op jit(solution)/shard_map/ppermute | solution.py:961
  325.7 41.8 %collective-permute-start.26 = (f32[4,8,128]{2,1,0:T(8,128)}, f32[4,8,128]{2,1,0:T(8,128)S(1)}, u32[]{:S(2)}, u32[]{:S(2)}) collective-permute-start(f32[4,8,128]{2,1,0:T(8,128)} %get-tuple-element.186), channel_id=1, source_target_pairs={{0,8},{1,9},{2,10},{3,11},{4,12},{5,13},{6,14},{7,15},{8,0},{9,1},... | collective-permute-start | bytes 49160 | tf_op jit(solution)/shard_map/ppermute | solution.py:961
  326.9 41.0 %collective-permute-start.18 = (f32[1,64,512]{2,1,0:T(8,128)}, f32[1,64,512]{2,1,0:T(8,128)S(1)}, u32[]{:S(2)}, u32[]{:S(2)}) collective-permute-start(f32[1,64,512]{2,1,0:T(8,128)} %get-tuple-element.170), channel_id=1, source_target_pairs={{0,16},{1,17},{2,18},{3,19},{4,20},{5,21},{6,22},{7,23},{8,24},{9,... | collective-permute-start | bytes 393224 | tf_op jit(solution)/shard_map/ppermute | solution.py:961
  375.5 14.0 %collective-permute-start.23 = (f32[4,64,512]{2,1,0:T(8,128)}, f32[4,64,512]{2,1,0:T(8,128)S(1)}, u32[]{:S(2)}, u32[]{:S(2)}) collective-permute-start(f32[4,64,512]{2,1,0:T(8,128)} %get-tuple-element.180), channel_id=1, source_target_pairs={{0,8},{1,9},{2,10},{3,11},{4,12},{5,13},{6,14},{7,15},{8,0},{9,1},... | collective-permute-start | bytes 1572872 | tf_op jit(solution)/shard_map/ppermute | solution.py:961
  375.6 14.0 %collective-permute-start.24 = (f32[2,128,512]{2,1,0:T(8,128)}, f32[2,128,512]{2,1,0:T(8,128)S(1)}, u32[]{:S(2)}, u32[]{:S(2)}) collective-permute-start(f32[2,128,512]{2,1,0:T(8,128)} %get-tuple-element.182), channel_id=1, source_target_pairs={{0,4},{1,3},{2,6},{3,1},{4,0},{5,7},{6,2},{7,5},{8,12},{9,11},{10,... | collective-permute-start | bytes 1572872 | tf_op jit(solution)/shard_map/ppermute | solution.py:961
  395.9 26.9 %collective-permute-start.28 = (f32[2,64,768]{2,1,0:T(8,128)}, f32[2,64,768]{2,1,0:T(8,128)S(1)}, u32[]{:S(2)}, u32[]{:S(2)}) collective-permute-start(f32[2,64,768]{2,1,0:T(8,128)} %get-tuple-element.193), channel_id=1, source_target_pairs={{0,4},{1,3},{2,6},{3,1},{4,0},{5,7},{6,2},{7,5},{8,12},{9,11},{10,... | collective-permute-start | bytes 1179656 | tf_op jit(solution)/shard_map/ppermute | solution.py:961
  395.9 26.8 %collective-permute-start.31 = (f32[2,64,768]{2,1,0:T(8,128)}, f32[2,64,768]{2,1,0:T(8,128)S(1)}, u32[]{:S(2)}, u32[]{:S(2)}) collective-permute-start(f32[2,64,768]{2,1,0:T(8,128)} %get-tuple-element.199), channel_id=1, source_target_pairs={{0,4},{1,3},{2,6},{3,1},{4,0},{5,7},{6,2},{7,5},{8,12},{9,11},{10,... | collective-permute-start | bytes 1179656 | tf_op jit(solution)/shard_map/ppermute | solution.py:961
  398.0 19.2 %collective-permute-start.27 = (f32[1,128,512]{2,1,0:T(8,128)}, f32[1,128,512]{2,1,0:T(8,128)S(1)}, u32[]{:S(2)}, u32[]{:S(2)}) collective-permute-start(f32[1,128,512]{2,1,0:T(8,128)} %get-tuple-element.191), channel_id=1, source_target_pairs={{0,16},{1,17},{2,18},{3,19},{4,20},{5,21},{6,22},{7,23},{8,24},{9,... | collective-permute-start | bytes 786440 | tf_op jit(solution)/shard_map/ppermute | solution.py:961
  398.2 19.1 %collective-permute-start.29 = (f32[2,64,512]{2,1,0:T(8,128)}, f32[2,64,512]{2,1,0:T(8,128)S(1)}, u32[]{:S(2)}, u32[]{:S(2)}) collective-permute-start(f32[2,64,512]{2,1,0:T(8,128)} %get-tuple-element.195), channel_id=1, source_target_pairs={{0,4},{1,3},{2,6},{3,1},{4,0},{5,7},{6,2},{7,5},{8,12},{9,11},{10,... | collective-permute-start | bytes 786440 | tf_op jit(solution)/shard_map/ppermute | solution.py:961
  408.2 14.5 %collective-permute-start.30 = (f32[1,128,512]{2,1,0:T(8,128)}, f32[1,128,512]{2,1,0:T(8,128)S(1)}, u32[]{:S(2)}, u32[]{:S(2)}) collective-permute-start(f32[1,128,512]{2,1,0:T(8,128)} %get-tuple-element.197), channel_id=1, source_target_pairs={{0,16},{1,17},{2,18},{3,19},{4,20},{5,21},{6,22},{7,23},{8,24},{9,... | collective-permute-start | bytes 786440 | tf_op jit(solution)/shard_map/ppermute | solution.py:961
  426.8 24.6 %collective-permute-start.33 = (f32[1,64,768]{2,1,0:T(8,128)}, f32[1,64,768]{2,1,0:T(8,128)S(1)}, u32[]{:S(2)}, u32[]{:S(2)}) collective-permute-start(f32[1,64,768]{2,1,0:T(8,128)} %get-tuple-element.203), channel_id=1, source_target_pairs={{0,16},{1,17},{2,18},{3,19},{4,20},{5,21},{6,22},{7,23},{8,24},{9,... | collective-permute-start | bytes 589832 | tf_op jit(solution)/shard_map/ppermute | solution.py:961
  426.9 24.5 %collective-permute-start.34 = (f32[1,64,512]{2,1,0:T(8,128)}, f32[1,64,512]{2,1,0:T(8,128)S(1)}, u32[]{:S(2)}, u32[]{:S(2)}) collective-permute-start(f32[1,64,512]{2,1,0:T(8,128)} %get-tuple-element.205), channel_id=1, source_target_pairs={{0,16},{1,17},{2,18},{3,19},{4,20},{5,21},{6,22},{7,23},{8,24},{9,... | collective-permute-start | bytes 393224 | tf_op jit(solution)/shard_map/ppermute | solution.py:961
  429.8 21.6 %collective-permute-start.35 = (f32[1,64,768]{2,1,0:T(8,128)}, f32[1,64,768]{2,1,0:T(8,128)S(1)}, u32[]{:S(2)}, u32[]{:S(2)}) collective-permute-start(f32[1,64,768]{2,1,0:T(8,128)} %get-tuple-element.207), channel_id=1, source_target_pairs={{0,16},{1,17},{2,18},{3,19},{4,20},{5,21},{6,22},{7,23},{8,24},{9,... | collective-permute-start | bytes 589832 | tf_op jit(solution)/shard_map/ppermute | solution.py:961
  429.9 21.5 %collective-permute-start.36 = (f32[1,8,128]{2,1,0:T(8,128)}, f32[1,8,128]{2,1,0:T(8,128)S(1)}, u32[]{:S(2)}, u32[]{:S(2)}) collective-permute-start(f32[1,8,128]{2,1,0:T(8,128)} %get-tuple-element.209), channel_id=1, source_target_pairs={{0,16},{1,17},{2,18},{3,19},{4,20},{5,21},{6,22},{7,23},{8,24},{9,... | collective-permute-start | bytes 12296 | tf_op jit(solution)/shard_map/ppermute | solution.py:961
  457.1 50.3 %collective-permute-start.37 = (f32[32,4096]{1,0:T(8,128)S(1)}, f32[32,4096]{1,0:T(8,128)S(1)}, u32[]{:S(2)}, u32[]{:S(2)}) collective-permute-start(f32[32,4096]{1,0:T(8,128)S(1)} %get-tuple-element.226), channel_id=1, source_target_pairs={{0,1},{1,0},{2,3},{3,2},{4,5},{5,4},{6,7},{7,6},{8,9},{9,8},{10,11... | collective-permute-start | bytes 1572872 | tf_op jit(solution)/shard_map/ppermute | solution.py:968
  (53 other events, 675.8 us)

commit v2 on v0

v2 whole, which is shorter than its diff:
```python
import math
from functools import partial

import jax
import jax.numpy as jnp
import numpy as np
from jax import lax
from jax.experimental import pallas as pl
from jax.experimental.pallas import tpu as pltpu
from jax.sharding import PartitionSpec as P

D = 1024
HEADS = 16
HEAD = 64
FF = 4096
ROT = 16
SLOT = 2048
EPSILON = 1e-05

f32 = jnp.float32
bf16 = jnp.bfloat16
VMEM_LIMIT = 60 * 1024 * 1024
BLK = 256
PAIR = 2 * HEAD


def dot(a, b):
    return lax.dot_general(a, b, (((1,), (0,)), ((), ())), preferred_element_type=f32)


def dot_nt(a, b):
    return lax.dot_general(a, b, (((1,), (1,)), ((), ())), preferred_element_type=f32)


def dot_tn(a, b):
    return lax.dot_general(a, b, (((0,), (0,)), ((), ())), preferred_element_type=f32)


def erf_inverse(y):
    x = 0.0
    for _ in range(200):
        step = (math.erf(x) - y) / (2.0 / math.sqrt(math.pi) * math.exp(-x * x))
        x -= max(-0.5, min(0.5, step))
    return x


def feature_table():
    i = np.arange(HEAD, dtype=np.float64)
    cos_table = np.cos(np.pi * (2.0 * i[:, None] + 1.0) * i[None, :] / (2.0 * HEAD))
    weights = np.where(i == 0, math.sqrt(1.0 / HEAD), math.sqrt(2.0 / HEAD))
    quantiles = math.sqrt(2.0) * np.array([erf_inverse(2.0 * (m + 0.5) / HEAD - 1.0) for m in range(HEAD)])
    return cos_table * (weights * 0.5 * quantiles)[None, :]


def split_table(table):
    high = table.astype(np.float32).astype(bf16)
    low = (table - high.astype(np.float64)).astype(np.float32).astype(bf16)
    return high, low


def attention_tables():
    half = ROT // 2
    pos = np.arange(SLOT, dtype=np.float32)
    inverse = (np.float32(10000.0) ** (-2.0 * np.arange(half, dtype=np.float32) / np.float32(ROT))).astype(np.float32)
    angles = (pos[:, None] * inverse[None, :]).astype(np.float32).astype(np.float64)
    cos_one = np.ones((SLOT, HEAD))
    sin_one = np.zeros((SLOT, HEAD))
    cos_one[:, :half] = np.cos(angles)
    cos_one[:, half:ROT] = np.cos(angles)
    sin_one[:, :half] = np.sin(angles)
    sin_one[:, half:ROT] = -np.sin(angles)
    cosine = np.concatenate([cos_one, cos_one], 1).astype(np.float32)
    sine = np.concatenate([sin_one, sin_one], 1).astype(np.float32)
    one = feature_table()
    pair = np.zeros((PAIR, PAIR))
    pair[:HEAD, :HEAD] = one
    pair[HEAD:, HEAD:] = one
    swapped = pair.copy()
    for base in (0, HEAD):
        swapped[base : base + half] = pair[base + half : base + ROT]
        swapped[base + half : base + ROT] = pair[base : base + half]
    both = np.concatenate([pair, swapped], 0)
    high, low = split_table(both)
    forward = np.concatenate([high, low], 1)
    back_high, back_low = split_table(np.concatenate([pair.T, swapped.T], 1))
    back_high2 = np.concatenate([back_high, back_high], 0)
    return cosine, sine, forward, back_high2, back_low


def params(**extra):
    return pltpu.CompilerParams(vmem_limit_bytes=VMEM_LIMIT, **extra)


ANY = pl.BlockSpec(memory_space=pl.ANY)
MESH = pl.DeviceIdType.MESH


def idiv(a, b):
    return lax.div(a, jnp.int32(b))


def irem(a, b):
    return lax.rem(a, jnp.int32(b))


FIRST_BITS = {
    "xy": ("xzy", "yzx"), "zz": ("zxy", "zyx"), "xx": ("xyz", "yxz"), "xz": ("xzy", "zyx"),
    "yz": ("yzx", "zxy"), "xp": ("xyz", "yzx"), "zx": ("zyx", "xyz"), "zy": ("zxy", "yxz"),
}


class Comm:
    def __init__(self, parts, streams):
        self.parts, self.streams = parts, streams
        self.steps = parts.bit_length() - 1
        self.kernels = 0

    def orders(self, kind):
        result = []
        for s in range(2):
            order = [1 << b for b in range(self.steps)]
            if self.steps >= 3:
                order[:3] = [1 << "xyz".index(axis) for axis in FIRST_BITS[kind][s]]
            result.append(order)
        return result

    def place(self, kinds, share, which=None):
        chip, core = lax.axis_index("dp"), lax.axis_index("stream")
        kinds = [kinds] if isinstance(kinds, str) else list(kinds)
        total = jnp.int32(0)
        for b in range(self.steps):
            mask = 1 << b
            weight = jnp.int32(0)
            for n, kind in enumerate(kinds):
                values = [1 << (self.steps - 1 - order.index(mask)) for order in self.orders(kind)]
                value = values[0] + core * (values[1] - values[0])
                weight = value if n == 0 else jnp.where(which == n, value, weight)
            own = irem(idiv(chip, mask), 2)
            theirs = (share >> b) & 1 if isinstance(share, int) else irem(idiv(share, mask), 2)
            total = total + weight * irem(own + theirs, 2)
        return total

    def partner(self, kind, step):
        chip, core = lax.axis_index("dp"), lax.axis_index("stream")
        chips = []
        for order in self.orders(kind):
            mask = order[step]
            chips.append(chip + mask - 2 * mask * irem(idiv(chip, mask), 2))
        return (chips[0] + core * (chips[1] - chips[0]), core)

    def other_core(self):
        return (lax.axis_index("dp"), 1 - lax.axis_index("stream"))


class Flow:
    def __init__(self, name, kind, first, shape, array=None, start=None, sums=(), ready=0):
        self.name, self.kind, self.first, self.shape, self.array = name, kind, first, tuple(shape), array
        self.start, self.sums, self.ready = start, tuple(sums), ready
        self.half = shape[0] // 2
        self.slots = sum(self.half >> k for k in range(len(self.sums)))

    def out_shape(self):
        return (self.shape[0] >> len(self.sums),) + self.shape[1:]

    def scratch(self):
        half, (_, rows, columns) = self.half, self.shape
        kept = [pltpu.VMEM((half, rows, columns), f32)] if self.array is not None else []
        count = max(len(self.sums), 1)
        return kept + [
            pltpu.VMEM((max(self.slots, 1), rows, columns), f32),
            pltpu.SemaphoreType.DMA((count,)),
            pltpu.SemaphoreType.DMA((count,)),
            pltpu.SemaphoreType.DMA((2,)),
        ]

    def bind(self, comm, own, source, out, scratch):
        self.comm, self.source, self.out = comm, source, out
        scratch = list(scratch)
        self.own = scratch.pop(0) if self.array is not None else own
        self.recv, self.send_sem, self.recv_sem, self.local_sem = scratch

    def offset(self, k):
        return sum(self.half >> j for j in range(k))

    def remote(self, k):
        count = self.half >> k
        if k == 0 and self.array is not None:
            source = self.source.at[pl.ds(count, count)]
        else:
            source = self.own.at[pl.ds(count, count)]
        return pltpu.make_async_remote_copy(
            src_ref=source,
            dst_ref=self.recv.at[pl.ds(self.offset(k), count)],
            send_sem=self.send_sem.at[k],
            recv_sem=self.recv_sem.at[k],
            device_id=self.comm.partner(self.kind, self.first + k),
            device_id_type=MESH,
        )

    def load(self):
        return pltpu.make_async_copy(self.source.at[pl.ds(0, self.half)], self.own, self.local_sem.at[0])

    def store(self):
        return pltpu.make_async_copy(
            self.own.at[pl.ds(0, self.shape[0] >> len(self.sums))], self.out, self.local_sem.at[1]
        )

    def moves(self):
        return self.start is not None

    def events(self, step, last):
        if not self.moves():
            when = self.ready

            @pl.when((step == when) if not last else (step < 0))
            def _():
                self.store().start()

            return

        if not last:

            @pl.when(step == self.start)
            def _():
                self.remote(0).start()
                if self.array is not None:
                    self.load().start()

        for k, at in enumerate(self.sums):
            if (at < 0) != last:
                continue

            @pl.when(step >= 0 if last else step == at)
            def _(k=k):
                self.remote(k).wait_recv()
                if k == 0 and self.array is not None:
                    self.load().wait()
                count = self.half >> k
                base = self.offset(k)

                def add(p, carry):
                    self.own[p] = self.own[p] + self.recv[base + p]
                    return carry

                lax.fori_loop(0, count, add, 0)
                if k + 1 < len(self.sums):
                    self.remote(k + 1).start()
                else:
                    self.store().start()

    def finish(self):
        if self.moves():
            for k in range(len(self.sums)):
                self.remote(k).wait_send()
        self.store().wait()


def with_comm(
    comm, kernel, steps, in_specs, out_specs, out_shape, flows, operands, scratch_shapes=(), inner=(), exchange=False,
    name=None, **call,
):
    base_in, base_out, base_scratch = len(in_specs), len(out_specs), len(scratch_shapes)
    every = list(flows) + [flow for flow, _, _ in inner]
    flow_scratch = [flow.scratch() if flow.moves() or flow.array is not None else [pltpu.SemaphoreType.DMA((2,))] for flow in every]
    remote = any(flow.moves() for flow in every)

    def run(*refs):
        refs = list(refs)

        def take(count):
            taken = refs[:count]
            del refs[:count]
            return taken

        own_in, flow_in = take(base_in), take(len(flows))
        own_out, flow_out = take(base_out), take(len(every))
        own_scratch = take(base_scratch)
        for n, flow in enumerate(every):
            got = take(len(flow_scratch[n]))
            if n < len(flows):
                flow.bind(comm, None, flow_in[n], flow_out[n], got)
            else:
                _, index, at = inner[n - len(flows)]
                if not flow.moves():
                    got = [None, None, None] + got
                own = own_scratch[index] if at is None else own_scratch[index].at[at]
                flow.bind(comm, own, None, flow_out[n], got)
        step = pl.program_id(0)
        if remote or exchange:

            @pl.when(step == 0)
            def _():
                barrier = pltpu.get_barrier_semaphore()
                chip, core = lax.axis_index("dp"), lax.axis_index("stream")
                others = []
                if remote:
                    for b in range(comm.steps):
                        mask = 1 << b
                        others.append((chip + mask - 2 * mask * irem(idiv(chip, mask), 2), core))
                if exchange:
                    others.append(comm.other_core())
                for other in others:
                    pl.semaphore_signal(barrier, inc=1, device_id=other, device_id_type=MESH)
                pl.semaphore_wait(barrier, len(others))

        for flow in every:
            flow.events(step, False)
        kernel(*own_in, *own_out, *own_scratch)

        @pl.when(step == steps - 1)
        def _():
            for flow in every:
                if flow.moves():
                    flow.events(step, True)
                elif flow.ready >= steps:
                    flow.store().start()
            for flow in every:
                flow.finish()

    extra = {}
    if remote or exchange:
        extra = dict(collective_id=comm.kernels, has_side_effects=True)
        comm.kernels += 1
    results = pl.pallas_call(
        run,
        grid=(steps,),
        in_specs=list(in_specs) + [ANY] * len(flows),
        out_specs=list(out_specs) + [ANY] * len(every),
        out_shape=list(out_shape) + [jax.ShapeDtypeStruct(flow.out_shape(), f32) for flow in every],
        scratch_shapes=list(scratch_shapes) + sum(flow_scratch, []),
        compiler_params=params(**extra),
        name=name,
        **call,
    )(*operands, *[flow.array for flow in flows])
    results = list(results)
    return results[:base_out], dict(zip([flow.name for flow in every], results[base_out:]))


def unit_strips(comm, w_in_ref, w_out_ref, first, units, gathered):
    if gathered:
        first = first if isinstance(first, int) else pl.multiple_of(first, 128)
        return [(w_in_ref.at[:, pl.ds(first, units)], w_out_ref.at[pl.ds(first, units), :], 0, units)]
    unit = FF // (comm.parts * comm.streams)
    core = lax.axis_index("stream")
    strips = []
    for n in range(units // unit):
        start = (idiv(jnp.int32(first), unit) + n) * comm.streams + core
        start = pl.multiple_of(start * unit, unit)
        strips.append((w_in_ref.at[:, pl.ds(start, unit)], w_out_ref.at[pl.ds(start, unit), :], n * unit, unit))
    return strips


def gather_units(comm, w_in, w_out):
    parts, streams = comm.parts, comm.streams
    unit = FF // (parts * streams)
    if unit % 128 == 0:
        return w_in, w_out, False
    core = lax.axis_index("stream")
    a = lax.dynamic_index_in_dim(w_in.reshape(D, parts, streams, unit), core, 2, False)
    b = lax.dynamic_index_in_dim(w_out.reshape(parts, streams, unit, D), core, 1, False)
    return a.reshape(D, parts * unit), b.reshape(parts * unit, D), True


def gelu_parts(x):
    density = jnp.exp(x * x * -0.5)
    t = 1.0 / (1.0 + (0.3275911 / math.sqrt(2.0)) * jnp.abs(x))
    poly = 1.061405429 * t - 1.453152027
    poly = poly * t + 1.421413741
    poly = poly * t - 0.284496736
    poly = (poly * t + 0.254829592) * t
    tail = 0.5 * poly * density
    cdf = jnp.where(x >= 0, 1.0 - tail, tail)
    return x * cdf, cdf + x * density * (1.0 / math.sqrt(2.0 * math.pi))


TILE = 256
UNITS = 512
CHUNK_STEPS = 6
OUT_COLUMNS = 256


def front_kernel(
    comm, kinds, out_kinds, gathered,
    tok_hbm, cot_hbm, valid_ref, gain_ref, win_hbm, wout_hbm,
    normed_hbm, g_hbm, act_hbm, dh_hbm,
    normed, g, win, wout, h_a, h_b, d_a, d_b, act, d_hidden, in_own, out_own,
    tok_sem, cot_sem, in_sem, out_sem, normed_sem, g_sem, act_sem, dh_sem,
):
    step = pl.program_id(0)
    rows = normed.shape[0]
    chunks = act.shape[0]
    tile = 2 * TILE
    tiles = rows // tile
    chunk = idiv(step, CHUNK_STEPS)
    phase = irem(step, CHUNK_STEPS)
    working = chunk < chunks
    slot = irem(chunk, 2)

    def tile_rows(i):
        return pl.ds(pl.multiple_of(i * tile, tile), tile)

    def row_load(i, hbm, vmem, sem):
        return pltpu.make_async_copy(hbm.at[tile_rows(i), :], vmem.at[tile_rows(i), :], sem.at[i])

    def row_store(i, vmem, hbm, sem):
        return pltpu.make_async_copy(vmem.at[tile_rows(i), :], hbm.at[tile_rows(i), :], sem.at[i])

    def weight_loads(c):
        s = irem(jnp.int32(c), 2)
        loads = []
        for n, (a, b, at, size) in enumerate(unit_strips(comm, win_hbm, wout_hbm, c * UNITS, UNITS, gathered)):
            loads.append(pltpu.make_async_copy(a, win.at[s, :, pl.ds(at, size)], in_sem.at[s, n]))
            loads.append(pltpu.make_async_copy(b, wout.at[s, pl.ds(at, size), :], out_sem.at[s, n]))
        return loads

    def low_stores(c):
        columns = pl.ds(pl.multiple_of(c * UNITS, UNITS), UNITS)
        here = pl.ds(TILE, rows)
        return (
            pltpu.make_async_copy(act.at[c, here, :], act_hbm.at[:, columns], act_sem.at[c]),
            pltpu.make_async_copy(d_hidden.at[irem(c, 2), here, :], dh_hbm.at[:, columns], dh_sem.at[c]),
        )

    @pl.when(step == 0)
    def _():
        row_load(0, tok_hbm, normed, tok_sem).start()
        row_load(0, cot_hbm, g, cot_sem).start()
        for load in weight_loads(0):
            load.start()
        for i in range(1, tiles):
            row_load(i, tok_hbm, normed, tok_sem).start()
            row_load(i, cot_hbm, g, cot_sem).start()

    @pl.when(working & (chunk == 0) & (phase < tiles))
    def _():
        row_load(phase, tok_hbm, normed, tok_sem).wait()
        row_load(phase, cot_hbm, g, cot_sem).wait()
        here = tile_rows(phase)
        x = normed[here, :].astype(f32)
        centered = x - jnp.mean(x, axis=-1, keepdims=True)
        var = jnp.mean(centered * centered, axis=-1, keepdims=True)
        normed[here, :] = (centered * lax.rsqrt(var + EPSILON) * gain_ref[...]).astype(bf16)
        g[here, :] = (g[here, :].astype(f32) * valid_ref[here, :]).astype(bf16)
        row_store(phase, normed, normed_hbm, normed_sem).start()
        row_store(phase, g, g_hbm, g_sem).start()

    @pl.when(working & (phase == 0))
    def _():
        for load in weight_loads(chunk):
            load.wait()

    @pl.when((phase == 0) & (chunk + 1 < chunks))
    def _():
        for load in weight_loads(chunk + 1):
            load.start()

    def finish_tile(h, d, place):
        value, slope = gelu_parts(h[...])
        here = pl.ds(pl.multiple_of(place, TILE), TILE)
        act[chunk, here, :] = value.astype(bf16)
        d_hidden[slot, here, :] = (d[...] * slope).astype(bf16)

    @pl.when(working & (phase < tiles))
    def _():
        first = pl.multiple_of(phase * tile, tile)
        here_a, here_b = pl.ds(first, TILE), pl.ds(first + TILE, TILE)
        finish_tile(h_b, d_b, phase * tile)
        h_a[...] = dot(normed[here_a, :], win[slot])
        d_a[...] = dot_nt(g[here_a, :], wout[slot])
        finish_tile(h_a, d_a, phase * tile + TILE)
        h_b[...] = dot(normed[here_b, :], win[slot])
        d_b[...] = dot_nt(g[here_b, :], wout[slot])

    share_rows = D // comm.parts
    wide = D // 2
    for m in range(2):

        @pl.when(working & (phase == tiles + m))
        def _(m=m):
            if m == 0:
                finish_tile(h_b, d_b, rows)
                for copy in low_stores(chunk):
                    copy.start()
            made = dot_tn(normed[:, m * wide : (m + 1) * wide], d_hidden[slot, TILE : TILE + rows, :])
            for n in range(wide // share_rows):
                share = m * (wide // share_rows) + n
                in_own[chunk, comm.place(kinds, share, chunk)] = made[n * share_rows : (n + 1) * share_rows, :]
            if m == 1:
                low_stores(chunk)[1].wait()

    unit_rows = FF // comm.streams // comm.parts
    blocks = D // OUT_COLUMNS
    for block in range(blocks):

        @pl.when(step == chunks * CHUNK_STEPS + block)
        def _(block=block):
            right = g[:, block * OUT_COLUMNS : (block + 1) * OUT_COLUMNS]
            for c in range(chunks):
                made = dot_tn(act[c, TILE : TILE + rows, :], right)
                for n in range(UNITS // unit_rows):
                    share = c * (UNITS // unit_rows) + n
                    out_own[block, comm.place(out_kinds[block], share)] = made[n * unit_rows : (n + 1) * unit_rows, :]

    @pl.when(step == pl.num_programs(0) - 1)
    def _():
        for i in range(tiles):
            row_store(i, normed, normed_hbm, normed_sem).wait()
            row_store(i, g, g_hbm, g_sem).wait()
        for c in range(chunks):
            low_stores(jnp.int32(c))[0].wait()


def front(comm, tokens, cotangent, valid, gain, weights, plan):
    w_in, w_out, gathered = weights
    rows = tokens.shape[0]
    units = FF // comm.streams
    chunks, blocks = units // UNITS, D // OUT_COLUMNS
    tiles = rows // (2 * TILE)
    parts = comm.parts
    strips = 1 if gathered else UNITS // (units // parts)
    share_rows, unit_rows = D // parts, units // parts
    kinds = [KIND[f"in{c}"] for c in range(chunks)]
    out_kinds = [KIND[f"o{b}"] for b in range(blocks)]
    steps = chunks * CHUNK_STEPS + blocks
    inner = []
    for c in range(chunks):
        start, sums = plan.get(f"in{c}", (None, ()))
        shape = (parts, share_rows, UNITS)
        flow = Flow(f"in{c}", kinds[c], 0, shape, None, start, sums, (c + 1) * CHUNK_STEPS)
        inner.append((flow, 10, c))
    for b in range(blocks):
        start, sums = plan.get(f"o{b}", (None, ()))
        shape = (parts, unit_rows, OUT_COLUMNS)
        flow = Flow(f"o{b}", out_kinds[b], 0, shape, None, start, sums, chunks * CHUNK_STEPS + b + 1)
        inner.append((flow, 11, b))
    low = jax.ShapeDtypeStruct((rows, D), bf16)
    wide = jax.ShapeDtypeStruct((rows, units), bf16)
    return with_comm(
        comm,
        partial(front_kernel, comm, kinds, out_kinds, gathered),
        steps,
        [ANY, ANY, pl.BlockSpec((rows, 1), lambda i: (0, 0)), pl.BlockSpec((1, D), lambda i: (0, 0)), ANY, ANY],
        [ANY] * 4,
        [low, low, wide, wide],
        [],
        [tokens, cotangent, valid, gain, w_in, w_out],
        [
            pltpu.VMEM((rows, D), bf16),
            pltpu.VMEM((rows, D), bf16),
            pltpu.VMEM((2, D, UNITS), bf16),
            pltpu.VMEM((2, UNITS, D), bf16),
            pltpu.VMEM((TILE, UNITS), f32),
            pltpu.VMEM((TILE, UNITS), f32),
            pltpu.VMEM((TILE, UNITS), f32),
            pltpu.VMEM((TILE, UNITS), f32),
            pltpu.VMEM((chunks, rows + TILE, UNITS), bf16),
            pltpu.VMEM((2, rows + TILE, UNITS), bf16),
            pltpu.VMEM((chunks, parts, share_rows, UNITS), f32),
            pltpu.VMEM((blocks, parts, unit_rows, OUT_COLUMNS), f32),
            pltpu.SemaphoreType.DMA((tiles,)),
            pltpu.SemaphoreType.DMA((tiles,)),
            pltpu.SemaphoreType.DMA((2, strips)),
            pltpu.SemaphoreType.DMA((2, strips)),
            pltpu.SemaphoreType.DMA((tiles,)),
            pltpu.SemaphoreType.DMA((tiles,)),
            pltpu.SemaphoreType.DMA((chunks,)),
            pltpu.SemaphoreType.DMA((chunks,)),
        ],
        inner,
        name="front",
        cost_estimate=pl.CostEstimate(
            flops=8 * rows * D * units, bytes_accessed=12 * rows * D + 8 * units * D, transcendentals=rows * units
        ),
    )


def causal_mask(transposed):
    row = lax.broadcasted_iota(jnp.int32, (BLK, BLK), 0)
    col = lax.broadcasted_iota(jnp.int32, (BLK, BLK), 1)
    return col >= row if transposed else row >= col


def head_masks():
    lane = lax.broadcasted_iota(jnp.int32, (1, PAIR), 1)
    first = lane < HEAD
    m0 = jnp.where(first, 1.0, 0.0)
    return m0.astype(bf16), (1.0 - m0).astype(bf16)


def state_mask():
    row = lax.broadcasted_iota(jnp.int32, (PAIR, 2 * PAIR), 0)
    col = lax.broadcasted_iota(jnp.int32, (PAIR, 2 * PAIR), 1)
    return (row < HEAD) == (col < PAIR)


def forward_kernel(
    comm, groups, kind,
    normed_ref, wq_ref, wk_ref, wv_ref, cos_ref, sin_ref, fw_ref, map_ref, valid_ref, right_ref,
    q_ref, k_ref, v_ref, mix_ref, den_ref, state_ref,
    state, mixed_all, sent, arrived, proj_own, send_sem, recv_sem,
):
    step = pl.program_id(0)
    blocks = sent.shape[0]

    def to_partner(i):
        return pltpu.make_async_remote_copy(
            src_ref=sent.at[i],
            dst_ref=arrived.at[i],
            send_sem=send_sem.at[i],
            recv_sem=recv_sem.at[i],
            device_id=comm.other_core(),
            device_id_type=MESH,
        )

    @pl.when(step == 0)
    def _():
        state[...] = jnp.zeros_like(state)

    @pl.when(step < blocks)
    def _():
        rows = normed_ref[...]
        queries_all, keys_all, values_all = dot(rows, wq_ref[...]), dot(rows, wk_ref[...]), dot(rows, wv_ref[...])
        cosine, sine = cos_ref[...], sin_ref[...]
        valid = valid_ref[...]
        m0, m1 = head_masks()
        causal = causal_mask(False)
        keep_state = state_mask()
        first = lax.broadcasted_iota(jnp.int32, (BLK, PAIR), 1) < HEAD
        place = pl.ds(pl.multiple_of(step * BLK, BLK), BLK)
        for group in range(groups):
            here = slice(group * PAIR, (group + 1) * PAIR)
            queries, keys = queries_all[:, here], keys_all[:, here]
            turned = jnp.concatenate(
                [
                    jnp.concatenate([queries * cosine, queries * sine], 1),
                    jnp.concatenate([keys * cosine, keys * sine], 1),
                ],
                0,
            )
            high = turned.astype(bf16)
            low = (turned - high.astype(f32)).astype(bf16)
            main = dot(high, map_ref[...])
            exponent = main[:, :PAIR] + main[:, PAIR:] + dot(low, map_ref[:, :PAIR])
            phi = jnp.exp(exponent) * fw_ref[:, here]
            q = phi[:BLK].astype(bf16)
            k = (phi[BLK:] * valid).astype(bf16)
            v = values_all[:, here].astype(bf16)
            q_ref[:, here] = q
            k_ref[:, here] = k
            v_ref[:, here] = v
            v0, v1 = v * m0 + m1, v * m1 + m0
            s0 = jnp.where(causal, dot_nt(q * m0, k), 0.0).astype(bf16)
            s1 = jnp.where(causal, dot_nt(q * m1, k), 0.0).astype(bf16)
            before = jnp.where(keep_state, state[group], 0.0).astype(bf16)
            state_ref[group, 0] = before
            far = dot(q, before)
            o0 = dot(s0, v0) + far[:, :PAIR]
            o1 = dot(s1, v1) + far[:, PAIR:]
            numerator = jnp.where(first, o0, o1)
            denominator = pltpu.roll(jnp.where(first, o1, o0), HEAD, 1)
            mixed = (numerator / denominator).astype(bf16)
            mix_ref[:, here] = mixed
            mixed_all[place, here] = mixed
            sent[step, :, here] = mixed.astype(f32)
            den_ref[:, here] = denominator
            state[group] += dot_tn(k, jnp.concatenate([v0, v1], 1))
        to_partner(step).start()

    share_rows = D // comm.parts
    width = groups * PAIR
    core = lax.axis_index("stream")
    for side in range(2):

        @pl.when(step == blocks + side)
        def _(side=side):
            if side == 0:
                left = mixed_all[...]
                base = core * (width // share_rows)
            else:
                for i in range(blocks):
                    to_partner(i).wait_recv()
                left = arrived[...].reshape(blocks * BLK, width).astype(bf16)
                base = (1 - core) * (width // share_rows)
            made = dot_tn(left, right_ref[...])
            for n in range(width // share_rows):
                proj_own[comm.place(kind, base + n)] = made[n * share_rows : (n + 1) * share_rows, :]
            if side == 1:
                for i in range(blocks):
                    to_partner(i).wait_send()


def forward(comm, normed, g, w_qkv, cosine, sine, fw, table, valid, flows, plan):
    rows = normed.shape[0]
    streams, parts = comm.streams, comm.parts
    groups = HEADS // streams // 2
    width = groups * PAIR
    blocks = rows // BLK

    def at(i):
        return jnp.minimum(i, blocks - 1)

    row_spec = pl.BlockSpec((BLK, width), lambda i: (at(i), 0))
    table_spec = pl.BlockSpec((BLK, PAIR), lambda i: (at(i), 0))
    low = jax.ShapeDtypeStruct((rows, width), bf16)

    def weight_spec(which):
        return pl.BlockSpec((D, width), lambda i: (0, which * streams + lax.axis_index("stream")))

    start, sums = plan.get("pr", (None, ()))
    kind = KIND["pr"]
    columns = D // streams
    inner = [(Flow("pr", kind, 0, (parts, D // parts, columns), None, start, sums, blocks + 2), 4, None)]
    return with_comm(
        comm,
        partial(forward_kernel, comm, groups, kind),
        blocks + 2,
        [
            pl.BlockSpec((BLK, D), lambda i: (at(i), 0)),
            weight_spec(0),
            weight_spec(1),
            weight_spec(2),
            table_spec,
            table_spec,
            pl.BlockSpec((1, width), lambda i: (0, lax.axis_index("stream"))),
            pl.BlockSpec((2 * PAIR, 2 * PAIR), lambda i: (0, 0)),
            pl.BlockSpec((BLK, 1), lambda i: (at(i), 0)),
            pl.BlockSpec((rows, columns), lambda i: (0, lax.axis_index("stream"))),
        ],
        [row_spec, row_spec, row_spec, row_spec, row_spec,
         pl.BlockSpec((groups, 1, PAIR, 2 * PAIR), lambda i: (0, at(i), 0, 0))],
        [low, low, low, low, jax.ShapeDtypeStruct((rows, width), f32),
         jax.ShapeDtypeStruct((groups, blocks, PAIR, 2 * PAIR), bf16)],
        flows,
        [normed, w_qkv, w_qkv, w_qkv, cosine, sine, fw, table, valid, g],
        [
            pltpu.VMEM((groups, PAIR, 2 * PAIR), f32),
            pltpu.VMEM((rows, width), bf16),
            pltpu.VMEM((blocks, BLK, width), f32),
            pltpu.VMEM((blocks, BLK, width), f32),
            pltpu.VMEM((parts, D // parts, columns), f32),
            pltpu.SemaphoreType.DMA((blocks,)),
            pltpu.SemaphoreType.DMA((blocks,)),
        ],
        inner,
        exchange=True,
        name="attention_forward",
        cost_estimate=pl.CostEstimate(
            flops=groups * blocks * 2 * 65536 * 5000,
            bytes_accessed=rows * D * 2 + 3 * D * width * 2 + rows * width * 16,
            transcendentals=2 * rows * width,
        ),
    )


GROUPS = 2
BACK_STEPS = 2


def backward_kernel(
    comm, blocks, kinds, feature_kind,
    g_ref, wp_ref, q_ref, k_ref, v_ref, mix_ref, den_ref, state_ref, cos_ref, sin_ref, back_ref, back_low_ref,
    sums_ref, fw_ref, normed_hbm,
    dq_ref, dk_ref, dv_ref,
    later, d_all, normed, fg, qkv_own, feature_own, load_sem,
):
    step = pl.program_id(0)
    per = blocks + BACK_STEPS
    call, phase = idiv(step, per), irem(step, per)
    width = GROUPS * PAIR
    load = pltpu.make_async_copy(normed_hbm, normed, load_sem)

    @pl.when(step == 0)
    def _():
        load.start()
        feature_own[...] = jnp.zeros_like(feature_own)

    @pl.when(phase == 0)
    def _():
        later[...] = jnp.zeros_like(later)
        fg[...] = jnp.zeros_like(fg)

    @pl.when(phase < blocks)
    def _():
        m0, m1 = head_masks()
        first = lax.broadcasted_iota(jnp.int32, (BLK, PAIR), 1) < HEAD
        left = lax.broadcasted_iota(jnp.int32, (PAIR, PAIR), 1) < HEAD
        own = (lax.broadcasted_iota(jnp.int32, (PAIR, PAIR), 0) < HEAD) == left
        causal, flipped = causal_mask(False), causal_mask(True)
        keep_state = state_mask()
        cosine, sine = cos_ref[...], sin_ref[...]
        d_mixed_all = dot_nt(g_ref[...], wp_ref[...])
        place = pl.ds(pl.multiple_of((blocks - 1 - phase) * BLK, BLK), BLK)
        for group in range(GROUPS):
            here = slice(group * PAIR, (group + 1) * PAIR)
            numer = d_mixed_all[:, here] / den_ref[:, here]
            product = numer * mix_ref[:, here].astype(f32)
            p_high = product.astype(bf16)
            p_low = (product - p_high.astype(f32)).astype(bf16)
            sums = dot(jnp.concatenate([p_high, p_low], 1), sums_ref[...])
            d_o0 = jnp.where(first, numer, -sums).astype(bf16)
            d_o1 = jnp.where(first, -sums, numer).astype(bf16)
            low = numer.astype(bf16)
            dn0, dn1 = low * m0, low * m1
            q, k, v = q_ref[:, here], k_ref[:, here], v_ref[:, here]
            q0, q1 = q * m0, q * m1
            v0, v1 = v * m0 + m1, v * m1 + m0
            ds0 = jnp.where(causal, dot_nt(d_o0, v0), 0.0).astype(bf16)
            ds1 = jnp.where(causal, dot_nt(d_o1, v1), 0.0).astype(bf16)
            st0 = jnp.where(flipped, dot_nt(k, q0), 0.0).astype(bf16)
            st1 = jnp.where(flipped, dot_nt(k, q1), 0.0).astype(bf16)
            dst0 = jnp.where(flipped, dot_nt(v0, d_o0), 0.0).astype(bf16)
            dst1 = jnp.where(flipped, dot_nt(v1, d_o1), 0.0).astype(bf16)
            d_o = jnp.concatenate([d_o0, d_o1], 1)
            behind = later[group]
            after = jnp.where(keep_state, behind, 0.0).astype(bf16)
            after_v = jnp.where(own, jnp.where(left, behind[:, :PAIR], behind[:, PAIR:]), 0.0).astype(bf16)
            k0, k1 = k * m0, k * m1
            d_q = dot_nt(d_o, state_ref[group, 0]) + dot(ds0, k0) + dot(ds1, k1)
            d_k = dot_nt(jnp.concatenate([v0, v1], 1), after) + dot(dst0, q0) + dot(dst1, q1)
            d_v = dot(k, after_v) + dot(st0, dn0) + dot(st1, dn1)
            later[group] += dot_tn(q, d_o)
            e_q = d_q * q.astype(f32)
            e_k = d_k * k.astype(f32)
            both = jnp.concatenate([e_q, e_k], 0)
            fg[:, here] += jnp.sum((e_q + e_k).reshape(BLK // 8, 8, PAIR), axis=0)
            high = both.astype(bf16)
            lower = (both - high.astype(f32)).astype(bf16)
            turned = dot(jnp.concatenate([high, lower], 1), back_ref[...]) + dot(high, back_low_ref[...])
            dq = (turned[:BLK, :PAIR] * cosine + turned[:BLK, PAIR:] * sine).astype(bf16)
            dk = (turned[BLK:, :PAIR] * cosine + turned[BLK:, PAIR:] * sine).astype(bf16)
            dv = d_v.astype(bf16)
            dq_ref[:, here] = dq
            dk_ref[:, here] = dk
            dv_ref[:, here] = dv
            d_all[place, group * PAIR : (group + 1) * PAIR] = dq
            d_all[place, width + group * PAIR : width + (group + 1) * PAIR] = dk
            d_all[place, 2 * width + group * PAIR : 2 * width + (group + 1) * PAIR] = dv

    @pl.when(step == blocks)
    def _():
        load.wait()

    share_rows = D // comm.parts
    wide = D // BACK_STEPS
    for m in range(BACK_STEPS):

        @pl.when(phase == blocks + m)
        def _(m=m):
            made = dot_tn(normed[:, m * wide : (m + 1) * wide], d_all[...])
            for n in range(wide // share_rows):
                share = m * (wide // share_rows) + n
                qkv_own[call, comm.place(kinds, share, call)] = made[n * share_rows : (n + 1) * share_rows, :]
            if m == 0:
                total = jnp.sum(fg[...], axis=0, keepdims=True) / fw_ref[...]
                size = D // comm.parts
                core = lax.axis_index("stream")
                for n in range(width // size):
                    pair, inside = divmod(n * size, PAIR)
                    row = total[:, pair * PAIR : (pair + 1) * PAIR]
                    row = jnp.broadcast_to(row, (8, PAIR))
                    if inside:
                        row = pltpu.roll(row, PAIR - inside, 1)
                    share = core * (D // comm.streams // size) + call * (width // size) + n
                    feature_own[comm.place(feature_kind, share)] = row


def backward(comm, normed, g, w_proj, kept, cosine, sine, backs, sums, fw, flows, plan):
    q, k, v, mixed, den, states = kept
    rows = g.shape[0]
    streams, parts = comm.streams, comm.parts
    calls = HEADS // streams // 2 // GROUPS
    blocks = rows // BLK
    per = blocks + BACK_STEPS
    width = GROUPS * PAIR

    def at(i):
        return jnp.maximum(blocks - 1 - irem(i, per), 0)

    def call(i):
        return idiv(i, per)

    row_spec = pl.BlockSpec((BLK, width), lambda i: (at(i), call(i)))
    table_spec = pl.BlockSpec((BLK, PAIR), lambda i: (at(i), 0))
    low = jax.ShapeDtypeStruct((rows, calls * width), bf16)
    inner = []
    for c in range(calls):
        start, when = plan.get(f"q{c}", (None, ()))
        shape = (parts, D // parts, 3 * width)
        inner.append((Flow(f"q{c}", KIND[f"q{c}"], 0, shape, None, start, when, (c + 1) * per), 4, c))
    inner.append((Flow("feature", KIND["feature"], 0, (parts, 8, PAIR), None, None, (), calls * per), 5, None))
    return with_comm(
        comm,
        partial(backward_kernel, comm, blocks, [KIND[f"q{c}"] for c in range(calls)], KIND["feature"]),
        calls * per,
        [
            pl.BlockSpec((BLK, D), lambda i: (at(i), 0)),
            pl.BlockSpec((width, D), lambda i: (lax.axis_index("stream") * calls + call(i), 0)),
            row_spec,
            row_spec,
            row_spec,
            row_spec,
            row_spec,
            pl.BlockSpec((GROUPS, 1, PAIR, 2 * PAIR), lambda i: (call(i), at(i), 0, 0)),
            table_spec,
            table_spec,
            pl.BlockSpec((2 * PAIR, 2 * PAIR), lambda i: (0, 0)),
            pl.BlockSpec((PAIR, 2 * PAIR), lambda i: (0, 0)),
            pl.BlockSpec((2 * PAIR, PAIR), lambda i: (0, 0)),
            pl.BlockSpec((1, width), lambda i: (0, lax.axis_index("stream") * calls + call(i))),
            ANY,
        ],
        [row_spec, row_spec, row_spec],
        [low, low, low],
        flows,
        [g, w_proj, q, k, v, mixed, den, states, cosine, sine, *backs, sums, fw, normed],
        [
            pltpu.VMEM((GROUPS, PAIR, 2 * PAIR), f32),
            pltpu.VMEM((rows, 3 * width), bf16),
            pltpu.VMEM((rows, D), bf16),
            pltpu.VMEM((8, width), f32),
            pltpu.VMEM((calls, parts, D // parts, 3 * width), f32),
            pltpu.VMEM((parts, 8, PAIR), f32),
            pltpu.SemaphoreType.DMA,
        ],
        inner,
        name="attention_backward",
        cost_estimate=pl.CostEstimate(
            flops=2 * 65536 * GROUPS * calls * (blocks * 6500 + 16384),
            bytes_accessed=2 * (2 * rows * D + width * D + rows * width * 24),
            transcendentals=0,
        ),
    )


def tail_kernel(
    comm, tiles, gathered,
    act_ref, dh_ref, mix_ref, dq_ref, dk_ref, dv_ref, tok_ref, cot_ref, valid_ref, gain_ref,
    wproj_ref, wq_ref, wk_ref, wv_ref, win_hbm, wout_hbm,
    out_ref, grad_ref,
    win, wout, mine, arrived, in_sem, out_sem, send_sem, recv_sem,
):
    step = pl.program_id(0)
    units = win.shape[1]
    strips = unit_strips(comm, win_hbm, wout_hbm, 0, units, gathered)
    loads = []
    for n, (a, b, at, size) in enumerate(strips):
        loads.append(pltpu.make_async_copy(a, win.at[:, pl.ds(at, size)], in_sem.at[n]))
        loads.append(pltpu.make_async_copy(b, wout.at[pl.ds(at, size), :], out_sem.at[n]))

    def send(i):
        return pltpu.make_async_remote_copy(
            src_ref=mine.at[irem(i, 2)],
            dst_ref=arrived.at[i],
            send_sem=send_sem.at[i],
            recv_sem=recv_sem.at[i],
            device_id=comm.other_core(),
            device_id_type=MESH,
        )

    @pl.when(step == 0)
    def _():
        for load in loads:
            load.start()
        for load in loads:
            load.wait()

    @pl.when((step >= 2) & (step < tiles))
    def _():
        send(step - 2).wait_send()

    @pl.when(step < tiles)
    def _():
        slot = irem(step, 2)
        mine[slot, 0] = dot(act_ref[...], wout[...]) + dot(mix_ref[...], wproj_ref[...])
        d_normed = dot_nt(dh_ref[...], win[...]) + dot_nt(dq_ref[...], wq_ref[...])
        d_normed += dot_nt(dk_ref[...], wk_ref[...]) + dot_nt(dv_ref[...], wv_ref[...])
        mine[slot, 1] = d_normed
        send(step).start()

    @pl.when(step >= 1)
    def _():
        send(step - 1).wait_recv()
        slot = irem(step + 1, 2)
        x = tok_ref[...].astype(f32)
        centered = x - jnp.mean(x, axis=-1, keepdims=True)
        var = jnp.mean(centered * centered, axis=-1, keepdims=True)
        inv_std = lax.rsqrt(var + EPSILON)
        unit = centered * inv_std
        out_ref[...] = (x + (mine[slot, 0] + arrived[step - 1, 0]) * valid_ref[...]).astype(bf16)
        scaled = (mine[slot, 1] + arrived[step - 1, 1]) * gain_ref[...]
        mean = jnp.mean(scaled, axis=-1, keepdims=True)
        cross = jnp.mean(scaled * unit, axis=-1, keepdims=True)
        grad_ref[...] = (cot_ref[...].astype(f32) + inv_std * (scaled - mean - unit * cross)).astype(bf16)

    @pl.when(step == tiles)
    def _():
        send(tiles - 2).wait_send()
        send(tiles - 1).wait_send()


def tail(comm, active, d_hidden, mixed, d_qkv, tokens, cotangent, valid, gain, weights, w_proj, w_qkv, flows):
    w_in, w_out, gathered = weights
    rows, units = active.shape
    width = mixed.shape[1]
    tiles = rows // TILE
    strips = 1 if gathered else comm.parts
    streams = comm.streams

    def now(i):
        return (jnp.minimum(i, tiles - 1), 0)

    def before(i):
        return (jnp.maximum(i - 1, 0), 0)

    def weight(which):
        return pl.BlockSpec((D, width), lambda i: (0, which * streams + lax.axis_index("stream")))

    shape = jax.ShapeDtypeStruct((rows, D), bf16)
    return with_comm(
        comm,
        partial(tail_kernel, comm, tiles, gathered),
        tiles + 1,
        [
            pl.BlockSpec((TILE, units), now),
            pl.BlockSpec((TILE, units), now),
            pl.BlockSpec((TILE, width), now),
            pl.BlockSpec((TILE, width), now),
            pl.BlockSpec((TILE, width), now),
            pl.BlockSpec((TILE, width), now),
            pl.BlockSpec((TILE, D), before),
            pl.BlockSpec((TILE, D), before),
            pl.BlockSpec((TILE, 1), before),
            pl.BlockSpec((1, D), lambda i: (0, 0)),
            pl.BlockSpec((width, D), lambda i: (lax.axis_index("stream"), 0)),
            weight(0),
            weight(1),
            weight(2),
            ANY,
            ANY,
        ],
        [pl.BlockSpec((TILE, D), before), pl.BlockSpec((TILE, D), before)],
        [shape, shape],
        flows,
        [active, d_hidden, mixed, *d_qkv, tokens, cotangent, valid, gain, w_proj, w_qkv, w_qkv, w_qkv, w_in, w_out],
        [
            pltpu.VMEM((D, units), bf16),
            pltpu.VMEM((units, D), bf16),
            pltpu.VMEM((2, 2, TILE, D), f32),
            pltpu.VMEM((tiles, 2, TILE, D), f32),
            pltpu.SemaphoreType.DMA((strips,)),
            pltpu.SemaphoreType.DMA((strips,)),
            pltpu.SemaphoreType.DMA((tiles,)),
            pltpu.SemaphoreType.DMA((tiles,)),
        ],
        exchange=True,
        name="tail",
        cost_estimate=pl.CostEstimate(
            flops=2 * rows * D * (2 * units + 4 * width),
            bytes_accessed=2 * (rows + D) * (2 * units + 4 * width) + 8 * rows * D,
            transcendentals=0,
        ),
    )


KIND = {
    "in0": "xp", "in1": "zx", "in2": "yz", "in3": "zx", "o0": "zy", "o1": "xx", "o2": "xp", "o3": "zz",
    "pr": "xp", "q0": "xp", "q1": "xx", "feature": "xy",
}
FRONT = {"in0": (6, (13, 20, 25, 27)), "in1": (12, (23,)), "in2": (18, (-1,))}
FORWARD = {"in1": (0, (7, 9)), "in2": (0, (5, 8)), "in3": (0, (9,)), "o0": (0, (9,)), "o1": (0, (9,))}
BACKWARD = {
    "in1": (0, (5,)), "in2": (0, (5,)), "in3": (0, (6, 11, 16)), "o0": (0, (6, 11, 16)), "o2": (0, (10, 19)),
    "o3": (4, (19,)), "pr": (8, (15, 19)), "q0": (14, (19,)),
}
TAIL = {
    "o1": (0, (4, 8, -1)), "o2": (0, (3, 7)), "pr": (0, (3, 7)), "q0": (0, (7, -1)), "q1": (3, (8, -1)),
    "feature": (0, (1, 3, 5, 7)),
}


def solution(mesh):
    comm = Comm(mesh.shape["dp"], mesh.shape["stream"])
    parts, streams = comm.parts, comm.streams
    cosine_np, sine_np, map_np, back_high_np, back_low_np = attention_tables()
    sums_np = np.zeros((2 * PAIR, PAIR), np.float32)
    for base in (0, PAIR):
        sums_np[base : base + HEAD, HEAD] = 1.0
        sums_np[base + HEAD : base + PAIR, 0] = 1.0

    def partner(value):
        pairs = []
        for d in range(parts):
            for s in range(streams):
                pairs.append((d * streams + s, d * streams + (s ^ 1)))
        return lax.ppermute(value, ("dp", "stream"), pairs)

    def body(tokens, norm_gain, w_qkv, w_proj, w_in, w_out, feature_weight, lengths, cotangent):
        comm.kernels = 0
        rows = tokens.shape[0]
        chip = lax.axis_index("dp")
        stream = lax.axis_index("stream")
        gain = norm_gain.reshape(1, D)
        fw = feature_weight.reshape(1, D)
        cosine, sine = jnp.asarray(cosine_np), jnp.asarray(sine_np)
        valid = (jnp.arange(rows) < lengths[0]).astype(f32).reshape(rows, 1)
        weights = gather_units(comm, w_in, w_out)
        units = FF // streams
        done = {}

        def flows_of(plan):
            flows = []
            for name, (start, sums) in plan.items():
                if name in done and done[name][0] < comm.steps:
                    taken, array = done[name]
                    sums = sums[: comm.steps - taken]
                    flows.append(Flow(name, KIND[name], taken, array.shape, array, start, sums))
            return flows

        def landed(shares, plan):
            for name, array in shares.items():
                taken = done[name][0] if name in done else 0
                done[name] = (taken + (len(plan[name][1][: comm.steps - taken]) if name in plan else 0), array)

        (normed, g, act, d_hidden), shares = front(comm, tokens, cotangent, valid, gain, weights, FRONT)
        landed(shares, FRONT)
        kept, shares = forward(
            comm, normed, g, w_qkv, cosine, sine, fw, jnp.asarray(map_np), valid, flows_of(FORWARD), FORWARD
        )
        landed(shares, FORWARD)
        backs = (jnp.asarray(back_high_np), jnp.asarray(back_low_np))
        d_qkv, shares = backward(
            comm, normed, g, w_proj, kept, cosine, sine, backs, jnp.asarray(sums_np, bf16), fw,
            flows_of(BACKWARD), BACKWARD,
        )
        landed(shares, BACKWARD)
        (output, input_grad), shares = tail(
            comm, act, d_hidden, kept[3], d_qkv, tokens, cotangent, valid, gain, weights, w_proj, w_qkv,
            flows_of(TAIL),
        )
        landed(shares, TAIL)
        left = {}
        for name, (taken, _) in done.items():
            if taken < comm.steps:
                left[name] = (0, tuple(range(1, comm.steps - taken + 1)))
        if left:
            length = 1 + max(len(sums) for _, sums in left.values())
            _, shares = with_comm(
                comm, lambda *refs: None, length, [], [], [], flows_of(left), [], name="rest"
            )
            landed(shares, left)
        final = {name: array[0] for name, (_, array) in done.items()}

        value = final["feature"]
        value = value + partner(value)
        share = D // (parts * streams)
        feature_grad = lax.dynamic_slice(value, (0, stream * share), (1, share)).reshape(share)

        half = D // parts // streams
        names = [f"in{c}" for c in range(units // UNITS)]
        names += [f"q{c}" for c in range(HEADS // streams // 2 // GROUPS)] + ["pr"]
        mine = jnp.concatenate([lax.dynamic_slice_in_dim(final[n], stream * half, half) for n in names], 1)
        other = partner(
            jnp.concatenate([lax.dynamic_slice_in_dim(final[n], (1 - stream) * half, half) for n in names], 1)
        )
        a = jnp.where(stream == 0, mine, other)
        b = jnp.where(stream == 0, other, mine)
        unit = units // parts
        in_grad = jnp.concatenate(
            [src[:, unit * i : unit * (i + 1)] for i in range(parts) for src in (a, b)], 1
        )
        qa, qb = a[:, units : units + 3 * D // streams], b[:, units : units + 3 * D // streams]
        wide = GROUPS * PAIR
        calls = HEADS // streams // 2 // GROUPS

        def third(src, which):
            return [src[:, (3 * n + which) * wide : (3 * n + which + 1) * wide] for n in range(calls)]

        qkv_grad = jnp.concatenate(sum([third(qa, w) + third(qb, w) for w in range(3)], []), 1)
        proj_grad = jnp.concatenate([a[:, units + 3 * D // streams :], b[:, units + 3 * D // streams :]], 1)
        out_grad = jnp.concatenate([final[f"o{n}"] for n in range(D // OUT_COLUMNS)], 1)
        first_row = (chip * streams + stream) * half
        w_in_rows = lax.dynamic_slice_in_dim(w_in, first_row, half).astype(f32)
        w_qkv_rows = lax.dynamic_slice_in_dim(w_qkv, first_row, half).astype(f32)
        gain_rows = lax.dynamic_slice_in_dim(norm_gain, first_row, half)
        gain_grad = (jnp.sum(w_in_rows * in_grad, 1) + jnp.sum(w_qkv_rows * qkv_grad, 1)) / gain_rows
        return output, input_grad, gain_grad, qkv_grad, proj_grad, in_grad, out_grad, feature_grad

    both = P(("dp", "stream"), None)
    return jax.shard_map(
        body,
        mesh=mesh,
        in_specs=(P("dp", None), P(), P(), P(), P(), P(), P(), P("dp"), P("dp", None)),
        out_specs=(
            P("dp", None), P("dp", None), P(("dp", "stream")), both, both, both, both, P(("dp", "stream")),
        ),
        check_vma=False,
    )
```

time: 1360 us -> 316 us (0.23)
  waiting for transfers between devices: 602 us -> 0.01 us
  matrix products: 340 us -> 0 us
  Pallas kernels: 0 us -> 297 us
  local copies, waits for them, and re-layouts: 245 us -> 8.59 us
  other arithmetic: 102 us -> 7.36 us
  blocking collectives: 41 us -> 0 us
  between operations: 16.8 us -> 1.9 us
    reduce_scatter x4 -> x0, waiting for transfers between devices: 552 us -> none  [the longest x1 187 us: body(): lax.psum_scatter(g_in, ('dp', 'stream'), scatter_dimension=0, tiled=True)]
    dot_general x24 -> x0, matrix products: 340 us -> none  [the longest x1 30.7 us: attention_half(): jnp.einsum('bshi,im->bshm', queries, feature_map, precision=HIGHEST)]
    pallas_call x0 -> x5, Pallas kernels: none -> 297 us  [with_comm(): pl.pallas_call(run, grid=(steps,), in_specs=list(in_specs) + [ANY] * len(...]
    reshape x9 -> x1, local copies, waits for them, and re-layouts: 103 us -> 0.59 us  [body(): lax.dynamic_slice(value, (0, stream * share), (1, share)).reshape(share)]
    psum x1 -> x0, waiting for transfers between devices: 47.9 us -> none  [body(): lax.psum((branch * valid_rows, d_normed), 'stream')]
    unnamed x1 -> x0, blocking collectives: 41 us -> none
    another operation x8 -> x0, other arithmetic: 38.5 us -> none  [the longest x2 14.7 us: exclusive_later(): running = jnp.flip(jnp.cumsum(jnp.flip(blocks_in, 2), axis=2), 2)]
    slice x11 -> x2, local copies, waits for them, and re-layouts: 38.3 us -> 0.01 us  [the longest x1 0.01 us: body(): a[:, units + 3 * D // streams:]]
  transfers between devices with their start and end apart: 5 -> 2, of which waited for: 5 -> 0; matrix products, arithmetic and copies ran while one was open for 3% -> 1% of each run, Pallas kernels for 0% -> 0%
where the time goes in v2:
time: 316 us
  Pallas kernels  297 us (94%)
  local copies, waits for them, and re-layouts  8.59 us (3%)
  other arithmetic  7.36 us (2%)
    pallas_call x5, Pallas kernels, with_comm(): pl.pallas_call(run, grid=(steps,), in_specs=list(in_specs) + [ANY] * len(...  297 us
    unnamed x76, local copies, waits for them, and re-layouts  7.96 us
  transfers between devices with their start and end apart: 2, of which 0 were waited for; matrix products, arithmetic and copies ran while one was open for 1% of the time, Pallas kernels for 0%

profile of v2, /device:TPU:0, one launch (start us, length us, event | category | flops | bytes accessed | tf_op | source)
XLA Modules:
  0.0 315.9 jit_solution(4177055977454384081)
XLA Ops:
  1.3 1.1 fusion.refs_2_.refs_8_
  2.4 75.7 %front.1 = (bf16[2048,1024]{1,0:T(8,128)(2,1)}, bf16[2048,1024]{1,0:T(8,128)(2,1)}, bf16[2048,2048]{1,0:T(8,128)(2,1)}, bf16[2048,2048]{1,0:T(8,128)(2,1)}, f32[...) custom-call(bf16[2048,1024]{1,0:T(8,128)(2,1)} %refs_6_.1, ...), custom_call_target="tpu_custom_call" | custom-call | flops 34359738368 | bytes 41943040 | tf_op jit(solution)/shard_map/front/pallas_call | solution.py:324
  78.0 46.1 %attention_forward.1 = (bf16[2048,512]{1,0:T(8,128)(2,1)}, bf16[2048,512]{1,0:T(8,128)(2,1)}, bf16[2048,512]{1,0:T(8,128)(2,1)}, bf16[2048,512]{1,0:T(8,128)(2,1...) custom-call(bf16[2048,1024]{1,0:T(8,128)(2,1)} %get-tuple-element.58, ...), custom_call_target="tpu_custom_call" | custom-call | flops 20971520000 | bytes 24117248 | tf_op jit(solution)/shard_map/attention_forward/pallas_call | solution.py:324
  124.1 64.1 %attention_backward.1 = (bf16[2048,512]{1,0:T(8,128)(2,1)}, bf16[2048,512]{1,0:T(8,128)(2,1)}, bf16[2048,512]{1,0:T(8,128)(2,1)}, f32[1,64,512]{2,1,0:T(8,128)},...) custom-call(bf16[2048,1024]{1,0:T(8,128)(2,1)} %get-tuple-element.59, ...), custom_call_target="tpu_custom_call" | custom-call | flops 35852910592 | bytes 34078720 | tf_op jit(solution)/shard_map/attention_backward/pallas_call | solution.py:324
  188.2 79.7 %tail.1 = (bf16[2048,1024]{1,0:T(8,128)(2,1)}, bf16[2048,1024]{1,0:T(8,128)(2,1)}, f32[1,128,256]{2,1,0:T(8,128)}, f32[1,128,256]{2,1,0:T(8,128)}, f32[1,64,512]...) custom-call(bf16[2048,2048]{1,0:T(8,128)(2,1)} %get-tuple-element.56.refs_0_, ...), custom_call_target="tpu_custom_call" | custom-call | flops 25769803776 | bytes 54525952 | tf_op jit(solution)/shard_map/tail/pallas_call | solution.py:324
  267.9 0.0 copy-start.6
  267.9 0.0 copy-start.12
  267.9 0.0 copy-start.9
  267.9 0.0 copy-start.10
  267.9 0.0 copy-start.11
  267.9 32.0 %rest.1 = (f32[1,128,256]{2,1,0:T(8,128)}, f32[1,64,768]{2,1,0:T(8,128)}, f32[1,64,768]{2,1,0:T(8,128)}) custom-call(f32[8,128,256]{2,1,0:T(8,128)} %get-tuple-element.93.refs_0_, f32[2,64,768]{2,1,0:T(8,128)} %get-tuple-element.94.refs_1_, f32[4,64,768]{2,1,0:T(8,128)} %get-tuple-element.95.refs_2_), custom_call_target="tpu_custom_call" | custom-call | tf_op jit(solution)/shard_map/rest/pallas_call | solution.py:324
  300.0 0.0 copy-done.8
  300.1 1.0 constant_dynamic-update-slice_fusion.9
  301.1 1.0 constant_dynamic-update-slice_fusion.8
  302.1 0.1 collective-permute-start
  302.2 0.0 copy-done.12
  302.2 0.5 collective-permute-start.1
  302.7 0.0 copy-done.9
  302.7 1.8 pad_maximum_fusion
  304.4 0.0 collective-permute-done.1
  304.4 0.6 fusion.1
  305.0 0.0 collective-permute-done
  305.0 0.1 broadcast_select_fusion
  305.3 0.0 copy-start.3
  305.7 0.0 copy-start.2
  305.7 1.4 multiply_reduce_fusion.1
  307.1 1.1 multiply_reduce_fusion
  308.2 0.7 pad_maximum_fusion.1
  308.9 1.3 dynamic-slice_divide_fusion
  310.2 2.1 copy.80
  312.3 1.6 copy-done
  313.9 2.0 copy.81
  (67 shorter events, 0.4 us)
Async XLA Ops:
  188.2 111.8 %copy-start.4 = (f32[1,64,512]{2,1,0:T(8,128)S(1)}, f32[1,64,512]{2,1,0:T(8,128)}, u32[]{:S(2)}) copy-start(f32[1,64,512]{2,1,0:T(8,128)} %get-tuple-element.89) | copy-start | bytes 393220
  188.2 111.8 %copy-start.8 = (f32[1,64,512]{2,1,0:T(8,128)S(1)}, f32[1,64,512]{2,1,0:T(8,128)}, u32[]{:S(2)}) copy-start(f32[1,64,512]{2,1,0:T(8,128)} %get-tuple-element.90) | copy-start | bytes 393220
  188.2 111.9 %copy-start.7 = (f32[1,64,512]{2,1,0:T(8,128)S(1)}, f32[1,64,512]{2,1,0:T(8,128)}, u32[]{:S(2)}) copy-start(f32[1,64,512]{2,1,0:T(8,128)} %get-tuple-element.91) | copy-start | bytes 393220
  188.2 111.9 %copy-start.5 = (f32[1,64,512]{2,1,0:T(8,128)S(1)}, f32[1,64,512]{2,1,0:T(8,128)}, u32[]{:S(2)}) copy-start(f32[1,64,512]{2,1,0:T(8,128)} %get-tuple-element.92) | copy-start | bytes 393220
  267.9 34.2 %copy-start.6 = (f32[1,64,512]{2,1,0:T(8,128)S(1)}, f32[1,64,512]{2,1,0:T(8,128)}, u32[]{:S(2)}) copy-start(f32[1,64,512]{2,1,0:T(8,128)} %get-tuple-element.98) | copy-start | bytes 393220
  267.9 34.3 %copy-start.12 = (f32[1,8,128]{2,1,0:T(8,128)S(1)}, f32[1,8,128]{2,1,0:T(8,128)}, u32[]{:S(2)}) copy-start(f32[1,8,128]{2,1,0:T(8,128)} %get-tuple-element.103) | copy-start | bytes 12292
  267.9 34.8 %copy-start.9 = (f32[1,128,256]{2,1,0:T(8,128)S(1)}, f32[1,128,256]{2,1,0:T(8,128)}, u32[]{:S(2)}) copy-start(f32[1,128,256]{2,1,0:T(8,128)} %get-tuple-element.99) | copy-start | bytes 393220
  267.9 34.8 %copy-start.10 = (f32[1,128,256]{2,1,0:T(8,128)S(1)}, f32[1,128,256]{2,1,0:T(8,128)}, u32[]{:S(2)}) copy-start(f32[1,128,256]{2,1,0:T(8,128)} %get-tuple-element.100) | copy-start | bytes 393220
  267.9 34.8 %copy-start.11 = (f32[1,128,256]{2,1,0:T(8,128)S(1)}, f32[1,128,256]{2,1,0:T(8,128)}, u32[]{:S(2)}) copy-start(f32[1,128,256]{2,1,0:T(8,128)} %get-tuple-element.101) | copy-start | bytes 393220
  302.1 2.9 collective-permute-start
  302.2 2.3 collective-permute-start.1
  304.4 5.8 %copy-start.1 = (bf16[2048,1024]{1,0:T(8,128)(2,1)S(1)}, bf16[2048,1024]{1,0:T(8,128)(2,1)}, u32[]{:S(2)}) copy-start(bf16[2048,1024]{1,0:T(8,128)(2,1)} %get-tuple-element.128) | copy-start | bytes 12582916
  305.3 7.0 %copy-start.3 = (f32[32,3072]{1,0:T(8,128)}, f32[32,3072]{1,0:T(8,128)S(1)}, u32[]{:S(2)}) copy-start(f32[32,3072]{1,0:T(8,128)S(1)} %constant_dynamic-update-slice_fusion.46) | copy-start | bytes 1179652
  305.7 6.6 %copy-start.2 = (f32[32,4096]{1,0:T(8,128)}, f32[32,4096]{1,0:T(8,128)S(1)}, u32[]{:S(2)}) copy-start(f32[32,4096]{1,0:T(8,128)S(1)} %constant_dynamic-update-slice_fusion.14) | copy-start | bytes 1572868
  310.2 3.7 %copy-start = (bf16[2048,1024]{1,0:T(8,128)(2,1)S(1)}, bf16[2048,1024]{1,0:T(8,128)(2,1)}, u32[]{:S(2)}) copy-start(bf16[2048,1024]{1,0:T(8,128)(2,1)} %get-tuple-element.129) | copy-start | bytes 12582916

commit v3 on v2

--- a/solution.py
+++ b/solution.py
@@ -164,7 +164,7 @@
 
     def scratch(self):
         half, (_, rows, columns) = self.half, self.shape
-        kept = [pltpu.VMEM((half, rows, columns), f32)] if self.array is not None else []
+        kept = [pltpu.VMEM((2 * half, rows, columns), f32)] if self.array is not None else []
         count = max(len(self.sums), 1)
         return kept + [
             pltpu.VMEM((max(self.slots, 1), rows, columns), f32),
@@ -184,12 +184,8 @@
 
     def remote(self, k):
         count = self.half >> k
-        if k == 0 and self.array is not None:
-            source = self.source.at[pl.ds(count, count)]
-        else:
-            source = self.own.at[pl.ds(count, count)]
         return pltpu.make_async_remote_copy(
-            src_ref=source,
+            src_ref=self.own.at[pl.ds(count, count)],
             dst_ref=self.recv.at[pl.ds(self.offset(k), count)],
             send_sem=self.send_sem.at[k],
             recv_sem=self.recv_sem.at[k],
@@ -198,7 +194,7 @@
         )
 
     def load(self):
-        return pltpu.make_async_copy(self.source.at[pl.ds(0, self.half)], self.own, self.local_sem.at[0])
+        return pltpu.make_async_copy(self.source, self.own, self.local_sem.at[0])
 
     def store(self):
         return pltpu.make_async_copy(
@@ -220,11 +216,17 @@
 
         if not last:
 
+            if self.array is not None and self.start > 0:
+
+                @pl.when(step == self.start - 1)
+                def _():
+                    self.load().start()
+
             @pl.when(step == self.start)
             def _():
+                if self.array is not None:
+                    self.load().wait()
                 self.remote(0).start()
-                if self.array is not None:
-                    self.load().start()
 
         for k, at in enumerate(self.sums):
             if (at < 0) != last:
@@ -233,8 +235,6 @@
             @pl.when(step >= 0 if last else step == at)
             def _(k=k):
                 self.remote(k).wait_recv()
-                if k == 0 and self.array is not None:
-                    self.load().wait()
                 count = self.half >> k
                 base = self.offset(k)
 
@@ -290,6 +290,9 @@
 
             @pl.when(step == 0)
             def _():
+                for flow in every:
+                    if flow.array is not None and flow.start == 0:
+                        flow.load().start()
                 barrier = pltpu.get_barrier_semaphore()
                 chip, core = lax.axis_index("dp"), lax.axis_index("stream")
                 others = []
@@ -362,20 +365,14 @@
 
 
 def gelu_parts(x):
-    density = jnp.exp(x * x * -0.5)
-    t = 1.0 / (1.0 + (0.3275911 / math.sqrt(2.0)) * jnp.abs(x))
-    poly = 1.061405429 * t - 1.453152027
-    poly = poly * t + 1.421413741
-    poly = poly * t - 0.284496736
-    poly = (poly * t + 0.254829592) * t
-    tail = 0.5 * poly * density
-    cdf = jnp.where(x >= 0, 1.0 - tail, tail)
-    return x * cdf, cdf + x * density * (1.0 / math.sqrt(2.0 * math.pi))
+    cdf = 0.5 + 0.5 * lax.erf(x * math.sqrt(0.5))
+    return x * cdf, cdf + x * jnp.exp(x * x * -0.5) * (1.0 / math.sqrt(2.0 * math.pi))
 
 
 TILE = 256
 UNITS = 512
-CHUNK_STEPS = 6
+FRONT_TILE = 1024
+CHUNK_STEPS = SLOT // FRONT_TILE + 1
 OUT_COLUMNS = 256
 
 
@@ -383,13 +380,13 @@
     comm, kinds, out_kinds, gathered,
     tok_hbm, cot_hbm, valid_ref, gain_ref, win_hbm, wout_hbm,
     normed_hbm, g_hbm, act_hbm, dh_hbm,
-    normed, g, win, wout, h_a, h_b, d_a, d_b, act, d_hidden, in_own, out_own,
+    normed, g, win, wout, act, d_hidden, in_own, out_own,
     tok_sem, cot_sem, in_sem, out_sem, normed_sem, g_sem, act_sem, dh_sem,
 ):
     step = pl.program_id(0)
     rows = normed.shape[0]
     chunks = act.shape[0]
-    tile = 2 * TILE
+    tile = FRONT_TILE
     tiles = rows // tile
     chunk = idiv(step, CHUNK_STEPS)
     phase = irem(step, CHUNK_STEPS)
@@ -415,10 +412,9 @@
 
     def low_stores(c):
         columns = pl.ds(pl.multiple_of(c * UNITS, UNITS), UNITS)
-        here = pl.ds(TILE, rows)
         return (
-            pltpu.make_async_copy(act.at[c, here, :], act_hbm.at[:, columns], act_sem.at[c]),
-            pltpu.make_async_copy(d_hidden.at[irem(c, 2), here, :], dh_hbm.at[:, columns], dh_sem.at[c]),
+            pltpu.make_async_copy(act.at[c], act_hbm.at[:, columns], act_sem.at[c]),
+            pltpu.make_async_copy(d_hidden.at[irem(c, 2)], dh_hbm.at[:, columns], dh_sem.at[c]),
         )
 
     @pl.when(step == 0)
@@ -454,39 +450,25 @@
         for load in weight_loads(chunk + 1):
             load.start()
 
-    def finish_tile(h, d, place):
-        value, slope = gelu_parts(h[...])
-        here = pl.ds(pl.multiple_of(place, TILE), TILE)
+    @pl.when(working & (phase < tiles))
+    def _():
+        here = tile_rows(phase)
+        hidden = dot(normed[here, :], win[slot])
+        d_active = dot_nt(g[here, :], wout[slot])
+        value, slope = gelu_parts(hidden)
         act[chunk, here, :] = value.astype(bf16)
-        d_hidden[slot, here, :] = (d[...] * slope).astype(bf16)
-
-    @pl.when(working & (phase < tiles))
-    def _():
-        first = pl.multiple_of(phase * tile, tile)
-        here_a, here_b = pl.ds(first, TILE), pl.ds(first + TILE, TILE)
-        finish_tile(h_b, d_b, phase * tile)
-        h_a[...] = dot(normed[here_a, :], win[slot])
-        d_a[...] = dot_nt(g[here_a, :], wout[slot])
-        finish_tile(h_a, d_a, phase * tile + TILE)
-        h_b[...] = dot(normed[here_b, :], win[slot])
-        d_b[...] = dot_nt(g[here_b, :], wout[slot])
+        d_hidden[slot, here, :] = (d_active * slope).astype(bf16)
 
     share_rows = D // comm.parts
-    wide = D // 2
-    for m in range(2):
-
-        @pl.when(working & (phase == tiles + m))
-        def _(m=m):
-            if m == 0:
-                finish_tile(h_b, d_b, rows)
-                for copy in low_stores(chunk):
-                    copy.start()
-            made = dot_tn(normed[:, m * wide : (m + 1) * wide], d_hidden[slot, TILE : TILE + rows, :])
-            for n in range(wide // share_rows):
-                share = m * (wide // share_rows) + n
-                in_own[chunk, comm.place(kinds, share, chunk)] = made[n * share_rows : (n + 1) * share_rows, :]
-            if m == 1:
-                low_stores(chunk)[1].wait()
+
+    @pl.when(working & (phase == tiles))
+    def _():
+        for copy in low_stores(chunk):
+            copy.start()
+        made = dot_tn(normed[...], d_hidden[slot])
+        for share in range(comm.parts):
+            in_own[chunk, comm.place(kinds, share, chunk)] = made[share * share_rows : (share + 1) * share_rows, :]
+        low_stores(chunk)[1].wait()
 
     unit_rows = FF // comm.streams // comm.parts
     blocks = D // OUT_COLUMNS
@@ -496,7 +478,7 @@
         def _(block=block):
             right = g[:, block * OUT_COLUMNS : (block + 1) * OUT_COLUMNS]
             for c in range(chunks):
-                made = dot_tn(act[c, TILE : TILE + rows, :], right)
+                made = dot_tn(act[c], right)
                 for n in range(UNITS // unit_rows):
                     share = c * (UNITS // unit_rows) + n
                     out_own[block, comm.place(out_kinds[block], share)] = made[n * unit_rows : (n + 1) * unit_rows, :]
@@ -515,7 +497,7 @@
     rows = tokens.shape[0]
     units = FF // comm.streams
     chunks, blocks = units // UNITS, D // OUT_COLUMNS
-    tiles = rows // (2 * TILE)
+    tiles = rows // FRONT_TILE
     parts = comm.parts
     strips = 1 if gathered else UNITS // (units // parts)
     share_rows, unit_rows = D // parts, units // parts
@@ -527,12 +509,12 @@
         start, sums = plan.get(f"in{c}", (None, ()))
         shape = (parts, share_rows, UNITS)
         flow = Flow(f"in{c}", kinds[c], 0, shape, None, start, sums, (c + 1) * CHUNK_STEPS)
-        inner.append((flow, 10, c))
+        inner.append((flow, 6, c))
     for b in range(blocks):
         start, sums = plan.get(f"o{b}", (None, ()))
         shape = (parts, unit_rows, OUT_COLUMNS)
         flow = Flow(f"o{b}", out_kinds[b], 0, shape, None, start, sums, chunks * CHUNK_STEPS + b + 1)
-        inner.append((flow, 11, b))
+        inner.append((flow, 7, b))
     low = jax.ShapeDtypeStruct((rows, D), bf16)
     wide = jax.ShapeDtypeStruct((rows, units), bf16)
     return with_comm(
@@ -549,12 +531,8 @@
             pltpu.VMEM((rows, D), bf16),
             pltpu.VMEM((2, D, UNITS), bf16),
             pltpu.VMEM((2, UNITS, D), bf16),
-            pltpu.VMEM((TILE, UNITS), f32),
-            pltpu.VMEM((TILE, UNITS), f32),
-            pltpu.VMEM((TILE, UNITS), f32),
-            pltpu.VMEM((TILE, UNITS), f32),
-            pltpu.VMEM((chunks, rows + TILE, UNITS), bf16),
-            pltpu.VMEM((2, rows + TILE, UNITS), bf16),
+            pltpu.VMEM((chunks, rows, UNITS), bf16),
+            pltpu.VMEM((2, rows, UNITS), bf16),
             pltpu.VMEM((chunks, parts, share_rows, UNITS), f32),
             pltpu.VMEM((blocks, parts, unit_rows, OUT_COLUMNS), f32),
             pltpu.SemaphoreType.DMA((tiles,)),
@@ -627,43 +605,52 @@
         keep_state = state_mask()
         first = lax.broadcasted_iota(jnp.int32, (BLK, PAIR), 1) < HEAD
         place = pl.ds(pl.multiple_of(step * BLK, BLK), BLK)
-        for group in range(groups):
-            here = slice(group * PAIR, (group + 1) * PAIR)
-            queries, keys = queries_all[:, here], keys_all[:, here]
-            turned = jnp.concatenate(
+        each = range(groups)
+        lanes = [slice(group * PAIR, (group + 1) * PAIR) for group in each]
+        turned = [
+            jnp.concatenate(
                 [
-                    jnp.concatenate([queries * cosine, queries * sine], 1),
-                    jnp.concatenate([keys * cosine, keys * sine], 1),
+                    jnp.concatenate([queries_all[:, here] * cosine, queries_all[:, here] * sine], 1),
+                    jnp.concatenate([keys_all[:, here] * cosine, keys_all[:, here] * sine], 1),
                 ],
                 0,
             )
-            high = turned.astype(bf16)
-            low = (turned - high.astype(f32)).astype(bf16)
-            main = dot(high, map_ref[...])
-            exponent = main[:, :PAIR] + main[:, PAIR:] + dot(low, map_ref[:, :PAIR])
-            phi = jnp.exp(exponent) * fw_ref[:, here]
-            q = phi[:BLK].astype(bf16)
-            k = (phi[BLK:] * valid).astype(bf16)
-            v = values_all[:, here].astype(bf16)
-            q_ref[:, here] = q
-            k_ref[:, here] = k
-            v_ref[:, here] = v
-            v0, v1 = v * m0 + m1, v * m1 + m0
-            s0 = jnp.where(causal, dot_nt(q * m0, k), 0.0).astype(bf16)
-            s1 = jnp.where(causal, dot_nt(q * m1, k), 0.0).astype(bf16)
-            before = jnp.where(keep_state, state[group], 0.0).astype(bf16)
-            state_ref[group, 0] = before
-            far = dot(q, before)
-            o0 = dot(s0, v0) + far[:, :PAIR]
-            o1 = dot(s1, v1) + far[:, PAIR:]
-            numerator = jnp.where(first, o0, o1)
-            denominator = pltpu.roll(jnp.where(first, o1, o0), HEAD, 1)
+            for here in lanes
+        ]
+        high = [t.astype(bf16) for t in turned]
+        low = [(t - h.astype(f32)).astype(bf16) for t, h in zip(turned, high)]
+        main = [dot(h, map_ref[...]) for h in high]
+        rest = [dot(l, map_ref[:, :PAIR]) for l in low]
+        phi = [
+            jnp.exp(m[:, :PAIR] + m[:, PAIR:] + r) * fw_ref[:, here] for m, r, here in zip(main, rest, lanes)
+        ]
+        q = [f[:BLK].astype(bf16) for f in phi]
+        k = [(f[BLK:] * valid).astype(bf16) for f in phi]
+        v = [values_all[:, here].astype(bf16) for here in lanes]
+        for n in each:
+            q_ref[:, lanes[n]] = q[n]
+            k_ref[:, lanes[n]] = k[n]
+            v_ref[:, lanes[n]] = v[n]
+        v0 = [x * m0 + m1 for x in v]
+        v1 = [x * m1 + m0 for x in v]
+        s0 = [jnp.where(causal, dot_nt(q[n] * m0, k[n]), 0.0).astype(bf16) for n in each]
+        s1 = [jnp.where(causal, dot_nt(q[n] * m1, k[n]), 0.0).astype(bf16) for n in each]
+        before = [jnp.where(keep_state, state[n], 0.0).astype(bf16) for n in each]
+        far = [dot(q[n], before[n]) for n in each]
+        o0 = [dot(s0[n], v0[n]) + far[n][:, :PAIR] for n in each]
+        o1 = [dot(s1[n], v1[n]) + far[n][:, PAIR:] for n in each]
+        for n in each:
+            state_ref[n, 0] = before[n]
+            state[n] += dot_tn(k[n], jnp.concatenate([v0[n], v1[n]], 1))
+        for n in each:
+            here = lanes[n]
+            numerator = jnp.where(first, o0[n], o1[n])
+            denominator = pltpu.roll(jnp.where(first, o1[n], o0[n]), HEAD, 1)
             mixed = (numerator / denominator).astype(bf16)
             mix_ref[:, here] = mixed
             mixed_all[place, here] = mixed
             sent[step, :, here] = mixed.astype(f32)
             den_ref[:, here] = denominator
-            state[group] += dot_tn(k, jnp.concatenate([v0, v1], 1))
         to_partner(step).start()
 
     share_rows = D // comm.parts
@@ -790,51 +777,63 @@
         cosine, sine = cos_ref[...], sin_ref[...]
         d_mixed_all = dot_nt(g_ref[...], wp_ref[...])
         place = pl.ds(pl.multiple_of((blocks - 1 - phase) * BLK, BLK), BLK)
-        for group in range(GROUPS):
-            here = slice(group * PAIR, (group + 1) * PAIR)
-            numer = d_mixed_all[:, here] / den_ref[:, here]
-            product = numer * mix_ref[:, here].astype(f32)
-            p_high = product.astype(bf16)
-            p_low = (product - p_high.astype(f32)).astype(bf16)
-            sums = dot(jnp.concatenate([p_high, p_low], 1), sums_ref[...])
-            d_o0 = jnp.where(first, numer, -sums).astype(bf16)
-            d_o1 = jnp.where(first, -sums, numer).astype(bf16)
-            low = numer.astype(bf16)
-            dn0, dn1 = low * m0, low * m1
-            q, k, v = q_ref[:, here], k_ref[:, here], v_ref[:, here]
-            q0, q1 = q * m0, q * m1
-            v0, v1 = v * m0 + m1, v * m1 + m0
-            ds0 = jnp.where(causal, dot_nt(d_o0, v0), 0.0).astype(bf16)
-            ds1 = jnp.where(causal, dot_nt(d_o1, v1), 0.0).astype(bf16)
-            st0 = jnp.where(flipped, dot_nt(k, q0), 0.0).astype(bf16)
-            st1 = jnp.where(flipped, dot_nt(k, q1), 0.0).astype(bf16)
-            dst0 = jnp.where(flipped, dot_nt(v0, d_o0), 0.0).astype(bf16)
-            dst1 = jnp.where(flipped, dot_nt(v1, d_o1), 0.0).astype(bf16)
-            d_o = jnp.concatenate([d_o0, d_o1], 1)
-            behind = later[group]
-            after = jnp.where(keep_state, behind, 0.0).astype(bf16)
-            after_v = jnp.where(own, jnp.where(left, behind[:, :PAIR], behind[:, PAIR:]), 0.0).astype(bf16)
-            k0, k1 = k * m0, k * m1
-            d_q = dot_nt(d_o, state_ref[group, 0]) + dot(ds0, k0) + dot(ds1, k1)
-            d_k = dot_nt(jnp.concatenate([v0, v1], 1), after) + dot(dst0, q0) + dot(dst1, q1)
-            d_v = dot(k, after_v) + dot(st0, dn0) + dot(st1, dn1)
-            later[group] += dot_tn(q, d_o)
-            e_q = d_q * q.astype(f32)
-            e_k = d_k * k.astype(f32)
-            both = jnp.concatenate([e_q, e_k], 0)
-            fg[:, here] += jnp.sum((e_q + e_k).reshape(BLK // 8, 8, PAIR), axis=0)
-            high = both.astype(bf16)
-            lower = (both - high.astype(f32)).astype(bf16)
-            turned = dot(jnp.concatenate([high, lower], 1), back_ref[...]) + dot(high, back_low_ref[...])
-            dq = (turned[:BLK, :PAIR] * cosine + turned[:BLK, PAIR:] * sine).astype(bf16)
-            dk = (turned[BLK:, :PAIR] * cosine + turned[BLK:, PAIR:] * sine).astype(bf16)
-            dv = d_v.astype(bf16)
+        each = range(GROUPS)
+        lanes = [slice(group * PAIR, (group + 1) * PAIR) for group in each]
+        q = [q_ref[:, here] for here in lanes]
+        k = [k_ref[:, here] for here in lanes]
+        v = [v_ref[:, here] for here in lanes]
+        q0, q1 = [x * m0 for x in q], [x * m1 for x in q]
+        k0, k1 = [x * m0 for x in k], [x * m1 for x in k]
+        v0, v1 = [x * m0 + m1 for x in v], [x * m1 + m0 for x in v]
+        st0 = [jnp.where(flipped, dot_nt(k[n], q0[n]), 0.0).astype(bf16) for n in each]
+        st1 = [jnp.where(flipped, dot_nt(k[n], q1[n]), 0.0).astype(bf16) for n in each]
+        numer = [d_mixed_all[:, here] / den_ref[:, here] for here in lanes]
+        product = [numer[n] * mix_ref[:, lanes[n]].astype(f32) for n in each]
+        p_high = [x.astype(bf16) for x in product]
+        p_low = [(x - h.astype(f32)).astype(bf16) for x, h in zip(product, p_high)]
+        sums = [dot(jnp.concatenate([p_high[n], p_low[n]], 1), sums_ref[...]) for n in each]
+        behind = [later[n] for n in each]
+        after = [jnp.where(keep_state, x, 0.0).astype(bf16) for x in behind]
+        after_v = [
+            jnp.where(own, jnp.where(left, x[:, :PAIR], x[:, PAIR:]), 0.0).astype(bf16) for x in behind
+        ]
+        d_v = [dot(k[n], after_v[n]) for n in each]
+        d_k = [dot_nt(jnp.concatenate([v0[n], v1[n]], 1), after[n]) for n in each]
+        d_o0 = [jnp.where(first, numer[n], -sums[n]).astype(bf16) for n in each]
+        d_o1 = [jnp.where(first, -sums[n], numer[n]).astype(bf16) for n in each]
+        d_o = [jnp.concatenate([d_o0[n], d_o1[n]], 1) for n in each]
+        low = [x.astype(bf16) for x in numer]
+        ds0 = [jnp.where(causal, dot_nt(d_o0[n], v0[n]), 0.0).astype(bf16) for n in each]
+        ds1 = [jnp.where(causal, dot_nt(d_o1[n], v1[n]), 0.0).astype(bf16) for n in each]
+        dst0 = [jnp.where(flipped, dot_nt(v0[n], d_o0[n]), 0.0).astype(bf16) for n in each]
+        dst1 = [jnp.where(flipped, dot_nt(v1[n], d_o1[n]), 0.0).astype(bf16) for n in each]
+        d_q = [dot_nt(d_o[n], state_ref[n, 0]) for n in each]
+        d_v = [d_v[n] + dot(st0[n], low[n] * m0) + dot(st1[n], low[n] * m1) for n in each]
+        d_q = [d_q[n] + dot(ds0[n], k0[n]) + dot(ds1[n], k1[n]) for n in each]
+        d_k = [d_k[n] + dot(dst0[n], q0[n]) + dot(dst1[n], q1[n]) for n in each]
+        for n in each:
+            later[n] += dot_tn(q[n], d_o[n])
+        e_q = [d_q[n] * q[n].astype(f32) for n in each]
+        e_k = [d_k[n] * k[n].astype(f32) for n in each]
+        both = [jnp.concatenate([e_q[n], e_k[n]], 0) for n in each]
+        high = [x.astype(bf16) for x in both]
+        lower = [(x - h.astype(f32)).astype(bf16) for x, h in zip(both, high)]
+        turned = [
+            dot(jnp.concatenate([high[n], lower[n]], 1), back_ref[...]) + dot(high[n], back_low_ref[...])
+            for n in each
+        ]
+        for n in each:
+            here = lanes[n]
+            fg[:, here] += jnp.sum((e_q[n] + e_k[n]).reshape(BLK // 8, 8, PAIR), axis=0)
+            dv = d_v[n].astype(bf16)
+            dq = (turned[n][:BLK, :PAIR] * cosine + turned[n][:BLK, PAIR:] * sine).astype(bf16)
+            dk = (turned[n][BLK:, :PAIR] * cosine + turned[n][BLK:, PAIR:] * sine).astype(bf16)
             dq_ref[:, here] = dq
             dk_ref[:, here] = dk
             dv_ref[:, here] = dv
-            d_all[place, group * PAIR : (group + 1) * PAIR] = dq
-            d_all[place, width + group * PAIR : width + (group + 1) * PAIR] = dk
-            d_all[place, 2 * width + group * PAIR : 2 * width + (group + 1) * PAIR] = dv
+            d_all[place, n * PAIR : (n + 1) * PAIR] = dq
+            d_all[place, width + n * PAIR : width + (n + 1) * PAIR] = dk
+            d_all[place, 2 * width + n * PAIR : 2 * width + (n + 1) * PAIR] = dv
 
     @pl.when(step == blocks)
     def _():
@@ -935,9 +934,9 @@
 def tail_kernel(
     comm, tiles, gathered,
     act_ref, dh_ref, mix_ref, dq_ref, dk_ref, dv_ref, tok_ref, cot_ref, valid_ref, gain_ref,
-    wproj_ref, wq_ref, wk_ref, wv_ref, win_hbm, wout_hbm,
+    wproj_ref, wqkv_hbm, win_hbm, wout_hbm,
     out_ref, grad_ref,
-    win, wout, mine, arrived, in_sem, out_sem, send_sem, recv_sem,
+    win, wout, wqkv, mine, arrived, in_sem, out_sem, qkv_sem, send_sem, recv_sem,
 ):
     step = pl.program_id(0)
     units = win.shape[1]
@@ -947,12 +946,20 @@
         loads.append(pltpu.make_async_copy(a, win.at[:, pl.ds(at, size)], in_sem.at[n]))
         loads.append(pltpu.make_async_copy(b, wout.at[pl.ds(at, size), :], out_sem.at[n]))
 
-    def send(i):
+    core = lax.axis_index("stream")
+    width = mix_ref.shape[1]
+    for n in range(3):
+        start = pl.multiple_of((n * comm.streams + core) * width, width)
+        loads.append(
+            pltpu.make_async_copy(wqkv_hbm.at[:, pl.ds(start, width)], wqkv.at[:, pl.ds(n * width, width)], qkv_sem.at[n])
+        )
+
+    def send(i, part):
         return pltpu.make_async_remote_copy(
-            src_ref=mine.at[irem(i, 2)],
-            dst_ref=arrived.at[i],
-            send_sem=send_sem.at[i],
-            recv_sem=recv_sem.at[i],
+            src_ref=mine.at[irem(i, 3), part],
+            dst_ref=arrived.at[i, part],
+            send_sem=send_sem.at[i, part],
+            recv_sem=recv_sem.at[i, part],
             device_id=comm.other_core(),
             device_id_type=MESH,
         )
@@ -964,38 +971,57 @@
         for load in loads:
             load.wait()
 
-    @pl.when((step >= 2) & (step < tiles))
-    def _():
-        send(step - 2).wait_send()
-
-    @pl.when(step < tiles)
-    def _():
-        slot = irem(step, 2)
-        mine[slot, 0] = dot(act_ref[...], wout[...]) + dot(mix_ref[...], wproj_ref[...])
-        d_normed = dot_nt(dh_ref[...], win[...]) + dot_nt(dq_ref[...], wq_ref[...])
-        d_normed += dot_nt(dk_ref[...], wk_ref[...]) + dot_nt(dv_ref[...], wv_ref[...])
-        mine[slot, 1] = d_normed
-        send(step).start()
-
-    @pl.when(step >= 1)
-    def _():
-        send(step - 1).wait_recv()
-        slot = irem(step + 1, 2)
+    @pl.when((step >= 3) & (step < tiles))
+    def _():
+        send(step - 3, 0).wait_send()
+        send(step - 3, 1).wait_send()
+
+    @pl.when(step >= 2)
+    def _():
+        send(step - 2, 0).wait_recv()
+        send(step - 2, 1).wait_recv()
+
+    def products():
+        slot = irem(step, 3)
+        mine[slot, 0] = dot(act_ref[...], wout[...])
+        mine[slot, 0] += dot(mix_ref[...], wproj_ref[...])
+        send(step, 0).start()
+        d_qkv = jnp.concatenate([dq_ref[...], dk_ref[...], dv_ref[...]], 1)
+        mine[slot, 1] = dot_nt(dh_ref[...], win[...])
+        mine[slot, 1] += dot_nt(d_qkv, wqkv[...])
+        send(step, 1).start()
+
+    def finish_rows():
+        slot = irem(step + 1, 3)
         x = tok_ref[...].astype(f32)
         centered = x - jnp.mean(x, axis=-1, keepdims=True)
         var = jnp.mean(centered * centered, axis=-1, keepdims=True)
         inv_std = lax.rsqrt(var + EPSILON)
         unit = centered * inv_std
-        out_ref[...] = (x + (mine[slot, 0] + arrived[step - 1, 0]) * valid_ref[...]).astype(bf16)
-        scaled = (mine[slot, 1] + arrived[step - 1, 1]) * gain_ref[...]
+        out_ref[...] = (x + (mine[slot, 0] + arrived[step - 2, 0]) * valid_ref[...]).astype(bf16)
+        scaled = (mine[slot, 1] + arrived[step - 2, 1]) * gain_ref[...]
         mean = jnp.mean(scaled, axis=-1, keepdims=True)
         cross = jnp.mean(scaled * unit, axis=-1, keepdims=True)
         grad_ref[...] = (cot_ref[...].astype(f32) + inv_std * (scaled - mean - unit * cross)).astype(bf16)
 
-    @pl.when(step == tiles)
-    def _():
-        send(tiles - 2).wait_send()
-        send(tiles - 1).wait_send()
+    @pl.when(step < 2)
+    def _():
+        products()
+
+    @pl.when((step >= 2) & (step < tiles))
+    def _():
+        finish_rows()
+        products()
+
+    @pl.when(step >= tiles)
+    def _():
+        finish_rows()
+
+    @pl.when(step == tiles + 1)
+    def _():
+        for i in (tiles - 3, tiles - 2, tiles - 1):
+            send(i, 0).wait_send()
+            send(i, 1).wait_send()
 
 
 def tail(comm, active, d_hidden, mixed, d_qkv, tokens, cotangent, valid, gain, weights, w_proj, w_qkv, flows):
@@ -1004,22 +1030,18 @@
     width = mixed.shape[1]
     tiles = rows // TILE
     strips = 1 if gathered else comm.parts
-    streams = comm.streams
 
     def now(i):
         return (jnp.minimum(i, tiles - 1), 0)
 
     def before(i):
-        return (jnp.maximum(i - 1, 0), 0)
-
-    def weight(which):
-        return pl.BlockSpec((D, width), lambda i: (0, which * streams + lax.axis_index("stream")))
+        return (jnp.maximum(i - 2, 0), 0)
 
     shape = jax.ShapeDtypeStruct((rows, D), bf16)
     return with_comm(
         comm,
         partial(tail_kernel, comm, tiles, gathered),
-        tiles + 1,
+        tiles + 2,
         [
             pl.BlockSpec((TILE, units), now),
             pl.BlockSpec((TILE, units), now),
@@ -1032,25 +1054,25 @@
             pl.BlockSpec((TILE, 1), before),
             pl.BlockSpec((1, D), lambda i: (0, 0)),
             pl.BlockSpec((width, D), lambda i: (lax.axis_index("stream"), 0)),
-            weight(0),
-            weight(1),
-            weight(2),
+            ANY,
             ANY,
             ANY,
         ],
         [pl.BlockSpec((TILE, D), before), pl.BlockSpec((TILE, D), before)],
         [shape, shape],
         flows,
-        [active, d_hidden, mixed, *d_qkv, tokens, cotangent, valid, gain, w_proj, w_qkv, w_qkv, w_qkv, w_in, w_out],
+        [active, d_hidden, mixed, *d_qkv, tokens, cotangent, valid, gain, w_proj, w_qkv, w_in, w_out],
         [
             pltpu.VMEM((D, units), bf16),
             pltpu.VMEM((units, D), bf16),
-            pltpu.VMEM((2, 2, TILE, D), f32),
+            pltpu.VMEM((D, 3 * width), bf16),
+            pltpu.VMEM((3, 2, TILE, D), f32),
             pltpu.VMEM((tiles, 2, TILE, D), f32),
             pltpu.SemaphoreType.DMA((strips,)),
             pltpu.SemaphoreType.DMA((strips,)),
-            pltpu.SemaphoreType.DMA((tiles,)),
-            pltpu.SemaphoreType.DMA((tiles,)),
+            pltpu.SemaphoreType.DMA((3,)),
+            pltpu.SemaphoreType.DMA((tiles, 2)),
+            pltpu.SemaphoreType.DMA((tiles, 2)),
         ],
         exchange=True,
         name="tail",
@@ -1063,18 +1085,52 @@
 
 
 KIND = {
-    "in0": "xp", "in1": "zx", "in2": "yz", "in3": "zx", "o0": "zy", "o1": "xx", "o2": "xp", "o3": "zz",
-    "pr": "xp", "q0": "xp", "q1": "xx", "feature": "xy",
+    "in0": "xx",
+    "in1": "xz",
+    "in2": "yz",
+    "in3": "xy",
+    "o0": "xz",
+    "o1": "xp",
+    "o2": "zx",
+    "o3": "xy",
+    "pr": "xx",
+    "q0": "xy",
+    "q1": "xp",
+    "feature": "xy",
 }
-FRONT = {"in0": (6, (13, 20, 25, 27)), "in1": (12, (23,)), "in2": (18, (-1,))}
-FORWARD = {"in1": (0, (7, 9)), "in2": (0, (5, 8)), "in3": (0, (9,)), "o0": (0, (9,)), "o1": (0, (9,))}
+FRONT = {
+    "in0": (3, (10, 15)),
+    "in1": (6, (14, -1)),
+    "in2": (11, (-1,)),
+    "o1": (14, (-1,)),
+    "o2": (15, (-1,)),
+}
+FORWARD = {
+    "o2": (0, (8, -1)),
+    "o0": (0, (8, -1)),
+    "o1": (0, (8, -1)),
+    "o3": (1, (-1,)),
+    "in2": (3, (8, -1)),
+}
 BACKWARD = {
-    "in1": (0, (5,)), "in2": (0, (5,)), "in3": (0, (6, 11, 16)), "o0": (0, (6, 11, 16)), "o2": (0, (10, 19)),
-    "o3": (4, (19,)), "pr": (8, (15, 19)), "q0": (14, (19,)),
+    "pr": (0, (12, -1)),
+    "in3": (0, (12, 18)),
+    "o3": (0, (14, 19, -1)),
+    "o2": (0, (8,)),
+    "o1": (0, (8,)),
+    "in2": (0, (8,)),
+    "in0": (1, (11,)),
+    "in1": (3, (8, 12)),
+    "q0": (11, (-1,)),
+    "o0": (12, (17, -1)),
 }
 TAIL = {
-    "o1": (0, (4, 8, -1)), "o2": (0, (3, 7)), "pr": (0, (3, 7)), "q0": (0, (7, -1)), "q1": (3, (8, -1)),
-    "feature": (0, (1, 3, 5, 7)),
+    "feature": (0, (5, 9)),
+    "q1": (0, (4, 8, -1)),
+    "q0": (0, (7, 9, -1)),
+    "in3": (0, (1, 4)),
+    "pr": (1, (5,)),
+    "in0": (2, (5,)),
 }
 
 

time: 316 us -> 301 us (0.953)
  Pallas kernels: 297 us -> 278 us
    pallas_call x5, Pallas kernels: 297 us -> 278 us  [with_comm(): pl.pallas_call(run, grid=(steps,), in_specs=list(in_specs) + [ANY] * len(...]
    unnamed x76 -> x70, local copies, waits for them, and re-layouts: 7.96 us -> 9.69 us
  transfers between devices with their start and end apart: 2 -> 2, of which waited for: 0 -> 1; matrix products, arithmetic and copies ran while one was open for 1% -> 1% of each run, Pallas kernels for 0% -> 0%
where the time goes in v3:
time: 301 us; the launch traced here: 300 us
  Pallas kernels  278 us (92%)
  local copies, waits for them, and re-layouts  11.2 us (4%)
  other arithmetic  7.38 us (2%)
    pallas_call x5, Pallas kernels, with_comm(): pl.pallas_call(run, grid=(steps,), in_specs=list(in_specs) + [ANY] * len(...  278 us
    unnamed x70, local copies, waits for them, and re-layouts  9.69 us
  transfers between devices with their start and end apart: 2, of which 1 were waited for; matrix products, arithmetic and copies ran while one was open for 1% of the time, Pallas kernels for 0%

profile of v3, /device:TPU:0, one launch (start us, length us, event | category | flops | bytes accessed | tf_op | source)
XLA Modules:
  0.0 300.1 jit_solution(3435001125492162080)
XLA Ops:
  1.3 1.1 fusion.refs_2_.refs_8_
  2.4 80.9 %front.1 = (bf16[2048,1024]{1,0:T(8,128)(2,1)}, bf16[2048,1024]{1,0:T(8,128)(2,1)}, bf16[2048,2048]{1,0:T(8,128)(2,1)}, bf16[2048,2048]{1,0:T(8,128)(2,1)}, f32[...) custom-call(bf16[2048,1024]{1,0:T(8,128)(2,1)} %refs_6_.1, ...), custom_call_target="tpu_custom_call" | custom-call | flops 34359738368 | bytes 41943040 | tf_op jit(solution)/shard_map/front/pallas_call | solution.py:327
  83.3 46.9 %attention_forward.1 = (bf16[2048,512]{1,0:T(8,128)(2,1)}, bf16[2048,512]{1,0:T(8,128)(2,1)}, bf16[2048,512]{1,0:T(8,128)(2,1)}, bf16[2048,512]{1,0:T(8,128)(2,1...) custom-call(bf16[2048,1024]{1,0:T(8,128)(2,1)} %get-tuple-element.60, ...), custom_call_target="tpu_custom_call" | custom-call | flops 20971520000 | bytes 24117248 | tf_op jit(solution)/shard_map/attention_forward/pallas_call | solution.py:327
  130.1 71.5 %attention_backward.1 = (bf16[2048,512]{1,0:T(8,128)(2,1)}, bf16[2048,512]{1,0:T(8,128)(2,1)}, bf16[2048,512]{1,0:T(8,128)(2,1)}, f32[4,64,512]{2,1,0:T(8,128)},...) custom-call(bf16[2048,1024]{1,0:T(8,128)(2,1)} %get-tuple-element.61, ...), custom_call_target="tpu_custom_call" | custom-call | flops 35852910592 | bytes 34078720 | tf_op jit(solution)/shard_map/attention_backward/pallas_call | solution.py:327
  201.6 0.0 copy-start.5
  201.7 65.4 %tail.1 = (bf16[2048,1024]{1,0:T(8,128)(2,1)}, bf16[2048,1024]{1,0:T(8,128)(2,1)}, f32[4,8,128]{2,1,0:T(8,128)}, f32[2,64,768]{2,1,0:T(8,128)}, f32[1,64,768]{2,...) custom-call(bf16[2048,2048]{1,0:T(8,128)(2,1)} %get-tuple-element.58.refs_0_, ...), custom_call_target="tpu_custom_call" | custom-call | flops 25769803776 | bytes 54525952 | tf_op jit(solution)/shard_map/tail/pallas_call | solution.py:327
  267.1 0.9 constant_dynamic-update-slice_fusion.13
  268.0 0.0 copy-done.4
  268.1 0.9 constant_dynamic-update-slice_fusion.10
  269.0 1.0 constant_dynamic-update-slice_fusion.9
  269.9 13.7 %rest.1 = (f32[1,64,512]{2,1,0:T(8,128)}, f32[1,64,768]{2,1,0:T(8,128)}, f32[1,8,128]{2,1,0:T(8,128)}) custom-call(f32[2,64,512]{2,1,0:T(8,128)} %get-tuple-element.98.refs_0_, f32[2,64,768]{2,1,0:T(8,128)} %get-tuple-element.99.refs_1_, f32[4,8,128]{2,1,0:T(8,128)} %get-tuple-element.100.refs_2_), custom_call_target="tpu_custom_call" | custom-call | tf_op jit(solution)/shard_map/rest/pallas_call | solution.py:327
  283.6 1.0 constant_dynamic-update-slice_fusion.8
  284.6 0.9 constant_dynamic-update-slice_fusion.7
  285.5 0.1 collective-permute-start
  285.6 0.5 collective-permute-start.1
  286.1 0.0 copy-done.7
  286.1 0.0 copy-done.9
  286.1 0.8 pad_maximum_fusion
  286.9 0.8 collective-permute-done.1
  287.7 1.0 bitcast_add_fusion
  288.7 0.6 fusion.1
  289.3 0.0 collective-permute-done
  289.3 0.1 broadcast_select_fusion
  289.9 0.0 copy-start.2
  290.0 0.0 copy-start.3
  290.0 1.3 multiply_reduce_fusion
  291.3 1.1 multiply_reduce_fusion.1
  292.4 1.3 dynamic-slice_divide_fusion
  293.7 0.7 pad_maximum_fusion.1
  294.4 2.1 copy.80
  296.5 1.6 copy-done
  298.1 2.0 copy.81
  (61 shorter events, 0.3 us)
Async XLA Ops:
  201.6 66.4 %copy-start.5 = (f32[1,64,512]{2,1,0:T(8,128)S(1)}, f32[1,64,512]{2,1,0:T(8,128)}, u32[]{:S(2)}) copy-start(f32[1,64,512]{2,1,0:T(8,128)} %get-tuple-element.94) | copy-start | bytes 393220
  201.6 66.4 %copy-start.4 = (f32[1,64,512]{2,1,0:T(8,128)S(1)}, f32[1,64,512]{2,1,0:T(8,128)}, u32[]{:S(2)}) copy-start(f32[1,64,512]{2,1,0:T(8,128)} %get-tuple-element.95) | copy-start | bytes 393220
  201.6 84.4 %copy-start.6 = (f32[1,128,256]{2,1,0:T(8,128)S(1)}, f32[1,128,256]{2,1,0:T(8,128)}, u32[]{:S(2)}) copy-start(f32[1,128,256]{2,1,0:T(8,128)} %get-tuple-element.106) | copy-start | bytes 393220
  201.7 84.4 %copy-start.7 = (f32[1,128,256]{2,1,0:T(8,128)S(1)}, f32[1,128,256]{2,1,0:T(8,128)}, u32[]{:S(2)}) copy-start(f32[1,128,256]{2,1,0:T(8,128)} %get-tuple-element.105) | copy-start | bytes 393220
  201.7 84.4 %copy-start.8 = (f32[1,128,256]{2,1,0:T(8,128)S(1)}, f32[1,128,256]{2,1,0:T(8,128)}, u32[]{:S(2)}) copy-start(f32[1,128,256]{2,1,0:T(8,128)} %get-tuple-element.104) | copy-start | bytes 393220
  201.7 84.4 %copy-start.9 = (f32[1,128,256]{2,1,0:T(8,128)S(1)}, f32[1,128,256]{2,1,0:T(8,128)}, u32[]{:S(2)}) copy-start(f32[1,128,256]{2,1,0:T(8,128)} %get-tuple-element.103) | copy-start | bytes 393220
  285.5 3.8 %collective-permute-start = (f32[32,4096]{1,0:T(8,128)S(1)}, f32[32,4096]{1,0:T(8,128)S(1)}, u32[]{:S(2)}, u32[]{:S(2)}) collective-permute-start(f32[32,4096]{1,0:T(8,128)S(1)} %get-tuple-element.114), channel_id=1, source_target_pairs={{0,1},{1,0},{2,3},{3,2},{4,5},{5,4},{6,7},{7,6},{8,9},{9,8},{10,11... | collective-permute-start | bytes 1572872 | tf_op jit(solution)/shard_map/ppermute | solution.py:1151
  285.6 2.1 collective-permute-start.1
  286.9 7.4 %copy-start.1 = (bf16[2048,1024]{1,0:T(8,128)(2,1)S(1)}, bf16[2048,1024]{1,0:T(8,128)(2,1)}, u32[]{:S(2)}) copy-start(bf16[2048,1024]{1,0:T(8,128)(2,1)} %get-tuple-element.132) | copy-start | bytes 12582916
  289.9 6.6 %copy-start.2 = (f32[32,4096]{1,0:T(8,128)}, f32[32,4096]{1,0:T(8,128)S(1)}, u32[]{:S(2)}) copy-start(f32[32,4096]{1,0:T(8,128)S(1)} %constant_dynamic-update-slice_fusion.14) | copy-start | bytes 1572868
  290.0 6.5 %copy-start.3 = (f32[32,3072]{1,0:T(8,128)}, f32[32,3072]{1,0:T(8,128)S(1)}, u32[]{:S(2)}) copy-start(f32[32,3072]{1,0:T(8,128)S(1)} %constant_dynamic-update-slice_fusion.46) | copy-start | bytes 1179652
  294.4 3.7 %copy-start = (bf16[2048,1024]{1,0:T(8,128)(2,1)S(1)}, bf16[2048,1024]{1,0:T(8,128)(2,1)}, u32[]{:S(2)}) copy-start(bf16[2048,1024]{1,0:T(8,128)(2,1)} %get-tuple-element.133) | copy-start | bytes 12582916

commit v4 on v3

--- a/solution.py
+++ b/solution.py
@@ -19,7 +19,7 @@
 
 f32 = jnp.float32
 bf16 = jnp.bfloat16
-VMEM_LIMIT = 60 * 1024 * 1024
+VMEM_LIMIT = 62 * 1024 * 1024
 BLK = 256
 PAIR = 2 * HEAD
 
@@ -257,7 +257,7 @@
 
 def with_comm(
     comm, kernel, steps, in_specs, out_specs, out_shape, flows, operands, scratch_shapes=(), inner=(), exchange=False,
-    name=None, **call,
+    share_flows=False, name=None, **call,
 ):
     base_in, base_out, base_scratch = len(in_specs), len(out_specs), len(scratch_shapes)
     every = list(flows) + [flow for flow, _, _ in inner]
@@ -308,7 +308,7 @@
 
         for flow in every:
             flow.events(step, False)
-        kernel(*own_in, *own_out, *own_scratch)
+        kernel(*own_in, *own_out, *own_scratch, **({"flows": every} if share_flows else {}))
 
         @pl.when(step == steps - 1)
         def _():
@@ -1053,7 +1053,7 @@
             pl.BlockSpec((TILE, D), before),
             pl.BlockSpec((TILE, 1), before),
             pl.BlockSpec((1, D), lambda i: (0, 0)),
-            pl.BlockSpec((width, D), lambda i: (lax.axis_index("stream"), 0)),
+            pl.BlockSpec((width, D), lambda i: (lax.axis_index("stream"), 0), pipeline_mode=pl.Buffered(1)),
             ANY,
             ANY,
             ANY,
@@ -1084,53 +1084,222 @@
     )
 
 
+def rest_kernel(comm, names, widths, ready, length, *refs, flows=()):
+    held = dict(zip(ready, refs))
+    refs = refs[len(ready) :]
+    other_ref, feature_ref, landing, feature_landing, send_sem, recv_sem = refs
+    moving = {flow.name: flow for flow in flows}
+    step = pl.program_id(0)
+    core = lax.axis_index("stream")
+    half = landing.shape[0]
+
+    def copy(n, name):
+        source = held[name] if name in held else moving[name].own
+        if name == "feature":
+            source, target = source.at[0], feature_landing
+        else:
+            source = source.at[0, pl.ds(pl.multiple_of((1 - core) * half, half), half), :]
+            target = landing.at[:, pl.ds(sum(widths[:n]), widths[n])]
+        return pltpu.make_async_remote_copy(
+            src_ref=source,
+            dst_ref=target,
+            send_sem=send_sem.at[n],
+            recv_sem=recv_sem.at[n],
+            device_id=comm.other_core(),
+            device_id_type=MESH,
+        )
+
+    @pl.when(step == 0)
+    def _():
+        for n, name in enumerate(names):
+            if name in held:
+                copy(n, name).start()
+
+    @pl.when(step == length - 1)
+    def _():
+        for n, name in enumerate(names):
+            if name not in held:
+                copy(n, name).start()
+        for n, name in enumerate(names):
+            copy(n, name).wait()
+        other_ref[...] = landing[...]
+        feature_ref[...] = feature_landing[...]
+
+
+def rest(comm, done, names, plan, flows):
+    half = D // comm.parts // comm.streams
+    ready = [name for name in names if name not in plan]
+    widths = [done[name][1].shape[2] if name != "feature" else 0 for name in names]
+    length = 2 + max([0] + [len(sums) for _, sums in plan.values()])
+    shape = (half, sum(widths))
+    return with_comm(
+        comm,
+        partial(rest_kernel, comm, names, widths, ready, length),
+        length,
+        [ANY] * len(ready),
+        [pl.BlockSpec(shape, lambda i: (0, 0)), pl.BlockSpec((8, PAIR), lambda i: (0, 0))],
+        [jax.ShapeDtypeStruct(shape, f32), jax.ShapeDtypeStruct((8, PAIR), f32)],
+        flows,
+        [done[name][1] for name in ready],
+        [
+            pltpu.VMEM(shape, f32),
+            pltpu.VMEM((8, PAIR), f32),
+            pltpu.SemaphoreType.DMA((len(names),)),
+            pltpu.SemaphoreType.DMA((len(names),)),
+        ],
+        exchange=True,
+        share_flows=True,
+        name="rest",
+    )
+
+
+def assemble_kernel(comm, in_count, call_count, out_count, *refs):
+    refs = list(refs)
+
+    def take(count):
+        taken = refs[:count]
+        del refs[:count]
+        return taken
+
+    ins, calls, (proj_ref,), outs = take(in_count), take(call_count), take(1), take(out_count)
+    other_ref, feature_ref, feature_other, win_ref, wqkv_ref, gain_ref, output_hbm, input_hbm = take(8)
+    in_grad, qkv_grad, proj_grad, out_grad, gain_grad, feature_grad, output_out, input_out, stage, in_sem, out_sem = refs
+    core = lax.axis_index("stream")
+    half = in_grad.shape[0]
+    chunks = stage.shape[1]
+    rows = stage.shape[2]
+    loads, stores = [], []
+    for n, (source, target) in enumerate(((output_hbm, output_out), (input_hbm, input_out))):
+        for c in range(chunks):
+            part = pl.ds(c * rows, rows)
+            loads.append(pltpu.make_async_copy(source.at[part, :], stage.at[n, c], in_sem.at[n, c]))
+            stores.append(pltpu.make_async_copy(stage.at[n, c], target.at[part, :], out_sem.at[n, c]))
+    for load in loads:
+        load.start()
+    for n, ref in enumerate(outs):
+        out_grad[:, n * OUT_COLUMNS : (n + 1) * OUT_COLUMNS] = ref[0]
+    here = pl.ds(pl.multiple_of(core * half, half), half)
+    unit = FF // comm.parts // comm.streams
+    units = FF // comm.streams
+    wide = GROUPS * PAIR
+    columns = D // comm.streams
+    for load, store in zip(loads, stores):
+        load.wait()
+        store.start()
+    for side in range(2):
+
+        @pl.when(core == side)
+        def _(side=side):
+            for n in range(comm.parts):
+                mine = ins[n * unit // UNITS][0, here, n * unit % UNITS : n * unit % UNITS + unit]
+                other = other_ref[:, n * unit : (n + 1) * unit]
+                pair = (mine, other) if side == 0 else (other, mine)
+                for k in range(2):
+                    at = (2 * n + k) * unit
+                    in_grad[:, at : at + unit] = pair[k]
+            for which in range(3):
+                for n in range(call_count):
+                    mine = calls[n][0, here, which * wide : (which + 1) * wide]
+                    at = units + (3 * n + which) * wide
+                    other = other_ref[:, at : at + wide]
+                    pair = (mine, other) if side == 0 else (other, mine)
+                    for k in range(2):
+                        at = which * D + k * columns + n * wide
+                        qkv_grad[:, at : at + wide] = pair[k]
+            at = units + 3 * columns
+            pair = (proj_ref[0, here, :], other_ref[:, at : at + columns])
+            for k in range(2):
+                proj_grad[:, k * columns : (k + 1) * columns] = pair[k if side == 0 else 1 - k]
+            share = feature_grad.shape[1]
+            total = feature_ref[0] + feature_other[...]
+            feature_grad[...] = total[0:1, side * share : (side + 1) * share]
+
+    total = jnp.sum(win_ref[...].astype(f32) * in_grad[...], axis=1, keepdims=True)
+    total += jnp.sum(wqkv_ref[...].astype(f32) * qkv_grad[...], axis=1, keepdims=True)
+    gain_grad[...] = total / gain_ref[...]
+    for store in stores:
+        store.wait()
+
+
+def assemble(comm, final, other, feature_other, w_in, w_qkv, norm_gain, output, input_grad):
+    parts, streams = comm.parts, comm.streams
+    half, share = D // parts // streams, D // (parts * streams)
+    in_names = [f"in{c}" for c in range(FF // streams // UNITS)]
+    call_names = [f"q{c}" for c in range(HEADS // streams // 2 // GROUPS)]
+    out_names = [f"o{b}" for b in range(D // OUT_COLUMNS)]
+
+    def whole(array):
+        return pl.BlockSpec(array.shape, lambda i, n=array.ndim: (0,) * n)
+
+    def rows_of(columns):
+        return pl.BlockSpec((half, columns), lambda i: (lax.axis_index("dp") * streams + lax.axis_index("stream"), 0))
+
+    pieces = [final[n] for n in in_names + call_names + ["pr"] + out_names] + [other, final["feature"], feature_other]
+    shapes = [(half, FF), (half, 3 * D), (half, D), (FF // parts // streams, D), (half, 1), (1, share)]
+    low = jax.ShapeDtypeStruct(output.shape, bf16)
+    return pl.pallas_call(
+        partial(assemble_kernel, comm, len(in_names), len(call_names), len(out_names)),
+        grid=(1,),
+        in_specs=[whole(piece) for piece in pieces] + [rows_of(FF), rows_of(3 * D), rows_of(1), ANY, ANY],
+        out_specs=[pl.BlockSpec(shape, lambda i: (0, 0)) for shape in shapes] + [ANY, ANY],
+        out_shape=[jax.ShapeDtypeStruct(shape, f32) for shape in shapes] + [low, low],
+        scratch_shapes=[
+            pltpu.VMEM((2, 4, output.shape[0] // 4, D), bf16),
+            pltpu.SemaphoreType.DMA((2, 4)),
+            pltpu.SemaphoreType.DMA((2, 4)),
+        ],
+        compiler_params=params(),
+        name="assemble",
+    )(*pieces, w_in, w_qkv, norm_gain.reshape(D, 1), output, input_grad)
+
+
 KIND = {
-    "in0": "xx",
-    "in1": "xz",
-    "in2": "yz",
+    "in0": "xz",
+    "in1": "yz",
+    "in2": "zx",
     "in3": "xy",
-    "o0": "xz",
-    "o1": "xp",
-    "o2": "zx",
-    "o3": "xy",
-    "pr": "xx",
-    "q0": "xy",
-    "q1": "xp",
+    "o0": "xx",
+    "o1": "zx",
+    "o2": "zz",
+    "o3": "xx",
+    "pr": "zx",
+    "q0": "xx",
+    "q1": "xx",
     "feature": "xy",
 }
 FRONT = {
-    "in0": (3, (10, 15)),
-    "in1": (6, (14, -1)),
-    "in2": (11, (-1,)),
-    "o1": (14, (-1,)),
-    "o2": (15, (-1,)),
+    "in0": (3, (10, -1)),
+    "in1": (6, (-1,)),
+    "in2": (9, (-1,)),
+    "o0": (13, (-1,)),
 }
 FORWARD = {
-    "o2": (0, (8, -1)),
-    "o0": (0, (8, -1)),
-    "o1": (0, (8, -1)),
-    "o3": (1, (-1,)),
-    "in2": (3, (8, -1)),
+    "in2": (0, (6,)),
+    "o1": (0, (8,)),
+    "o3": (0, (-1,)),
+    "o2": (4, (-1,)),
+    "o0": (5, (-1,)),
+    "in0": (7, (-1,)),
+    "in3": (8, (-1,)),
 }
 BACKWARD = {
-    "pr": (0, (12, -1)),
-    "in3": (0, (12, 18)),
-    "o3": (0, (14, 19, -1)),
-    "o2": (0, (8,)),
-    "o1": (0, (8,)),
-    "in2": (0, (8,)),
-    "in0": (1, (11,)),
-    "in1": (3, (8, 12)),
-    "q0": (11, (-1,)),
-    "o0": (12, (17, -1)),
+    "o1": (0, (7, 14, 17)),
+    "pr": (0, (14, -1)),
+    "o3": (1, (9, 16, 19)),
+    "in1": (1, (9, 13)),
+    "o0": (5, (11, 15)),
+    "in0": (8, (13,)),
+    "q0": (10, (-1,)),
+    "in2": (15, (19, -1)),
 }
 TAIL = {
     "feature": (0, (5, 9)),
-    "q1": (0, (4, 8, -1)),
-    "q0": (0, (7, 9, -1)),
-    "in3": (0, (1, 4)),
-    "pr": (1, (5,)),
-    "in0": (2, (5,)),
+    "q1": (0, (8, -1)),
+    "in1": (0, (2,)),
+    "q0": (0, (6, 9, -1)),
+    "in3": (0, (5, 7, 9)),
+    "pr": (1, (5, 7)),
+    "o2": (2, (7,)),
 }
 
 
@@ -1143,18 +1312,9 @@
         sums_np[base : base + HEAD, HEAD] = 1.0
         sums_np[base + HEAD : base + PAIR, 0] = 1.0
 
-    def partner(value):
-        pairs = []
-        for d in range(parts):
-            for s in range(streams):
-                pairs.append((d * streams + s, d * streams + (s ^ 1)))
-        return lax.ppermute(value, ("dp", "stream"), pairs)
-
     def body(tokens, norm_gain, w_qkv, w_proj, w_in, w_out, feature_weight, lengths, cotangent):
         comm.kernels = 0
         rows = tokens.shape[0]
-        chip = lax.axis_index("dp")
-        stream = lax.axis_index("stream")
         gain = norm_gain.reshape(1, D)
         fw = feature_weight.reshape(1, D)
         cosine, sine = jnp.asarray(cosine_np), jnp.asarray(sine_np)
@@ -1198,48 +1358,17 @@
         for name, (taken, _) in done.items():
             if taken < comm.steps:
                 left[name] = (0, tuple(range(1, comm.steps - taken + 1)))
-        if left:
-            length = 1 + max(len(sums) for _, sums in left.values())
-            _, shares = with_comm(
-                comm, lambda *refs: None, length, [], [], [], flows_of(left), [], name="rest"
-            )
-            landed(shares, left)
-        final = {name: array[0] for name, (_, array) in done.items()}
-
-        value = final["feature"]
-        value = value + partner(value)
-        share = D // (parts * streams)
-        feature_grad = lax.dynamic_slice(value, (0, stream * share), (1, share)).reshape(share)
-
-        half = D // parts // streams
         names = [f"in{c}" for c in range(units // UNITS)]
-        names += [f"q{c}" for c in range(HEADS // streams // 2 // GROUPS)] + ["pr"]
-        mine = jnp.concatenate([lax.dynamic_slice_in_dim(final[n], stream * half, half) for n in names], 1)
-        other = partner(
-            jnp.concatenate([lax.dynamic_slice_in_dim(final[n], (1 - stream) * half, half) for n in names], 1)
+        names += [f"q{c}" for c in range(HEADS // streams // 2 // GROUPS)] + ["pr", "feature"]
+        (other, feature_other), shares = rest(comm, done, names, left, flows_of(left))
+        landed(shares, left)
+        final = {name: array for name, (_, array) in done.items()}
+        in_grad, qkv_grad, proj_grad, out_grad, gain_grad, feature_grad, output, input_grad = assemble(
+            comm, final, other, feature_other, w_in, w_qkv, norm_gain, output, input_grad
         )
-        a = jnp.where(stream == 0, mine, other)
-        b = jnp.where(stream == 0, other, mine)
-        unit = units // parts
-        in_grad = jnp.concatenate(
-            [src[:, unit * i : unit * (i + 1)] for i in range(parts) for src in (a, b)], 1
+        return (
+            output, input_grad, gain_grad.reshape(-1), qkv_grad, proj_grad, in_grad, out_grad, feature_grad.reshape(-1)
         )
-        qa, qb = a[:, units : units + 3 * D // streams], b[:, units : units + 3 * D // streams]
-        wide = GROUPS * PAIR
-        calls = HEADS // streams // 2 // GROUPS
-
-        def third(src, which):
-            return [src[:, (3 * n + which) * wide : (3 * n + which + 1) * wide] for n in range(calls)]
-
-        qkv_grad = jnp.concatenate(sum([third(qa, w) + third(qb, w) for w in range(3)], []), 1)
-        proj_grad = jnp.concatenate([a[:, units + 3 * D // streams :], b[:, units + 3 * D // streams :]], 1)
-        out_grad = jnp.concatenate([final[f"o{n}"] for n in range(D // OUT_COLUMNS)], 1)
-        first_row = (chip * streams + stream) * half
-        w_in_rows = lax.dynamic_slice_in_dim(w_in, first_row, half).astype(f32)
-        w_qkv_rows = lax.dynamic_slice_in_dim(w_qkv, first_row, half).astype(f32)
-        gain_rows = lax.dynamic_slice_in_dim(norm_gain, first_row, half)
-        gain_grad = (jnp.sum(w_in_rows * in_grad, 1) + jnp.sum(w_qkv_rows * qkv_grad, 1)) / gain_rows
-        return output, input_grad, gain_grad, qkv_grad, proj_grad, in_grad, out_grad, feature_grad
 
     both = P(("dp", "stream"), None)
     return jax.shard_map(

time: 301 us -> 290 us (0.963)
  local copies, waits for them, and re-layouts: 11.2 us -> 1.04 us
  Pallas kernels: 278 us -> 285 us
  other arithmetic: 7.38 us -> 2.42 us
    unnamed x70 -> x2, local copies, waits for them, and re-layouts: 9.69 us -> 0.01 us
    pallas_call x0 -> x1, Pallas kernels: none -> 9.33 us  [assemble(): pl.pallas_call(partial(assemble_kernel, comm, len(in_names), len(call_nam...]
  transfers between devices with their start and end apart: 2 -> 0, of which waited for: 1 -> 0; matrix products, arithmetic and copies ran while one was open for 1% -> 0% of each run, Pallas kernels for 0% -> 0%
where the time goes in v4:
time: 290 us
  Pallas kernels  285 us (98%)
    pallas_call x5, Pallas kernels, with_comm(): pl.pallas_call(run, grid=(steps,), in_specs=list(in_specs) + [ANY] * len(...  276 us
    pallas_call x1, Pallas kernels, assemble(): pl.pallas_call(partial(assemble_kernel, comm, len(in_names), len(call_nam...  9.33 us

profile of v4, /device:TPU:0, one launch (start us, length us, event | category | flops | bytes accessed | tf_op | source)
XLA Modules:
  0.0 289.7 jit_solution(17581416358093625763)
XLA Ops:
  1.3 1.1 fusion.refs_2_.refs_8_
  2.4 67.7 %front.1 = (bf16[2048,1024]{1,0:T(8,128)(2,1)}, bf16[2048,1024]{1,0:T(8,128)(2,1)}, bf16[2048,2048]{1,0:T(8,128)(2,1)}, bf16[2048,2048]{1,0:T(8,128)(2,1)}, f32[...) custom-call(bf16[2048,1024]{1,0:T(8,128)(2,1)} %refs_6_.1, ...), custom_call_target="tpu_custom_call" | custom-call | flops 34359738368 | bytes 41943040 | tf_op jit(solution)/shard_map/front/pallas_call | solution.py:327
  70.1 52.2 %attention_forward.1 = (bf16[2048,512]{1,0:T(8,128)(2,1)}, bf16[2048,512]{1,0:T(8,128)(2,1)}, bf16[2048,512]{1,0:T(8,128)(2,1)}, bf16[2048,512]{1,0:T(8,128)(2,1...) custom-call(bf16[2048,1024]{1,0:T(8,128)(2,1)} %get-tuple-element.70, ...), custom_call_target="tpu_custom_call" | custom-call | flops 20971520000 | bytes 24117248 | tf_op jit(solution)/shard_map/attention_forward/pallas_call | solution.py:327
  122.3 66.1 %attention_backward.1 = (bf16[2048,512]{1,0:T(8,128)(2,1)}, bf16[2048,512]{1,0:T(8,128)(2,1)}, bf16[2048,512]{1,0:T(8,128)(2,1)}, f32[1,128,256]{2,1,0:T(8,128)}...) custom-call(bf16[2048,1024]{1,0:T(8,128)(2,1)} %get-tuple-element.69, ...), custom_call_target="tpu_custom_call" | custom-call | flops 35852910592 | bytes 34078720 | tf_op jit(solution)/shard_map/attention_backward/pallas_call | solution.py:327
  188.4 0.0 copy-start
  188.4 64.1 %tail.1 = (bf16[2048,1024]{1,0:T(8,128)(2,1)}, bf16[2048,1024]{1,0:T(8,128)(2,1)}, f32[4,8,128]{2,1,0:T(8,128)}, f32[4,64,768]{2,1,0:T(8,128)}, f32[1,64,512]{2,...) custom-call(bf16[2048,2048]{1,0:T(8,128)(2,1)} %get-tuple-element.92, ...), custom_call_target="tpu_custom_call" | custom-call | flops 25769803776 | bytes 54525952 | tf_op jit(solution)/shard_map/tail/pallas_call | solution.py:327
  252.5 25.5 %rest.1 = (f32[32,4096]{1,0:T(8,128)}, f32[8,128]{1,0:T(8,128)}, f32[1,128,256]{2,1,0:T(8,128)}, f32[1,64,768]{2,1,0:T(8,128)}, f32[1,8,128]{2,1,0:T(8,128)}) custom-call(f32[1,64,512]{2,1,0:T(8,128)} %get-tuple-element.91.refs_0_, f32[1,64,512]{2,1,0:T(8,128)} %get-tuple-element.104.refs_1_, f32[1,64,512]{2,1,0:T(8,128)} %get-tuple-element.105.refs_2_, ...), custom_call_target="tpu_custom_call" | custom-call | tf_op jit(solution)/shard_map/rest/pallas_call | solution.py:327
  278.0 0.0 copy-done
  278.0 1.0 copy.23.refs_16_
  279.1 9.3 %assemble.1 = (f32[32,4096]{1,0:T(8,128)}, f32[32,3072]{1,0:T(8,128)}, f32[32,1024]{1,0:T(8,128)}, f32[128,1024]{1,0:T(8,128)}, f32[32,1]{1,0:T(8,128)}, /*index...) custom-call(f32[1,64,512]{2,1,0:T(8,128)} %get-tuple-element.91.refs_0_, ...), custom_call_target="tpu_custom_call" | custom-call | tf_op jit(solution)/shard_map/assemble/pallas_call | solution.py:1240
  288.4 1.3 reduce
Async XLA Ops:
  188.4 89.6 %copy-start = (f32[1024]{0:T(1024)S(1)}, f32[1024]{0:T(1024)}, u32[]{:S(2)}) copy-start(f32[1024]{0:T(1024)} %param.16) | copy-start | bytes 12292
